TPU v7x, 32 devices: a whole 2x2x4 slice. The times are simulated.
32 devices in a mesh: ctx: 8 (over z, y), tp: 2 (over x), fs: 2 (over core).
Axes of the slice: x: 2, y: 2, z: 4, core: 2. Of those that a mesh axis runs over, the one named last changes fastest.
Arguments:
- tokens: bfloat16 [2, 8192, 1024], P('fs', 'ctx'), may hold values from -6 to 6
- cotangent: bfloat16 [2, 8192, 1024], P('fs', 'ctx'), may hold values from -6 to 6
- lengths: int32 [2, 3], P('fs'), may hold values from 512 to 4096, as said below
- order: int32 [2, 8192], P('fs'), may hold values from 0 to 8191, as said below
- mixer_gain: bfloat16 [1024], P('fs'), may hold values from 0.5 to 1.5
- w_query: bfloat16 [1024, 1024], P('fs', 'tp'), may hold values from -0.1875 to 0.1875
- w_key: bfloat16 [1024, 1024], P('fs', 'tp'), may hold values from -0.1875 to 0.1875
- w_value: bfloat16 [1024, 2048], P('fs', 'tp'), may hold values from -0.1875 to 0.1875
- w_outgate: bfloat16 [1024, 2048], P('fs', 'tp'), may hold values from -0.1875 to 0.1875
- w_decay: bfloat16 [1024, 8], P('fs', 'tp'), may hold values from -0.1875 to 0.1875
- w_beta: bfloat16 [1024, 8], P('fs', 'tp'), may hold values from -0.1875 to 0.1875
- conv_query: bfloat16 [1024, 4], P(('tp', 'fs')), may hold values from -3 to 3
- conv_key: bfloat16 [1024, 4], P(('tp', 'fs')), may hold values from -3 to 3
- conv_value: bfloat16 [2048, 4], P(('tp', 'fs')), may hold values from -3 to 3
- decay_log: float32 [8], P('tp'), may hold values from -5 to 1
- decay_bias: float32 [8], P('tp'), may hold values from -4 to 0
- out_gain: bfloat16 [256], P('fs'), may hold values from 0.5 to 1.5
- w_output: bfloat16 [2048, 1024], P(('tp', 'fs')), may hold values from -0.25 to 0.25
- mlp_gain: bfloat16 [1024], P('fs'), may hold values from 0.5 to 1.5
- w_gate: bfloat16 [1024, 2816], P('fs', 'tp'), may hold values from -0.1875 to 0.1875
- w_up: bfloat16 [1024, 2816], P('fs', 'tp'), may hold values from -0.1875 to 0.1875
- w_down: bfloat16 [2816, 1024], P(('tp', 'fs')), may hold values from -0.21875 to 0.21875
Outputs:
- block_out: bfloat16 [2, 8192, 1024], P('fs', 'ctx')
- grad_tokens: bfloat16 [2, 8192, 1024], P('fs', 'ctx')
- grad_mixer_gain: float32 [1024], P('fs')
- grad_query: float32 [1024, 1024], P('fs', 'tp')
- grad_key: float32 [1024, 1024], P('fs', 'tp')
- grad_value: float32 [1024, 2048], P('fs', 'tp')
- grad_outgate: float32 [1024, 2048], P('fs', 'tp')
- grad_decay: float32 [1024, 8], P('fs', 'tp')
- grad_beta: float32 [1024, 8], P('fs', 'tp')
- grad_conv_query: float32 [1024, 4], P(('tp', 'fs'))
- grad_conv_key: float32 [1024, 4], P(('tp', 'fs'))
- grad_conv_value: float32 [2048, 4], P(('tp', 'fs'))
- grad_decay_log: float32 [8], P('tp')
- grad_decay_bias: float32 [8], P('tp')
- grad_out_gain: float32 [256], P('fs')
- grad_output: float32 [2048, 1024], P(('tp', 'fs'))
- grad_mlp_gain: float32 [1024], P('fs')
- grad_gate: float32 [1024, 2816], P('fs', 'tp')
- grad_up: float32 [1024, 2816], P('fs', 'tp')
- grad_down: float32 [2816, 1024], P(('tp', 'fs'))
Inputs may be any that keep to these rules, and one draw needn't show every extreme that they name: `lengths`: each pack holds 3 sequences laid end to end that fill all 8192 places; in every pack exactly one, which one drawn, has the length 4096. `order`: each row is a permutation of the 8192 places. Of the tokens at given places i * 1024 to (i + 1) * 1024 - 1, exactly 128 lie at packed places j * 1024 to (j + 1) * 1024 - 1, for every i and j.
All inputs are finite; a program needn't handle non-finite values.
Results may differ from a plain program's by a relative error of at most 0.014.
Values may be sent and summed in bfloat16 or wider, within the bound.
A program may use at most 448 MiB of HBM per device.

v0:
```python
from functools import partial

import jax
import jax.numpy as jnp
from jax import lax
from jax.sharding import PartitionSpec as P

CONV = 4
BLOCK = 64


epsilon = 1e-06
precision_highest = lax.Precision.HIGHEST


def passed_along(block, axis, distance):
    devices = range(lax.axis_size(axis))
    route = [(i - distance, i) for i in devices if i - distance in devices]
    return lax.ppermute(block, axis, route)


def entering_2(value, axis, join, neutral):
    count, mine = (lax.axis_size(axis), lax.axis_index(axis))
    pieces = jax.tree.map(lambda part: lax.all_gather(part, axis), value)
    so_far = jax.tree.map(
        lambda part, zero: jnp.full_like(part, 0) + jnp.asarray(zero, part.dtype), value, neutral
    )

    def entering_lap(position, so_far):
        longer = join(so_far, jax.tree.map(lambda part: part[position], pieces))
        return jax.tree.map(lambda new, old: jnp.where(position < mine, new, old), longer, so_far)

    return lax.fori_loop(0, count - 1, entering_lap, so_far)


def carried_in(shard, axis, combine, identity):
    devices, position = (lax.axis_size(axis), lax.axis_index(axis))
    everything = jax.tree.map(
        lambda part, kind: lax.all_gather(part.astype(kind), axis),
        shard,
        jax.tree.map(lambda a: jnp.bfloat16 if a.dtype == jnp.float32 else a.dtype, shard),
    )
    start = jax.tree.map(
        lambda part, zero: jnp.broadcast_to(jnp.asarray(zero, part.dtype), part.shape),
        shard,
        identity,
    )

    def carried_lap(k, before):
        at = devices - 1 - k
        reached = at > position
        new = combine(
            before, jax.tree.map(lambda part, own: part[at].astype(own.dtype), everything, shard)
        )
        return jax.tree.map(lambda a, b: jnp.where(reached, a, b), new, before)

    return lax.fori_loop(0, devices, carried_lap, start)


def silu_grad(values):
    sig_val = jax.nn.sigmoid(values)
    return sig_val * (1.0 + values * (1.0 - sig_val))


def rms_scale(values):
    return lax.rsqrt(jnp.mean(values * values, axis=-1, keepdims=True) + epsilon)


def rms_back(values, inv_rms, gain_vec, grad_rows):
    scaled = gain_vec * grad_rows
    mean_dot = jnp.mean(scaled * values, axis=-1, keepdims=True)
    return inv_rms * scaled - values * inv_rms * inv_rms * inv_rms * mean_dot


def unit_rows(values):
    return values * lax.rsqrt(jnp.sum(values * values, axis=-1, keepdims=True) + epsilon)


def affine_join(earlier, later):
    return (
        jnp.einsum("hij,hjk->hik", later[0], earlier[0], precision=precision_highest),
        later[1] + jnp.einsum("hij,hjk->hik", later[0], earlier[1], precision=precision_highest),
    )


def causal_mix(extended, weight, tap_valid):
    row_count = tap_valid.shape[0]
    taps = weight.shape[1]
    summed = jnp.zeros((row_count, extended.shape[1]), jnp.float32)
    for tap_index in range(taps):
        summed = (
            summed
            + extended[tap_index : tap_index + row_count]
            * weight[:, tap_index]
            * tap_valid[:, taps - 1 - tap_index][:, None]
        )
    return summed


def blocked(values, block_len):
    block_count = values.shape[0] // block_len
    if values.ndim == 3:
        return values.reshape(block_count, block_len, values.shape[1], values.shape[2]).transpose(
            0, 2, 1, 3
        )
    return values.reshape(block_count, block_len, values.shape[1]).transpose(0, 2, 1)


def prepare(
    query_ext,
    key_ext,
    value_ext,
    decay_proj,
    beta_proj,
    weight_query,
    weight_key,
    weight_value,
    decay_log,
    decay_bias,
    tap_valid,
    block_len,
):
    row_count = tap_valid.shape[0]
    head_count = decay_proj.shape[1]
    query_rows = unit_rows(
        jax.nn.silu(causal_mix(query_ext, weight_query, tap_valid)).reshape(
            row_count, head_count, -1
        )
    )
    query_rows = query_rows * query_rows.shape[-1] ** (-0.5)
    key_vectors = unit_rows(
        jax.nn.silu(causal_mix(key_ext, weight_key, tap_valid)).reshape(row_count, head_count, -1)
    )
    value_vecs = jax.nn.silu(causal_mix(value_ext, weight_value, tap_valid)).reshape(
        row_count, head_count, -1
    )
    beta_vals = jax.nn.sigmoid(beta_proj)
    log_decay = -jnp.exp(decay_log) * jax.nn.softplus(decay_proj + decay_bias)
    return (
        blocked(query_rows, block_len),
        blocked(key_vectors, block_len),
        blocked(value_vecs, block_len),
        blocked(beta_vals, block_len),
        blocked(log_decay, block_len),
    )


def block_parts(query_rows, key_vectors, value_vecs, beta_vals, log_decay, seq_start):
    block_len = query_rows.shape[2]
    key_width = query_rows.shape[3]
    cumul = jnp.cumsum(log_decay, axis=-1)
    starts = jnp.cumsum(seq_start, axis=-1)
    later_idx = lax.broadcasted_iota(jnp.int32, (block_len, block_len), 0)
    earlier_idx = lax.broadcasted_iota(jnp.int32, (block_len, block_len), 1)
    lower_mask = later_idx >= earlier_idx
    linked = (lower_mask[None] & (starts[:, :, None] == starts[:, None, :]))[:, None]
    log_gap = cumul[..., :, None] - cumul[..., None, :]
    weights_decay = jnp.where(linked, jnp.exp(jnp.where(linked, log_gap, 0.0)), 0.0)
    entry_gain = jnp.exp(cumul) * (starts == 0.0).astype(jnp.float32)[:, None, :]
    key_key = jnp.einsum("nhck,nhdk->nhcd", key_vectors, key_vectors, precision=precision_highest)
    strict = (later_idx > earlier_idx)[None, None]
    system = jnp.where(strict, beta_vals[..., :, None] * weights_decay * key_key, 0.0) + jnp.eye(
        block_len, dtype=jnp.float32
    )
    solved_values = jax.scipy.linalg.solve_triangular(
        system, beta_vals[..., None] * value_vecs, lower=True, unit_diagonal=True
    )
    solved_keys = jax.scipy.linalg.solve_triangular(
        system, (beta_vals * entry_gain)[..., None] * key_vectors, lower=True, unit_diagonal=True
    )
    attend = weights_decay * jnp.einsum(
        "nhck,nhdk->nhcd", query_rows, key_vectors, precision=precision_highest
    )
    output_local = jnp.einsum("nhcd,nhdv->nhcv", attend, solved_values, precision=precision_highest)
    query_effective = entry_gain[..., None] * query_rows - jnp.einsum(
        "nhcd,nhdk->nhck", attend, solved_keys, precision=precision_highest
    )
    tail_decay = weights_decay[..., block_len - 1, :]
    carry_gain = entry_gain[..., block_len - 1]
    transfer_matrix = carry_gain[..., None, None] * jnp.eye(
        key_width, dtype=jnp.float32
    ) - jnp.einsum(
        "nhck,nhc,nhcj->nhkj", key_vectors, tail_decay, solved_keys, precision=precision_highest
    )
    start_offset = jnp.einsum(
        "nhck,nhc,nhcv->nhkv", key_vectors, tail_decay, solved_values, precision=precision_highest
    )
    return (output_local, query_effective, transfer_matrix, start_offset)


def run_blocks(block_terms, memory_state):

    def run_advance(running_state, element):
        output_local, query_effective, transfer_matrix, start_offset = element
        produced_rows = output_local + jnp.einsum(
            "awg,ago->awo", query_effective, running_state, precision=precision_highest
        )
        return (
            jnp.einsum("clf,cfq->clq", transfer_matrix, running_state, precision=precision_highest)
            + start_offset,
            produced_rows,
        )

    last_memory, produced_rows = lax.scan(run_advance, memory_state, block_terms)
    return (produced_rows, last_memory)


def compose(block_terms):
    transfer_matrix = block_terms[2]
    key_width = transfer_matrix.shape[-1]
    begin = (
        jnp.broadcast_to(jnp.eye(key_width, dtype=jnp.float32), transfer_matrix.shape[1:]),
        jnp.zeros_like(block_terms[3][0]),
    )

    def compose_advance(running_state, element):
        return (affine_join(running_state, element), None)

    joined, unused = lax.scan(compose_advance, begin, (block_terms[2], block_terms[3]))
    return joined


def regroup(grad_rows, ctx_count, fs_count):
    lead = grad_rows.reshape(
        (fs_count, ctx_count, grad_rows.shape[0] // (fs_count * ctx_count)) + grad_rows.shape[1:]
    )
    return jnp.swapaxes(lead, 0, 1).reshape(grad_rows.shape)


def per_device(
    tokens,
    cotangent,
    lengths,
    order,
    mixer_gain,
    w_query,
    w_key,
    w_value,
    w_outgate,
    w_decay,
    w_beta,
    conv_query,
    conv_key,
    conv_value,
    decay_log,
    decay_bias,
    out_gain,
    w_output,
    mlp_gain,
    w_gate,
    w_up,
    w_down,
):
    row_count = tokens.shape[1]
    ctx_count = lax.axis_size("ctx")
    fs_count = lax.axis_size("fs")
    ctx_index = lax.axis_index("ctx")
    per_peer = row_count // ctx_count
    block_len = BLOCK
    halo_rows = CONV - 1
    order_row = order[0]
    total_rows = order_row.shape[0]
    owner_of = (
        jnp.zeros((total_rows,), jnp.int32)
        .at[order_row]
        .set(jnp.arange(total_rows, dtype=jnp.int32))
    )
    local_iota = jnp.arange(row_count, dtype=jnp.int32)
    target = lax.dynamic_slice_in_dim(owner_of, ctx_index * row_count, row_count) // row_count
    earlier_rows = local_iota[None, :] < local_iota[:, None]
    send_rank = jnp.sum(
        ((target[None, :] == target[:, None]) & earlier_rows).astype(jnp.int32), axis=1
    )
    send_slot = target * per_peer + send_rank
    send_order = jnp.zeros((row_count,), jnp.int32).at[send_slot].set(local_iota)
    given_here = lax.dynamic_slice_in_dim(order_row, ctx_index * row_count, row_count)
    source = given_here // row_count
    recv_rank = jnp.sum(
        ((source[None, :] == source[:, None]) & (given_here[None, :] < given_here[:, None])).astype(
            jnp.int32
        ),
        axis=1,
    )
    recv_slot = source * per_peer + recv_rank
    back_order = jnp.zeros((row_count,), jnp.int32).at[recv_slot].set(local_iota)
    arrived = (
        lax.all_to_all(tokens[0][send_order], "ctx", split_axis=0, concat_axis=0, tiled=True),
        lax.all_to_all(cotangent[0][send_order], "ctx", split_axis=0, concat_axis=0, tiled=True),
    )
    resident = arrived[0][recv_slot]
    grad_rows = arrived[1][recv_slot]
    seq_lengths = lengths[0]
    offsets = jnp.cumsum(seq_lengths) - seq_lengths
    positions = (
        ctx_index * row_count - halo_rows + jnp.arange(row_count + halo_rows, dtype=jnp.int32)
    )
    seq_number = jnp.sum((offsets[None, :] <= positions[:, None]).astype(jnp.int32), axis=1)
    tap_valid = jnp.stack(
        [
            (
                seq_number[halo_rows - tap_lag : halo_rows - tap_lag + row_count]
                == seq_number[halo_rows:]
            ).astype(jnp.float32)
            for tap_lag in range(CONV)
        ],
        axis=1,
    )
    seq_start = (
        jnp.any(offsets[None, :] == positions[halo_rows:, None], axis=1)
        .astype(jnp.float32)
        .reshape(row_count // block_len, block_len)
    )
    gathered = (
        lax.all_gather(mixer_gain, "fs", axis=0, tiled=True),
        lax.all_gather(w_query, "fs", axis=0, tiled=True),
        lax.all_gather(w_key, "fs", axis=0, tiled=True),
        lax.all_gather(w_value, "fs", axis=0, tiled=True),
        lax.all_gather(w_outgate, "fs", axis=0, tiled=True),
        lax.all_gather(w_decay, "fs", axis=0, tiled=True),
        lax.all_gather(w_beta, "fs", axis=0, tiled=True),
        lax.all_gather(conv_query, "fs", axis=0, tiled=True),
        lax.all_gather(conv_key, "fs", axis=0, tiled=True),
        lax.all_gather(conv_value, "fs", axis=0, tiled=True),
        lax.all_gather(out_gain, "fs", axis=0, tiled=True),
        lax.all_gather(w_output, "fs", axis=0, tiled=True),
        lax.all_gather(mlp_gain, "fs", axis=0, tiled=True),
        lax.all_gather(w_gate, "fs", axis=0, tiled=True),
        lax.all_gather(w_up, "fs", axis=0, tiled=True),
        lax.all_gather(w_down, "fs", axis=0, tiled=True),
    )
    inputs = resident.astype(jnp.float32)
    inv_one = rms_scale(inputs)
    normed_one = (inputs * inv_one * gathered[0].astype(jnp.float32)).astype(jnp.bfloat16)
    query_proj = jnp.dot(normed_one, gathered[1], preferred_element_type=jnp.float32)
    key_proj = jnp.dot(normed_one, gathered[2], preferred_element_type=jnp.float32)
    value_proj = jnp.dot(normed_one, gathered[3], preferred_element_type=jnp.float32)
    outgate_proj = jnp.dot(normed_one, gathered[4], preferred_element_type=jnp.float32)
    decay_proj = jnp.dot(normed_one, gathered[5], preferred_element_type=jnp.float32)
    beta_proj = jnp.dot(normed_one, gathered[6], preferred_element_type=jnp.float32)
    edges = passed_along(
        (
            query_proj[row_count - halo_rows :],
            key_proj[row_count - halo_rows :],
            value_proj[row_count - halo_rows :],
        ),
        "ctx",
        1,
    )
    query_ext = jnp.concatenate([edges[0], query_proj], axis=0)
    key_ext = jnp.concatenate([edges[1], key_proj], axis=0)
    value_ext = jnp.concatenate([edges[2], value_proj], axis=0)
    prepared, prep_back = jax.vjp(
        partial(prepare, tap_valid=tap_valid, block_len=block_len),
        query_ext,
        key_ext,
        value_ext,
        decay_proj,
        beta_proj,
        gathered[7].astype(jnp.float32),
        gathered[8].astype(jnp.float32),
        gathered[9].astype(jnp.float32),
        decay_log,
        decay_bias,
    )
    block_terms, terms_back = jax.vjp(
        partial(block_parts, seq_start=seq_start),
        prepared[0],
        prepared[1],
        prepared[2],
        prepared[3],
        prepared[4],
    )
    own_map = compose(block_terms)
    key_width = own_map[0].shape[-1]
    identity = (
        jnp.broadcast_to(jnp.eye(key_width, dtype=jnp.float32), own_map[0].shape),
        jnp.zeros_like(own_map[1]),
    )
    entering = entering_2((own_map[0], own_map[1]), "ctx", affine_join, identity)
    run_result, run_back = jax.vjp(run_blocks, block_terms, entering[1])
    head_count = decay_proj.shape[1]
    heads_out = run_result[0].transpose(0, 2, 1, 3).reshape(row_count, head_count, -1)
    gain_out = gathered[10].astype(jnp.float32)
    inv_out = rms_scale(heads_out)
    normalized = heads_out * inv_out
    gate_raw = outgate_proj.reshape(row_count, head_count, -1)
    gate_act = jax.nn.silu(gate_raw)
    mixer_rows = (normalized * gain_out * gate_act).reshape(row_count, -1).astype(jnp.bfloat16)
    mixer_term = lax.psum(
        jnp.dot(mixer_rows, gathered[11], preferred_element_type=jnp.float32), "tp"
    )
    middle = inputs + mixer_term
    inv_two = rms_scale(middle)
    normed_two = (middle * inv_two * gathered[12].astype(jnp.float32)).astype(jnp.bfloat16)
    gate_proj = jnp.dot(normed_two, gathered[13], preferred_element_type=jnp.float32)
    up_proj = jnp.dot(normed_two, gathered[14], preferred_element_type=jnp.float32)
    gate_silu = jax.nn.silu(gate_proj)
    hidden = (gate_silu * up_proj).astype(jnp.bfloat16)
    mlp_term = lax.psum(
        jnp.dot(hidden, gathered[15], preferred_element_type=jnp.float32).astype(jnp.bfloat16), "tp"
    ).astype(jnp.float32)
    result = (middle + mlp_term).astype(jnp.bfloat16)
    grad_down = jnp.dot(hidden.T, grad_rows, preferred_element_type=jnp.float32)
    grad_hidden = jnp.dot(grad_rows, gathered[15].T, preferred_element_type=jnp.float32)
    grad_gate_rows = (grad_hidden * up_proj * silu_grad(gate_proj)).astype(jnp.bfloat16)
    grad_up_rows = (grad_hidden * gate_silu).astype(jnp.bfloat16)
    grad_gate = jnp.dot(normed_two.T, grad_gate_rows, preferred_element_type=jnp.float32)
    grad_up = jnp.dot(normed_two.T, grad_up_rows, preferred_element_type=jnp.float32)
    back_two = lax.psum(
        jnp.dot(grad_gate_rows, gathered[13].T, preferred_element_type=jnp.float32)
        + jnp.dot(grad_up_rows, gathered[14].T, preferred_element_type=jnp.float32),
        "tp",
    )
    grad_mlp_gain = jnp.sum(back_two * middle * inv_two, axis=0)
    grad_middle = grad_rows.astype(jnp.float32) + rms_back(
        middle, inv_two, gathered[12].astype(jnp.float32), back_two
    )
    grad_mix = grad_middle.astype(jnp.bfloat16)
    grad_output = jnp.dot(mixer_rows.T, grad_mix, preferred_element_type=jnp.float32)
    grad_mixed = jnp.dot(grad_mix, gathered[11].T, preferred_element_type=jnp.float32).reshape(
        row_count, head_count, -1
    )
    gain_out_back = gathered[10].astype(jnp.float32)
    outgain_part = jnp.sum(grad_mixed * normalized * gate_act, axis=(0, 1))
    grad_gate_out = (
        (grad_mixed * normalized * gain_out_back * silu_grad(gate_raw))
        .reshape(row_count, -1)
        .astype(jnp.bfloat16)
    )
    grad_heads = rms_back(heads_out, inv_out, gain_out_back, grad_mixed * gate_act)
    grad_blocks = grad_heads.reshape(row_count // block_len, block_len, head_count, -1).transpose(
        0, 2, 1, 3
    )
    local_pull = run_back((grad_blocks, jnp.zeros_like(entering[1])))[1]
    leaving = carried_in((jnp.swapaxes(own_map[0], 1, 2), local_pull), "ctx", affine_join, identity)
    grad_terms = run_back((grad_blocks, leaving[1]))[0]
    grad_prepared = terms_back(grad_terms)
    grad_prep = prep_back(grad_prepared)
    back_edges = passed_along(
        (grad_prep[0][:halo_rows], grad_prep[1][:halo_rows], grad_prep[2][:halo_rows]), "ctx", -1
    )

    def settle(grad_ext, incoming):
        return jnp.concatenate(
            [grad_ext[halo_rows:row_count], grad_ext[row_count:] + incoming], axis=0
        ).astype(jnp.bfloat16)

    grad_query_rows = settle(grad_prep[0], back_edges[0])
    grad_key_rows = settle(grad_prep[1], back_edges[1])
    grad_value_rows = settle(grad_prep[2], back_edges[2])
    grad_decay_rows = grad_prep[3].astype(jnp.bfloat16)
    grad_beta_rows = grad_prep[4].astype(jnp.bfloat16)
    grad_query = jnp.dot(normed_one.T, grad_query_rows, preferred_element_type=jnp.float32)
    grad_key = jnp.dot(normed_one.T, grad_key_rows, preferred_element_type=jnp.float32)
    grad_value = jnp.dot(normed_one.T, grad_value_rows, preferred_element_type=jnp.float32)
    grad_outgate = jnp.dot(normed_one.T, grad_gate_out, preferred_element_type=jnp.float32)
    grad_decay = jnp.dot(normed_one.T, grad_decay_rows, preferred_element_type=jnp.float32)
    grad_beta = jnp.dot(normed_one.T, grad_beta_rows, preferred_element_type=jnp.float32)
    back_one_part = (
        jnp.dot(grad_query_rows, gathered[1].T, preferred_element_type=jnp.float32)
        + jnp.dot(grad_key_rows, gathered[2].T, preferred_element_type=jnp.float32)
        + jnp.dot(grad_value_rows, gathered[3].T, preferred_element_type=jnp.float32)
        + jnp.dot(grad_gate_out, gathered[4].T, preferred_element_type=jnp.float32)
        + jnp.dot(grad_decay_rows, gathered[5].T, preferred_element_type=jnp.float32)
        + jnp.dot(grad_beta_rows, gathered[6].T, preferred_element_type=jnp.float32)
    )
    back_one, outgain_sum = (
        lax.psum(back_one_part.astype(jnp.bfloat16), "tp").astype(jnp.float32),
        lax.psum(outgain_part.astype(jnp.bfloat16), "tp").astype(jnp.float32),
    )
    grad_mixer_gain = jnp.sum(back_one * inputs * inv_one, axis=0)
    grad_input = (
        grad_middle + rms_back(inputs, inv_one, gathered[0].astype(jnp.float32), back_one)
    ).astype(jnp.bfloat16)
    returned = (
        lax.all_to_all(result[back_order], "ctx", split_axis=0, concat_axis=0, tiled=True),
        lax.all_to_all(grad_input[back_order], "ctx", split_axis=0, concat_axis=0, tiled=True),
    )
    block_out = returned[0][send_slot][None]
    grad_tokens = returned[1][send_slot][None]
    tile_rows = ctx_count * fs_count
    decay_log_rows = jnp.broadcast_to(grad_prep[8][None, :], (tile_rows, head_count))
    decay_bias_rows = jnp.broadcast_to(grad_prep[9][None, :], (tile_rows, head_count))
    reduced = (
        lax.psum_scatter(
            regroup(grad_mixer_gain, ctx_count, fs_count),
            ("ctx", "fs"),
            scatter_dimension=0,
            tiled=True,
        ),
        lax.psum_scatter(
            regroup(grad_query, ctx_count, fs_count), ("ctx", "fs"), scatter_dimension=0, tiled=True
        ),
        lax.psum_scatter(
            regroup(grad_key, ctx_count, fs_count), ("ctx", "fs"), scatter_dimension=0, tiled=True
        ),
        lax.psum_scatter(
            regroup(grad_value, ctx_count, fs_count), ("ctx", "fs"), scatter_dimension=0, tiled=True
        ),
        lax.psum_scatter(
            regroup(grad_outgate, ctx_count, fs_count),
            ("ctx", "fs"),
            scatter_dimension=0,
            tiled=True,
        ),
        lax.psum_scatter(
            regroup(grad_decay, ctx_count, fs_count), ("ctx", "fs"), scatter_dimension=0, tiled=True
        ),
        lax.psum_scatter(
            regroup(grad_beta, ctx_count, fs_count), ("ctx", "fs"), scatter_dimension=0, tiled=True
        ),
        lax.psum_scatter(
            regroup(grad_prep[5], ctx_count, fs_count),
            ("ctx", "fs"),
            scatter_dimension=0,
            tiled=True,
        ),
        lax.psum_scatter(
            regroup(grad_prep[6], ctx_count, fs_count),
            ("ctx", "fs"),
            scatter_dimension=0,
            tiled=True,
        ),
        lax.psum_scatter(
            regroup(grad_prep[7], ctx_count, fs_count),
            ("ctx", "fs"),
            scatter_dimension=0,
            tiled=True,
        ),
        lax.psum_scatter(decay_log_rows, ("ctx", "fs"), scatter_dimension=0, tiled=True),
        lax.psum_scatter(decay_bias_rows, ("ctx", "fs"), scatter_dimension=0, tiled=True),
        lax.psum_scatter(
            regroup(outgain_sum, ctx_count, fs_count),
            ("ctx", "fs"),
            scatter_dimension=0,
            tiled=True,
        ),
        lax.psum_scatter(
            regroup(grad_output, ctx_count, fs_count),
            ("ctx", "fs"),
            scatter_dimension=0,
            tiled=True,
        ),
        lax.psum_scatter(
            regroup(grad_mlp_gain, ctx_count, fs_count),
            ("ctx", "fs"),
            scatter_dimension=0,
            tiled=True,
        ),
        lax.psum_scatter(
            regroup(grad_gate, ctx_count, fs_count), ("ctx", "fs"), scatter_dimension=0, tiled=True
        ),
        lax.psum_scatter(
            regroup(grad_up, ctx_count, fs_count), ("ctx", "fs"), scatter_dimension=0, tiled=True
        ),
        lax.psum_scatter(
            regroup(grad_down, ctx_count, fs_count), ("ctx", "fs"), scatter_dimension=0, tiled=True
        ),
    )
    spread = (
        lax.all_gather(reduced[0].astype(jnp.bfloat16), "ctx", axis=0, tiled=True).astype(
            jnp.float32
        ),
        lax.all_gather(reduced[1].astype(jnp.bfloat16), "ctx", axis=0, tiled=True).astype(
            jnp.float32
        ),
        lax.all_gather(reduced[2].astype(jnp.bfloat16), "ctx", axis=0, tiled=True).astype(
            jnp.float32
        ),
        lax.all_gather(reduced[3].astype(jnp.bfloat16), "ctx", axis=0, tiled=True).astype(
            jnp.float32
        ),
        lax.all_gather(reduced[4].astype(jnp.bfloat16), "ctx", axis=0, tiled=True).astype(
            jnp.float32
        ),
        lax.all_gather(reduced[5].astype(jnp.bfloat16), "ctx", axis=0, tiled=True).astype(
            jnp.float32
        ),
        lax.all_gather(reduced[6].astype(jnp.bfloat16), "ctx", axis=0, tiled=True).astype(
            jnp.float32
        ),
        lax.all_gather(reduced[7].astype(jnp.bfloat16), "ctx", axis=0, tiled=True).astype(
            jnp.float32
        ),
        lax.all_gather(reduced[8].astype(jnp.bfloat16), "ctx", axis=0, tiled=True).astype(
            jnp.float32
        ),
        lax.all_gather(reduced[9].astype(jnp.bfloat16), "ctx", axis=0, tiled=True).astype(
            jnp.float32
        ),
        lax.all_gather(reduced[10].astype(jnp.bfloat16), "ctx", axis=0, tiled=True).astype(
            jnp.float32
        ),
        lax.all_gather(reduced[11].astype(jnp.bfloat16), "ctx", axis=0, tiled=True).astype(
            jnp.float32
        ),
        lax.all_gather(reduced[12].astype(jnp.bfloat16), "ctx", axis=0, tiled=True).astype(
            jnp.float32
        ),
        lax.all_gather(reduced[13].astype(jnp.bfloat16), "ctx", axis=0, tiled=True).astype(
            jnp.float32
        ),
        lax.all_gather(reduced[14].astype(jnp.bfloat16), "ctx", axis=0, tiled=True).astype(
            jnp.float32
        ),
        lax.all_gather(reduced[15].astype(jnp.bfloat16), "ctx", axis=0, tiled=True).astype(
            jnp.float32
        ),
        lax.all_gather(reduced[16].astype(jnp.bfloat16), "ctx", axis=0, tiled=True).astype(
            jnp.float32
        ),
        lax.all_gather(reduced[17].astype(jnp.bfloat16), "ctx", axis=0, tiled=True).astype(
            jnp.float32
        ),
    )
    return (
        block_out,
        grad_tokens,
        spread[0],
        spread[1],
        spread[2],
        spread[3],
        spread[4],
        spread[5],
        spread[6],
        spread[7],
        spread[8],
        spread[9],
        spread[10][0],
        spread[11][0],
        spread[12],
        spread[13],
        spread[14],
        spread[15],
        spread[16],
        spread[17],
    )


def solution(mesh):
    in_specs = (
        P("fs", "ctx", None),
        P("fs", "ctx", None),
        P("fs", None),
        P("fs", None),
        P("fs"),
        P("fs", "tp"),
        P("fs", "tp"),
        P("fs", "tp"),
        P("fs", "tp"),
        P("fs", "tp"),
        P("fs", "tp"),
        P(("tp", "fs"), None),
        P(("tp", "fs"), None),
        P(("tp", "fs"), None),
        P("tp"),
        P("tp"),
        P("fs"),
        P(("tp", "fs"), None),
        P("fs"),
        P("fs", "tp"),
        P("fs", "tp"),
        P(("tp", "fs"), None),
    )
    out_specs = (
        P("fs", "ctx", None),
        P("fs", "ctx", None),
        P("fs"),
        P("fs", "tp"),
        P("fs", "tp"),
        P("fs", "tp"),
        P("fs", "tp"),
        P("fs", "tp"),
        P("fs", "tp"),
        P(("tp", "fs"), None),
        P(("tp", "fs"), None),
        P(("tp", "fs"), None),
        P("tp"),
        P("tp"),
        P("fs"),
        P(("tp", "fs"), None),
        P("fs"),
        P("fs", "tp"),
        P("fs", "tp"),
        P(("tp", "fs"), None),
    )
    return jax.shard_map(
        per_device, mesh=mesh, in_specs=in_specs, out_specs=out_specs, check_vma=False
    )
```

profile of v0, /device:TPU:0, one launch (start us, length us, event | category | flops | bytes accessed | tf_op | source)
XLA Modules:
  0.0 2734.5 jit_solution(18320694290137072650)
XLA Ops:
  9.5 30.5 %scatter_custom_fusion = s32[8192]{0:T(1024)S(1)} fusion(s32[8192]{0:T(1024)S(1)} %bitcast.686, s32[8192]{0:T(1024)S(1)} %iota.175, s32[]{:T(128)} %constant.290.clone.1), kind=kCustom, calls=%fused_computation.392 | custom fusion | bytes 32772 | tf_op jit(solution)/shard_map/scatter | solution.py:266
  73.1 33.5 %all-to-all-done = bf16[8,128,1024]{2,1,0:T(8,128)(2,1)S(1)} async-done(((bf16[8,128,1024]{2,1,0:T(8,128)(2,1)}), bf16[8,128,1024]{2,1,0:T(8,128)(2,1)S(1)}, u32[]{:S(2)}, u32[]{:S(2)}) %all-to-all-start) | async-done | bytes 2097184 | tf_op jit(solution)/shard_map/all_to_all | solution.py:287
  163.6 316.0 %custom-call.16 = f32[16,4,1,64,64]{3,4,2,1,0:T(8,128)} custom-call(f32[16,4,1,64,64]{4,3,2,1,0:T(8,128)} %get-tuple-element.961), custom_call_target="InvertDiagBlocksLowerTriangular" | custom-call | tf_op jit(solution)/shard_map/jvp(jit(_solve_triangular))/vmap(vmap())/triangular_solve | solution.py:168
  527.5 51.0 %while.96 = (s32[]{:T(128)}, f32[4,128,128]{2,1,0:T(8,128)S(1)}, f32[4,128,256]{2,1,0:T(8,128)S(1)}, f32[16,4,128,128]{3,2,1,0:T(8,128)}, f32[16,4,128,256]{3,2,1,0:T(8,128)}, /*index=5*/s32[]{:T(128)}, s32[]{:T(128)}) while((s32[]{:T(128)}, f32[4,128,128]{2,1,0:T(8,128)S(1)}, f32[4,128,256]{2,1,0:T(8,128)S(1)}, ...), condition=%wide.region_12.13_spmd.clone, body=%wide.region_11.12_spmd.clone.sunk | while | flops 302252032 | bytes 4195938 | solution.py:219
  627.8 74.5 %all-gather.61.cloned.1.call-done = f32[32,128,256]{2,1,0:T(8,128)} async-done(((f32[4,128,256]{2,1,0:T(8,128)}), f32[32,128,256]{2,1,0:T(8,128)}) %all-gather.61.cloned.1.call-update) | async-done | bytes 4194320 | tf_op jit(solution)/shard_map/all_gather | solution.py:24
  719.4 79.3 %while.94 = (s32[]{:T(128)}, f32[4,128,256]{2,1,0:T(8,128)S(1)}, f32[16,4,64,256]{3,1,2,0:T(4,128)}, f32[16,4,128,256]{3,2,1,0:T(8,128)}, f32[16,4,128,128]{3,2,...) while((s32[]{:T(128)}, f32[4,128,256]{2,1,0:T(8,128)S(1)}, ...), condition=%wide.region_17.18_spmd, body=%wide.region_16.17_spmd.sunk | while | flops 302186496 | bytes 5638253 | solution.py:204
  841.3 44.6 %all-to-all-done.2 = bf16[8,128,1024]{2,1,0:T(8,128)(2,1)S(1)} async-done(((bf16[8,128,1024]{2,1,0:T(8,128)(2,1)}), bf16[8,128,1024]{2,1,0:T(8,128)(2,1)S(1)}, u32[]{:S(2)}, u32[]{:S(2)}) %all-to-all-start.2) | async-done | bytes 2097184 | tf_op jit(solution)/shard_map/all_to_all | solution.py:288
  891.5 42.3 %all-reduce.41.cloned.1.call-done = f32[1024,1024]{1,0:T(8,128)} async-done(((f32[1024,1024]{1,0:T(8,128)}), f32[1024,1024]{1,0:T(8,128)}) %all-reduce.41.cloned.1.call-update) | async-done | bytes 4194320 | tf_op jit(solution)/shard_map/psum | solution.py:389
  1007.7 96.8 %all-reduce.43.cloned.1.call-done = f32[1024,1024]{1,0:T(8,128)} async-done(((f32[1024,1024]{1,0:T(8,128)}), f32[1024,1024]{1,0:T(8,128)}) %all-reduce.43.cloned.1.call-update) | async-done | bytes 4194320 | tf_op jit(solution)/shard_map/psum | solution.py:409
  1145.5 52.0 %while.98 = (s32[]{:T(128)}, f32[4,128,256]{2,1,0:T(8,128)S(1)}, f32[16,4,128,128]{2,3,1,0:T(8,128)}, f32[16,4,64,128]{3,2,1,0:T(8,128)}, f32[16,4,64,256]{3,2,1,0:T(8,128)}, /*index=5*/s32[]{:T(128)}, s32[]{:T(128)}, s32[]{:T(128)}) while((s32[]{:T(128)}, f32[4,128,256]{2,1,0:T(8,128)S(1)}, f32[16,4,128,128]{2,3,1,0:T(8,128)}, ...), condition=%wide.region_27.28_spmd.clone, body=%wide.region_26.27_spmd.clone.sunk | while | flops 302252032 | bytes 2753655 | solution.py:204
  1272.0 169.7 %while.95 = (s32[]{:T(128)}, f32[4,128,256]{2,1,0:T(8,128)S(1)}, f32[16,4,64,256]{3,2,1,0:T(8,128)}, f32[16,4,64,128]{3,2,1,0:T(8,128)}, f32[16,4,128,128]{2,3,1...) while((s32[]{:T(128)}, f32[4,128,256]{2,1,0:T(8,128)S(1)}, ...), condition=%wide.region_31.32_spmd, body=%wide.region_30.31_spmd.sunk | while | flops 604110848 | bytes 6557333 | solution.py:204
  1714.1 57.2 %all-reduce.45.cloned.1.call-done = (bf16[1024,1024]{1,0:T(8,128)(2,1)}, bf16[1024,1024]{1,0:T(8,128)(2,1)}) async-done(((bf16[1024,1024]{1,0:T(8,128)(2,1)}, bf16[1024,1024]{1,0:T(8,128)(2,1)}), (bf16[1024,1024]{1,0:T(8,128)(2,1)}, bf16[1024,1024]{1,0:T(8,128)(2,1)})) %all-reduce.45.cloned.1.call-update) | async-done | bytes 4194320 | tf_op jit(solution)/shard_map/psum | solution.py:399
  1785.8 83.0 %reduce-scatter.30.cloned.1.call-done = f32[64,1024]{1,0:T(8,128)} async-done(((f32[1024,1024]{1,0:T(8,128)}), f32[64,1024]{1,0:T(8,128)}) %reduce-scatter.30.cloned.1.call-update) | async-done | bytes 262160 | tf_op jit(solution)/shard_map/reduce_scatter | solution.py:500
  1870.5 73.5 %reduce-scatter.32.cloned.1.call-done = f32[64,1024]{1,0:T(8,128)} async-done(((f32[1024,1024]{1,0:T(8,128)}), f32[64,1024]{1,0:T(8,128)}) %reduce-scatter.32.cloned.1.call-update) | async-done | bytes 262160 | tf_op jit(solution)/shard_map/reduce_scatter | solution.py:538
  1975.6 37.4 %reduce-scatter.44.cloned.1.call-done = f32[32,4]{1,0:T(8,128)} async-done(((f32[512,4]{1,0:T(8,128)}), f32[32,4]{1,0:T(8,128)}) %reduce-scatter.44.cloned.1.call-update) | async-done | bytes 528
  2013.8 57.2 %reduce-scatter.46.cloned.1.call-done = f32[32,4]{1,0:T(8,128)} async-done(((f32[512,4]{1,0:T(8,128)}), f32[32,4]{1,0:T(8,128)}) %reduce-scatter.46.cloned.1.call-update) | async-done | bytes 528
  2071.9 18.6 all-gather.9
  2106.8 40.1 %reduce-scatter.28.cloned.1.call-done = f32[64,1024]{1,0:T(8,128)} async-done(((f32[1024,1024]{1,0:T(8,128)}), f32[64,1024]{1,0:T(8,128)}) %reduce-scatter.28.cloned.1.call-update) | async-done | bytes 262160 | tf_op jit(solution)/shard_map/reduce_scatter | solution.py:497
  2149.8 55.9 %reduce-scatter.40.cloned.1.call-done = f32[64,4]{1,0:T(8,128)} async-done(((f32[1024,4]{1,0:T(8,128)}), f32[64,4]{1,0:T(8,128)}) %reduce-scatter.40.cloned.1.call-update) | async-done | bytes 1040
  2206.6 18.6 all-gather.7
  2225.8 39.3 %reduce-scatter.42.cloned.1.call-done = f32[64,4]{1,0:T(8,128)} async-done(((f32[1024,4]{1,0:T(8,128)}), f32[64,4]{1,0:T(8,128)}) %reduce-scatter.42.cloned.1.call-update) | async-done | bytes 1040
  2266.0 18.6 all-gather.8
  2285.2 38.1 %reduce-scatter.48.cloned.1.call-done = f32[64,4]{1,0:T(8,128)} async-done(((f32[1024,4]{1,0:T(8,128)}), f32[64,4]{1,0:T(8,128)}) %reduce-scatter.48.cloned.1.call-update) | async-done | bytes 1040
  2324.2 18.6 all-gather.11
  2343.5 45.1 %reduce-scatter.24.cloned.1.call-done = f32[64,512]{1,0:T(8,128)} async-done(((f32[1024,512]{1,0:T(8,128)}), f32[64,512]{1,0:T(8,128)}) %reduce-scatter.24.cloned.1.call-update) | async-done | bytes 131088 | tf_op jit(solution)/shard_map/reduce_scatter | solution.py:491
  2389.5 31.5 %all_gather.151 = bf16[512,512]{1,0:T(8,128)(2,1)S(1)} all-gather(bf16[64,512]{1,0:T(8,128)(2,1)S(1)} %convert_element_type.311), channel_id=1, replica_groups=mesh['ctx'=8,'tp'=2,'fs'=2] {'ctx'}, dimensions={0}, use_global_device_ids=true | all-gather | bytes 589824 | tf_op jit(solution)/shard_map/all_gather | solution.py:564
  2422.1 31.4 %reduce-scatter.26.cloned.1.call-done = f32[64,512]{1,0:T(8,128)} async-done(((f32[1024,512]{1,0:T(8,128)}), f32[64,512]{1,0:T(8,128)}) %reduce-scatter.26.cloned.1.call-update) | async-done | bytes 131088 | tf_op jit(solution)/shard_map/reduce_scatter | solution.py:494
  2454.4 31.9 %all_gather.152 = bf16[512,512]{1,0:T(8,128)(2,1)S(1)} all-gather(bf16[64,512]{1,0:T(8,128)(2,1)S(1)} %convert_element_type.313), channel_id=1, replica_groups=mesh['ctx'=8,'tp'=2,'fs'=2] {'ctx'}, dimensions={0}, use_global_device_ids=true | all-gather | bytes 589824 | tf_op jit(solution)/shard_map/all_gather | solution.py:567
  2501.7 41.2 %all-gather.57.cloned.1.call-done = bf16[512,1408]{1,0:T(8,128)(2,1)} async-done(((bf16[64,1408]{1,0:T(8,128)(2,1)}), bf16[512,1408]{1,0:T(8,128)(2,1)}) %all-gather.57.cloned.1.call-update) | async-done | bytes 1441808 | tf_op jit(solution)/shard_map/all_gather | solution.py:609
  2546.1 40.7 %all-gather.59.cloned.1.call-done = bf16[704,1024]{1,0:T(8,128)(2,1)} async-done(((bf16[88,1024]{1,0:T(8,128)(2,1)}), bf16[704,1024]{1,0:T(8,128)(2,1)}) %all-gather.59.cloned.1.call-update) | async-done | bytes 1441808 | tf_op jit(solution)/shard_map/all_gather | solution.py:612
  2590.2 58.4 %all-reduce.34 = (bf16[1024]{0:T(1024)(128)(2,1)S(1)}, bf16[16,4]{1,0:T(8,128)(2,1)S(1)}, bf16[16,4]{1,0:T(8,128)(2,1)S(1)}, bf16[256]{0:T(256)(128)(2,1)S(1)}, bf16[1024]{0:T(1024)(128)(2,1)S(1)}) all-reduce(f32[1024]{0:T(1024)S(1)} %reshape.657, ...), channel_id=6, replica_groups=mesh['ctx'=8,'tp'=2,'fs'=2] {'ctx','fs'}, use_global_device_ids=true, to_apply=%region_45.47.clone | all-reduce | flops 2432 | bytes 14080
  2666.3 18.0 all-gather.13
  (1188 shorter events, 1244.0 us)
Async XLA Ops:
  58.3 526.5 %all-gather.37.cloned.1.call-start = ((), (), s32[]{:S(2)}) async-start(), calls=%async_computation.19 | async-start | bytes 1572864 | tf_op jit(solution)/shard_map/all_gather | solution.py:315
  59.1 568.7 %all-gather.63.cloned.1.call-start = ((), (), s32[]{:S(2)}) async-start(), calls=%async_computation.42 | async-start | bytes 2359296 | tf_op jit(solution)/shard_map/all_gather | solution.py:24
  133.9 362.8 %collective-permute-start.1 = (f32[3,1024]{1,0:T(4,128)}, f32[3,1024]{1,0:T(4,128)}, u32[]{:S(2)}, u32[]{:S(2)}) collective-permute-start(f32[3,1024]{1,0:T(4,128)} %slice.237), channel_id=1, source_target_pairs={{0,4},{4,8},{8,12},{12,16},{16,20},{20,24},{24,28},{1,5},{5,9},{9,... | collective-permute-start | bytes 36872 | tf_op jit(solution)/shard_map/ppermute | solution.py:19
  579.8 230.2 %all-gather.39.cloned.1.call-start = ((), (), s32[]{:S(2)}) async-start(), calls=%async_computation.20 | async-start | bytes 3145728 | tf_op jit(solution)/shard_map/all_gather | solution.py:318
  580.4 240.6 %all-gather.41.cloned.1.call-start = ((), (), s32[]{:S(2)}) async-start(), calls=%async_computation.21 | async-start | bytes 3145728 | tf_op jit(solution)/shard_map/all_gather | solution.py:325
  581.1 352.7 %all-reduce.41.cloned.1.call-start = ((), (), s32[]{:S(2)}) async-start(), calls=%async_computation.22 | async-start | bytes 8388608 | tf_op jit(solution)/shard_map/psum | solution.py:389
  838.7 137.5 %all-gather.47.cloned.1.call-start = ((), (), s32[]{:S(2)}) async-start(), calls=%async_computation.25 | async-start | bytes 4325376 | tf_op jit(solution)/shard_map/all_gather | solution.py:329
  839.4 265.1 %all-reduce.43.cloned.1.call-start = ((), (), s32[]{:S(2)}) async-start(), calls=%async_computation.26 | async-start | bytes 8388608 | tf_op jit(solution)/shard_map/psum | solution.py:409
  995.4 241.5 %all-gather.67.cloned.1.call-start = ((), (), s32[]{:S(2)}) async-start(), calls=%async_computation.44 | async-start | bytes 1179648 | tf_op jit(solution)/shard_map/all_gather | solution.py:39
  1001.7 246.0 %all-gather.65.cloned.1.call-start = ((), (), s32[]{:S(2)}) async-start(), calls=%async_computation.43 | async-start | bytes 2359296 | tf_op jit(solution)/shard_map/all_gather | solution.py:39
  1198.3 506.1 %reduce-scatter.34.cloned.1.call-start = ((), (), s32[]{:S(2)}) async-start(), calls=%async_computation.35 | async-start | bytes 6127616 | tf_op jit(solution)/shard_map/reduce_scatter | solution.py:550
  1206.8 499.3 %reduce-scatter.36.cloned.1.call-start = ((), (), s32[]{:S(2)}) async-start(), calls=%async_computation.37 | async-start | bytes 6127616 | tf_op jit(solution)/shard_map/reduce_scatter | solution.py:553
  1215.1 492.8 %reduce-scatter.38.cloned.1.call-start = ((), (), s32[]{:S(2)}) async-start(), calls=%async_computation.39 | async-start | bytes 6127616 | tf_op jit(solution)/shard_map/reduce_scatter | solution.py:556
  1224.8 546.4 %all-reduce.45.cloned.1.call-start = ((), (), s32[]{:S(2)}) async-start(), calls=%async_computation.50 | async-start | bytes 8388608 | tf_op jit(solution)/shard_map/psum | solution.py:399
  1659.9 208.9 %reduce-scatter.30.cloned.1.call-start = ((), (), s32[]{:S(2)}) async-start(), calls=%async_computation.31 | async-start | bytes 4456448 | tf_op jit(solution)/shard_map/reduce_scatter | solution.py:500
  1672.4 271.6 %reduce-scatter.32.cloned.1.call-start = ((), (), s32[]{:S(2)}) async-start(), calls=%async_computation.33 | async-start | bytes 4456448 | tf_op jit(solution)/shard_map/reduce_scatter | solution.py:538
  1684.3 328.7 %reduce-scatter.44.cloned.1.call-start = ((), (), s32[]{:S(2)}) async-start(), calls=%async_computation.47 | async-start | bytes 278528
  1685.4 385.7 %reduce-scatter.46.cloned.1.call-start = ((), (), s32[]{:S(2)}) async-start(), calls=%async_computation.48 | async-start | bytes 278528
  1686.4 460.4 %reduce-scatter.28.cloned.1.call-start = ((), (), s32[]{:S(2)}) async-start(), calls=%async_computation.29 | async-start | bytes 4456448 | tf_op jit(solution)/shard_map/reduce_scatter | solution.py:497
  1692.8 512.9 %reduce-scatter.40.cloned.1.call-start = ((), (), s32[]{:S(2)}) async-start(), calls=%async_computation.45 | async-start | bytes 557056
  1694.4 570.7 %reduce-scatter.42.cloned.1.call-start = ((), (), s32[]{:S(2)}) async-start(), calls=%async_computation.46 | async-start | bytes 557056
  1696.0 627.3 %reduce-scatter.48.cloned.1.call-start = ((), (), s32[]{:S(2)}) async-start(), calls=%async_computation.49 | async-start | bytes 557056
  1697.3 691.3 %reduce-scatter.24.cloned.1.call-start = ((), (), s32[]{:S(2)}) async-start(), calls=%async_computation.27 | async-start | bytes 2228224 | tf_op jit(solution)/shard_map/reduce_scatter | solution.py:491
  1700.2 753.3 %reduce-scatter.26.cloned.1.call-start = ((), (), s32[]{:S(2)}) async-start(), calls=%async_computation.28 | async-start | bytes 2228224 | tf_op jit(solution)/shard_map/reduce_scatter | solution.py:494
  1704.3 794.3 %all-gather.55.cloned.1.call-start = ((), (), s32[]{:S(2)}) async-start(), calls=%async_computation.36 | async-start | bytes 1622016 | tf_op jit(solution)/shard_map/all_gather | solution.py:606
  1706.0 836.9 %all-gather.57.cloned.1.call-start = ((), (), s32[]{:S(2)}) async-start(), calls=%async_computation.38 | async-start | bytes 1622016 | tf_op jit(solution)/shard_map/all_gather | solution.py:609
  1707.8 879.0 %all-gather.59.cloned.1.call-start = ((), (), s32[]{:S(2)}) async-start(), calls=%async_computation.40 | async-start | bytes 1622016 | tf_op jit(solution)/shard_map/all_gather | solution.py:612
  1780.2 181.7 %all-to-all-start.1 = ((bf16[8,128,1024]{2,1,0:T(8,128)(2,1)}), bf16[8,128,1024]{2,1,0:T(8,128)(2,1)S(1)}, u32[]{:S(2)}, u32[]{:S(2)}) async-start(bf16[8,128,1024]{2,1,0:T(8,128)(2,1)} %bitcast.624), calls=%async_computation.1 | async-start | bytes 4194304 | tf_op jit(solution)/shard_map/all_to_all | solution.py:476
  1785.8 919.7 %all-gather.51.cloned.1.call-start = ((), (), s32[]{:S(2)}) async-start(), calls=%async_computation.32 | async-start | bytes 1179648 | tf_op jit(solution)/shard_map/all_gather | solution.py:573
  1870.4 837.8 %all-gather.53.cloned.1.call-start = ((), (), s32[]{:S(2)}) async-start(), calls=%async_computation.34 | async-start | bytes 1179648 | tf_op jit(solution)/shard_map/all_gather | solution.py:600
  1962.0 754.4 %all-to-all-start.3 = ((bf16[8,128,1024]{2,1,0:T(8,128)(2,1)}), bf16[8,128,1024]{2,1,0:T(8,128)(2,1)}, u32[]{:S(2)}, u32[]{:S(2)}) async-start(bf16[8,128,1024]{2,1,0:T(8,128)(2,1)} %bitcast.621), calls=%async_computation.3 | async-start | bytes 4194304 | tf_op jit(solution)/shard_map/all_to_all | solution.py:477
  1966.5 758.0 %all-gather.49.cloned.1.call-start = ((), (), s32[]{:S(2)}) async-start(), calls=%async_computation.30 | async-start | bytes 1179648 | tf_op jit(solution)/shard_map/all_gather | solution.py:570
  (230 other events, 7278.7 us)
Sparse Core Ops, SparseCore 0:
  9.6 11.7 all-gather.32
  22.9 11.7 all-gather.34
  579.3 48.3 all-gather.62
  630.3 71.8 all-gather.60
  714.1 11.7 all-gather.40
  827.7 106.0 all-reduce.40
  935.4 11.7 all-gather.42
  948.7 12.8 all-gather.44
  963.2 12.8 all-gather.46
  995.5 108.9 all-reduce.42
  1107.2 40.1 all-gather.66
  1198.4 49.2 all-gather.64
  1251.5 80.0 reduce-scatter.33
  1335.3 80.7 reduce-scatter.35
  1419.9 80.7 reduce-scatter.37
  1660.0 111.1 all-reduce.44
  1775.6 93.1 reduce-scatter.29
  1872.5 71.4 reduce-scatter.31
  1947.9 65.0 reduce-scatter.43
  2016.9 54.0 reduce-scatter.45
  2075.4 71.3 reduce-scatter.27
  2150.8 54.8 reduce-scatter.39
  2210.3 54.7 reduce-scatter.41
  2268.5 54.7 reduce-scatter.47
  2328.0 60.5 reduce-scatter.23
  2392.9 60.5 reduce-scatter.25
  2455.9 42.5 all-gather.54
  2500.8 42.0 all-gather.56
  2545.4 41.3 all-gather.58
  2589.1 38.6 all-gather.50
  2630.1 38.9 all-gather.52
  2671.4 39.0 all-gather.48
  (2 shorter events, 19.2 us)
where the time goes:
time: 2750 us; the launch traced here: 2730 us
  waiting for transfers between devices  981 us (36%)
  matrix products  606 us (22%)
  other arithmetic  481 us (17%)
  local copies, waits for them, and re-layouts  324 us (12%)
  blocking collectives  284 us (10%)
  starting transfers between devices  35.1 us (1%)
    another operation x4, other arithmetic, block_parts(): jax.scipy.linalg.solve_triangular(system, (beta_vals * entry_gain)[..., N...  317 us
    unnamed x39, waiting for transfers between devices  234 us
    dot_general x64, matrix products, run_advance(): jnp.einsum('awg,ago->awo', query_effective, running_state, precision=prec...  116 us
    dot_general x64, matrix products, run_advance(): jnp.einsum('clf,cfq->clq', transfer_matrix, running_state, precision=prec...  115 us
    psum x1, waiting for transfers between devices, per_device(): lax.psum(jnp.dot(grad_gate_rows, gathered[13].T, preferred_element_type=j...  96.8 us
    reduce_scatter x1, waiting for transfers between devices, per_device(): lax.psum_scatter(regroup(grad_outgate, ctx_count, fs_count), ('ctx', 'fs'...  83 us
    unnamed x2, blocking collectives  76 us
    all_gather x2, waiting for transfers between devices, entering_2(): pieces = jax.tree.map(lambda part: lax.all_gather(part, axis), value)  74.9 us
  transfers between devices with their start and end apart: 44, of which 26 were waited for; matrix products, arithmetic and copies ran while one was open for 49% of the time, Pallas kernels for 0%

commit v1 on v0

v1 whole, which is shorter than its diff:
```python
import functools

import jax
import jax.numpy as jnp
from jax import lax
from jax.experimental import pallas as pl
from jax.experimental.pallas import tpu as pltpu
from jax.sharding import PartitionSpec as P

TAPS = 4
CHUNK = 128
EPS = 1e-6
LANES = 128
START, VALID, AHEAD = 8, 8, 11
HI = lax.Precision.HIGHEST
bf16 = jnp.bfloat16
f32 = jnp.float32
MIB = 1024 * 1024


def mm(a, b):
    return jnp.dot(a.astype(bf16), b.astype(bf16), preferred_element_type=f32)


def mm_nt(a, b):
    return lax.dot_general(
        a.astype(bf16), b.astype(bf16), (((1,), (1,)), ((), ())), preferred_element_type=f32
    )


def mm_tn(a, b):
    return lax.dot_general(
        a.astype(bf16), b.astype(bf16), (((0,), (0,)), ((), ())), preferred_element_type=f32
    )


def mm_hi(a, b):
    return jnp.dot(a, b, precision=HI, preferred_element_type=f32)


def silu(x):
    return x * jax.nn.sigmoid(x)


def silu_grad(x):
    s = jax.nn.sigmoid(x)
    return s * (1.0 + x * (1.0 - s))


def softplus(x):
    return jnp.maximum(x, 0.0) + jnp.log1p(jnp.exp(-jnp.abs(x)))


def grid_of(rows, cols):
    return (
        lax.broadcasted_iota(jnp.int32, (rows, cols), 0),
        lax.broadcasted_iota(jnp.int32, (rows, cols), 1),
    )


def lower_inverses(systems):
    size = systems[0].shape[0]
    row, col = grid_of(size, size)
    eye = (row == col).astype(f32)
    first = ((row >> 1) == (col >> 1)) & (row > col)
    inverses = [eye - jnp.where(first, low, 0.0) for low in systems]
    level = 1
    while (1 << level) < size:
        block = (
            ((row >> (level + 1)) == (col >> (level + 1)))
            & (((row >> level) & 1) == 1)
            & (((col >> level) & 1) == 0)
        )
        parts = [mm(jnp.where(block, low, 0.0), inv) for low, inv in zip(systems, inverses)]
        inverses = [inv - mm(inv, part) for inv, part in zip(inverses, parts)]
        level += 1
    return inverses


def chunk_gates(cum, heads):
    size = cum.shape[0]
    row, col = grid_of(size, size)
    across = jnp.transpose(cum)
    seg_col = cum[:, START : START + 1]
    linked = (row >= col) & (seg_col == across[START : START + 1, :])
    from_start = seg_col == 0.0
    to_end = seg_col == cum[size - 1 : size, START : START + 1]
    out = []
    for h in range(heads):
        down = cum[:, h : h + 1]
        gap = jnp.where(linked, down - across[h : h + 1, :], 0.0)
        decay = jnp.where(linked, jnp.exp(gap), 0.0)
        entry = jnp.where(from_start, jnp.exp(down), 0.0)
        last = cum[size - 1 : size, h : h + 1]
        tail = jnp.where(to_end, jnp.exp(jnp.where(to_end, last - down, 0.0)), 0.0)
        out.append((decay, entry, tail, entry[size - 1 : size, :]))
    return out


def unit_scale(x):
    return lax.rsqrt(jnp.sum(x * x, axis=-1, keepdims=True) + EPS)


def forward_kernel(
    heads, dk, dv,
    proj, ab, flags, halo, taps, head,
    conv, local, qa, states, tinv, uval, wkey, qeff, ktail, cum_out, last,
    ext, state,
):
    step = pl.program_id(0)
    size = proj.shape[0]
    width = proj.shape[1]

    @pl.when(step == 0)
    def _():
        ext[0:8, :] = halo[...]
        row, col = grid_of(dk, dk)
        for h in range(heads):
            state[h, :, 0:dv] = jnp.zeros((dk, dv), f32)
            state[h, :, dv : dv + dk] = (row == col).astype(f32)

    @pl.when(step > 0)
    def _():
        ext[0:8, :] = ext[size : size + 8, :]

    ext[8 : 8 + size, :] = proj[...]
    fl = flags[...]
    valid = [jnp.broadcast_to(fl[:, VALID + s : VALID + s + 1], (size, LANES)) for s in (1, 2, 3)]
    for lo in range(0, width, LANES):
        at = slice(lo, lo + LANES)
        total = ext[8 : 8 + size, at] * taps[3:4, at]
        for s in (1, 2, 3):
            total += ext[8 - s : 8 - s + size, at] * taps[3 - s : 4 - s, at] * valid[s - 1]
        conv[:, at] = total

    raw = ab[...]
    lane = lax.broadcasted_iota(jnp.int32, (size, LANES), 1)
    log_decay = -jnp.exp(head[0:1, :]) * softplus(raw + head[1:2, :])
    row, col = grid_of(size, size)
    cum = mm_hi((row >= col).astype(f32), jnp.where(lane < heads, log_decay, fl))
    cum_out[...] = cum
    beta_all = jax.nn.sigmoid(raw)
    gates = chunk_gates(cum, heads)

    every = range(heads)
    betas = [beta_all[:, heads + h : heads + h + 1] for h in every]
    queries, keys, values = [], [], []
    for h in every:
        q = silu(conv[:, h * dk : (h + 1) * dk])
        k = silu(conv[:, (heads + h) * dk : (heads + h + 1) * dk])
        base = 2 * heads * dk + h * dv
        queries.append(q * unit_scale(q) * dk**-0.5)
        keys.append(k * unit_scale(k))
        values.append(silu(conv[:, base : base + dv]))
    keys16 = [k.astype(bf16) for k in keys]
    kk = [mm_nt(k, k) for k in keys16]
    qk = [mm_nt(q, k) for q, k in zip(queries, keys16)]
    strict = row > col
    systems = [jnp.where(strict, betas[h] * gates[h][0] * kk[h], 0.0) for h in every]
    inverses = lower_inverses(systems)
    solved = []
    for h in every:
        right = jnp.concatenate([betas[h] * values[h], (betas[h] * gates[h][1]) * keys[h]], axis=1)
        solved.append(mm(inverses[h], right))
    mixed = [mm(gates[h][0] * qk[h], solved[h]) for h in every]
    for h in every:
        before = state[h]
        before16 = before.astype(bf16)
        states[0, h] = before16
        w = solved[h][:, dv:].astype(bf16)
        q_now = (gates[h][1] * queries[h] - mixed[h][:, dv:]).astype(bf16)
        k_end = (gates[h][2] * keys[h]).astype(bf16)
        both = mm(jnp.concatenate([q_now, w], axis=0), before16)
        local[:, h * dv : (h + 1) * dv] = mixed[h][:, :dv] + both[:size, :dv]
        qa[:, h * dk : (h + 1) * dk] = both[:size, dv:].astype(bf16)
        fed = jnp.concatenate(
            [solved[h][:, :dv] - both[size:, :dv], -both[size:, dv:]], axis=1
        )
        after = gates[h][3] * before + mm_tn(k_end, fed)
        state[h] = after
        last[h] = after.astype(bf16)
        tinv[:, h * size : (h + 1) * size] = inverses[h].astype(bf16)
        uval[:, h * dv : (h + 1) * dv] = solved[h][:, :dv].astype(bf16)
        wkey[:, h * dk : (h + 1) * dk] = w
        qeff[:, h * dk : (h + 1) * dk] = q_now
        ktail[:, h * dk : (h + 1) * dk] = k_end


def vmem(limit=56):
    return pltpu.CompilerParams(vmem_limit_bytes=limit * MIB, dimension_semantics=("arbitrary",))


def whole(shape):
    return pl.BlockSpec(shape, lambda n: (0,) * len(shape))


def delta_forward(proj, flags, halo, taps, head, heads, dk, dv):
    rows = proj.shape[0]
    size = CHUNK
    steps = rows // size
    width = 2 * heads * dk + heads * dv
    ab_at = (width + heads * dv) // LANES

    def rowwise(cols):
        return pl.BlockSpec((size, cols), lambda n: (n, 0))

    outs = [
        ((rows, width), f32, rowwise(width)),
        ((rows, heads * dv), f32, rowwise(heads * dv)),
        ((rows, heads * dk), bf16, rowwise(heads * dk)),
        ((steps, heads, dk, dv + dk), bf16, pl.BlockSpec((1, heads, dk, dv + dk), lambda n: (n, 0, 0, 0))),
        ((rows, heads * size), bf16, rowwise(heads * size)),
        ((rows, heads * dv), bf16, rowwise(heads * dv)),
        ((rows, heads * dk), bf16, rowwise(heads * dk)),
        ((rows, heads * dk), bf16, rowwise(heads * dk)),
        ((rows, heads * dk), bf16, rowwise(heads * dk)),
        ((rows, LANES), f32, rowwise(LANES)),
        ((heads, dk, dv + dk), bf16, whole((heads, dk, dv + dk))),
    ]
    return pl.pallas_call(
        functools.partial(forward_kernel, heads, dk, dv),
        grid=(steps,),
        in_specs=[
            rowwise(width),
            pl.BlockSpec((size, LANES), lambda n: (n, ab_at)),
            rowwise(LANES),
            whole((8, width)),
            whole((8, width)),
            whole((8, LANES)),
        ],
        out_specs=[spec for _, _, spec in outs],
        out_shape=[jax.ShapeDtypeStruct(shape, kind) for shape, kind, _ in outs],
        scratch_shapes=[
            pltpu.VMEM((size + 8, width), f32),
            pltpu.VMEM((heads, dk, dv + dk), f32),
        ],
        compiler_params=vmem(),
        cost_estimate=pl.CostEstimate(
            flops=rows * heads * 2 * (16 * size * size + 8 * dk * (dv + dk)),
            bytes_accessed=rows * width * 14,
            transcendentals=rows * width * 2,
        ),
    )(proj, proj, flags, halo, taps, head)


def mix_kernel(heads, dk, dv, local, qa, entering, zgate, gain, wout, y_out, part_out):
    for h in range(heads):
        at = slice(h * dv, (h + 1) * dv)
        o = local[:, at] + mm(qa[:, h * dk : (h + 1) * dk], entering[h])
        so = lax.rsqrt(jnp.mean(o * o, axis=-1, keepdims=True) + EPS)
        y_out[:, at] = (o * so * gain[0:1, :] * silu(zgate[:, at])).astype(bf16)
    part_out[...] = mm(y_out[...], wout[...]).astype(part_out.dtype)


def delta_mix(local, qa, entering, proj, gain, wout, heads, dk, dv):
    rows = local.shape[0]
    size = 2 * CHUNK
    model = wout.shape[1]
    z_at = (2 * heads * dk + heads * dv) // (heads * dv)

    def rowwise(cols, at=0):
        return pl.BlockSpec((size, cols), lambda n: (n, at))

    return pl.pallas_call(
        functools.partial(mix_kernel, heads, dk, dv),
        grid=(rows // size,),
        in_specs=[
            rowwise(heads * dv),
            rowwise(heads * dk),
            whole((heads, dk, dv)),
            rowwise(heads * dv, z_at),
            whole((8, dv)),
            whole(wout.shape),
        ],
        out_specs=[rowwise(heads * dv), rowwise(model)],
        out_shape=[
            jax.ShapeDtypeStruct((rows, heads * dv), bf16),
            jax.ShapeDtypeStruct((rows, model), bf16),
        ],
        compiler_params=vmem(),
        cost_estimate=pl.CostEstimate(
            flops=2 * rows * heads * dv * (model + dk),
            bytes_accessed=rows * heads * dv * 14,
            transcendentals=rows * heads * dv,
        ),
    )(local, qa, entering, proj, gain, wout)


def back_kernel(
    heads, dk, dv,
    er, local, qa, entering, zgate, gain, wout, qeff, wkey, ktail, cum,
    dz_out, do_out, gain_out, first, state, gain_sum,
):
    step = pl.program_id(0)
    size = er.shape[0]

    @pl.when(step == 0)
    def _():
        state[...] = jnp.zeros_like(state)
        gain_sum[...] = jnp.zeros_like(gain_sum)

    dy = mm_nt(er[...], wout[...])
    ends = cum[size - 1 : size, :]
    for h in range(heads):
        at = slice(h * dv, (h + 1) * dv)
        kat = slice(h * dk, (h + 1) * dk)
        z = zgate[:, at]
        sig = jax.nn.sigmoid(z)
        act = z * sig
        o = local[:, at] + mm(qa[:, kat], entering[h])
        so = lax.rsqrt(jnp.mean(o * o, axis=-1, keepdims=True) + EPS)
        normed = o * so
        g = dy[:, at]
        scaled = gain[0:1, :] * g
        gain_sum[0:1, :] += jnp.sum(g * normed * act, axis=0, keepdims=True)
        dz_out[:, at] = (scaled * normed * (sig * (1.0 + z * (1.0 - sig)))).astype(bf16)
        back = scaled * act
        dots = jnp.mean(back * o, axis=-1, keepdims=True)
        do = (so * back - o * (so * so * so * dots)).astype(bf16)
        do_out[:, at] = do
        after = state[h]
        kept = jnp.where(ends[:, START : START + 1] == 0.0, jnp.exp(ends[:, h : h + 1]), 0.0)
        pulled = mm(ktail[:, kat], after)
        now = kept * after + mm_tn(
            jnp.concatenate([qeff[:, kat], wkey[:, kat]], axis=0),
            jnp.concatenate([do, (-pulled).astype(bf16)], axis=0),
        )
        state[h] = now
        first[h] = now.astype(bf16)
    gain_out[...] = gain_sum[...]


def delta_back(er, local, qa, entering, proj, gain, wout, qeff, wkey, ktail, cum, heads, dk, dv):
    rows, model = er.shape
    size = CHUNK
    steps = rows // size
    z_at = (2 * heads * dk + heads * dv) // (heads * dv)

    def rowwise(cols, at=0):
        return pl.BlockSpec((size, cols), lambda n: (steps - 1 - n, at))

    outs = [
        ((rows, heads * dv), bf16, rowwise(heads * dv)),
        ((rows, heads * dv), bf16, rowwise(heads * dv)),
        ((8, dv), f32, whole((8, dv))),
        ((heads, dk, dv), bf16, whole((heads, dk, dv))),
    ]
    return pl.pallas_call(
        functools.partial(back_kernel, heads, dk, dv),
        grid=(steps,),
        in_specs=[
            rowwise(model),
            rowwise(heads * dv),
            rowwise(heads * dk),
            whole((heads, dk, dv)),
            rowwise(heads * dv, z_at),
            whole((8, dv)),
            whole(wout.shape),
            rowwise(heads * dk),
            rowwise(heads * dk),
            rowwise(heads * dk),
            rowwise(LANES),
        ],
        out_specs=[spec for _, _, spec in outs],
        out_shape=[jax.ShapeDtypeStruct(shape, kind) for shape, kind, _ in outs],
        scratch_shapes=[pltpu.VMEM((heads, dk, dv), f32), pltpu.VMEM((8, dv), f32)],
        compiler_params=vmem(),
        cost_estimate=pl.CostEstimate(
            flops=2 * rows * heads * dv * (model + 4 * dk),
            bytes_accessed=rows * heads * dv * 18,
            transcendentals=rows * heads * dv,
        ),
    )(er, local, qa, entering, proj, gain, wout, qeff, wkey, ktail, cum)


def grad_kernel(
    heads, dk, dv,
    proj, conv, ab, flags, cum_in, halo, taps, head, do_in, tinv, uval, wkey, states, entering, leaving,
    dproj, dab, tail_rows, head_rows, dtaps, dhead,
    state, ext, tap_sum, head_sum,
):
    step = pl.program_id(0)
    steps = pl.num_programs(0)
    size = proj.shape[0]
    width = proj.shape[1]
    every = range(heads)

    @pl.when(step == 0)
    def _():
        state[...] = leaving[...].astype(f32)
        ext[size : size + 8, :] = jnp.zeros((8, width), f32)
        tap_sum[...] = jnp.zeros_like(tap_sum)
        head_sum[...] = jnp.zeros_like(head_sum)

    @pl.when(step > 0)
    def _():
        ext[size : size + 8, :] = ext[0:8, :]

    fl = flags[...]
    raw = ab[...]
    beta_all = jax.nn.sigmoid(raw)
    cum = cum_in[...]
    gates = chunk_gates(cum, heads)
    row, col = grid_of(size, size)
    strict = row > col
    betas = [beta_all[:, heads + h : heads + h + 1] for h in every]

    cq = [conv[:, h * dk : (h + 1) * dk] for h in every]
    ck = [conv[:, (heads + h) * dk : (heads + h + 1) * dk] for h in every]
    vbase = 2 * heads * dk
    sq = [silu(c) for c in cq]
    sk = [silu(c) for c in ck]
    rq = [unit_scale(s) for s in sq]
    rk = [unit_scale(s) for s in sk]
    queries = [s * r * dk**-0.5 for s, r in zip(sq, rq)]
    keys = [s * r for s, r in zip(sk, rk)]
    q16 = [q.astype(bf16) for q in queries]
    k16 = [k.astype(bf16) for k in keys]
    kk = [mm_nt(k, k) for k in k16]
    qk = [mm_nt(q, k) for q, k in zip(q16, k16)]
    attend = [gates[h][0] * qk[h] for h in every]
    weak = [jnp.where(strict, gates[h][0] * kk[h], 0.0) for h in every]

    dsum_row = jnp.zeros((LANES, size), f32)
    dsum_col = jnp.zeros((size, LANES), f32)
    end_add = jnp.zeros((1, LANES), f32)
    dbeta_all = jnp.zeros((size, LANES), f32)
    lane = lax.broadcasted_iota(jnp.int32, (size, LANES), 1)
    lane_row = lax.broadcasted_iota(jnp.int32, (1, LANES), 1)
    sub = lax.broadcasted_iota(jnp.int32, (LANES, size), 0)

    starts, users, dos, dstates, dks16 = [], [], [], [], []
    for h in every:
        entry16 = entering[h]
        start = states[0, h, :, 0:dv].astype(f32) + mm(states[0, h, :, dv : dv + dk], entry16)
        start16 = start.astype(bf16)
        both = mm(jnp.concatenate([wkey[:, h * dk : (h + 1) * dk], k16[h]], axis=0), start16)
        starts.append((start, start16, both[size:]))
        users.append((uval[:, h * dv : (h + 1) * dv].astype(f32) - both[:size]).astype(bf16))
        dos.append(do_in[:, h * dv : (h + 1) * dv])
        dstates.append(state[h])
    d16 = [d.astype(bf16) for d in dstates]
    du = [
        mm_tn(attend[h], dos[h]) + mm(gates[h][2] * keys[h], d16[h]) for h in every
    ]
    dright = [mm_tn(tinv[:, h * size : (h + 1) * size], du[h]) for h in every]
    for h in every:
        decay, entry, tail, kept = gates[h]
        beta = betas[h]
        start, start16, recalled = starts[h]
        dr = dright[h]
        pair = jnp.concatenate([dos[h], dr.astype(bf16)], axis=0)
        wide = mm_nt(pair, jnp.concatenate([users[h], start16], axis=0))
        dattend = wide[:size, :size]
        dqe = wide[:size, size:]
        dlow = -wide[size:, :size]
        dke = -beta * wide[size:, size:]
        user_end = mm_nt(users[h], d16[h])
        state[h] = kept * dstates[h] + mm_tn(
            jnp.concatenate([entry * queries[h], -(beta * entry) * keys[h]], axis=0), pair
        )
        dqk = dattend * decay
        dkk = jnp.where(strict, dlow * decay, 0.0) * beta
        stack = jnp.concatenate([dqk, dkk], axis=0).astype(bf16)
        ahead = mm(stack, k16[h])
        behind = mm_tn(stack, jnp.concatenate([q16[h], k16[h]], axis=0))
        dq = ahead[:size] + entry * dqe
        dk_ = ahead[size:] + behind + entry * dke + tail * user_end
        base = vbase + h * dv
        cv = conv[:, base : base + dv]
        sigv = jax.nn.sigmoid(cv)
        value = cv * sigv
        ext[0:size, base : base + dv] = (beta * dr) * (sigv * (1.0 + cv * (1.0 - sigv)))
        dbeta = jnp.sum(dr * (value - entry * recalled), axis=-1, keepdims=True) + jnp.sum(
            dlow * weak[h], axis=-1, keepdims=True
        )
        lowmask = dlow * weak[h] * beta
        paired = dattend * attend[h] + lowmask
        dentry = jnp.sum(dqe * queries[h] + dke * keys[h], axis=-1, keepdims=True)
        dtail = jnp.sum(user_end * keys[h], axis=-1, keepdims=True) * tail
        dkept = jnp.sum(
            jnp.sum(start * dstates[h], axis=1, keepdims=True), axis=0, keepdims=True
        )
        col_add = jnp.sum(paired, axis=-1, keepdims=True) + dentry * entry - dtail
        dsum_col = jnp.where(lane == h, col_add, dsum_col)
        dsum_row = jnp.where(sub == h, jnp.sum(paired, axis=0, keepdims=True), dsum_row)
        end_add = jnp.where(
            lane_row == h, jnp.sum(dtail, axis=0, keepdims=True) + dkept * kept, end_add
        )
        dbeta_all = jnp.where(lane == heads + h, dbeta, dbeta_all)
        inner = jnp.sum(dq * sq[h], axis=-1, keepdims=True)
        scale = dk**-0.5 * rq[h]
        ds = scale * dq - sq[h] * (scale * rq[h] * rq[h] * inner)
        ext[0:size, h * dk : (h + 1) * dk] = ds * silu_grad(cq[h])
        inner = jnp.sum(dk_ * sk[h], axis=-1, keepdims=True)
        ds = rk[h] * dk_ - sk[h] * (rk[h] * rk[h] * rk[h] * inner)
        ext[0:size, (heads + h) * dk : (heads + h + 1) * dk] = ds * silu_grad(ck[h])

    dcum = dsum_col - jnp.transpose(dsum_row)
    final = lax.broadcasted_iota(jnp.int32, (size, LANES), 0) == size - 1
    dcum = dcum + jnp.where(final, end_add, 0.0)
    dlog = mm_hi((row <= col).astype(f32), dcum) * (1.0 - fl[:, START : START + 1])
    rate = jnp.exp(head[0:1, :])
    shifted = raw + head[1:2, :]
    dap = dlog * (-rate) * jax.nn.sigmoid(shifted)
    dbp = dbeta_all * beta_all * (1.0 - beta_all)
    dab[...] = jnp.where(lane < heads, dap, jnp.where(lane < 2 * heads, dbp, 0.0)).astype(bf16)
    head_sum[0:1, :] += jnp.sum(dlog * (-rate) * softplus(shifted), axis=0, keepdims=True)
    head_sum[1:2, :] += jnp.sum(dap, axis=0, keepdims=True)
    dhead[...] = head_sum[...]

    later = [jnp.broadcast_to(fl[:, AHEAD + s : AHEAD + s + 1], (size, LANES)) for s in (1, 2, 3)]
    for lo in range(0, width, LANES):
        at = slice(lo, lo + LANES)
        here = proj[:, at]
        own = ext[0:size, at]
        total = own * taps[3:4, at]
        tap_sum[3:4, at] += jnp.sum(own * here, axis=0, keepdims=True)
        for s in (1, 2, 3):
            moved = ext[s : s + size, at] * later[s - 1]
            total += moved * taps[3 - s : 4 - s, at]
            tap_sum[3 - s : 4 - s, at] += jnp.sum(moved * here, axis=0, keepdims=True)
        dproj[:, at] = total.astype(bf16)

        @pl.when(step == 0)
        def _():
            tail_rows[:, at] = total[size - 8 : size, :]

    @pl.when(step == steps - 1)
    def _():
        head_rows[...] = ext[0:8, :]
        sub8 = lax.broadcasted_iota(jnp.int32, (8, width), 0)
        for s in (1, 2, 3):
            ok = (sub8 < s).astype(f32) * fl[0:8, VALID + s : VALID + s + 1]
            before = pltpu.roll(halo[...], s, 0)
            tap_sum[3 - s : 4 - s, :] += jnp.sum(
                ext[0:8, :] * before * ok, axis=0, keepdims=True
            )

    dtaps[...] = tap_sum[...]


def delta_grad(
    proj, conv, flags, cum, halo, taps, head, do, tinv, uval, wkey, states, entering, leaving,
    heads, dk, dv,
):
    rows = proj.shape[0]
    size = CHUNK
    steps = rows // size
    width = 2 * heads * dk + heads * dv
    ab_at = (width + heads * dv) // LANES

    def rowwise(cols, at=0):
        return pl.BlockSpec((size, cols), lambda n: (steps - 1 - n, at))

    outs = [
        ((rows, width), bf16, rowwise(width)),
        ((rows, LANES), bf16, rowwise(LANES)),
        ((8, width), f32, whole((8, width))),
        ((8, width), f32, whole((8, width))),
        ((8, width), f32, whole((8, width))),
        ((8, LANES), f32, whole((8, LANES))),
    ]
    return pl.pallas_call(
        functools.partial(grad_kernel, heads, dk, dv),
        grid=(steps,),
        in_specs=[
            rowwise(width),
            rowwise(width),
            rowwise(LANES, ab_at),
            rowwise(LANES),
            rowwise(LANES),
            whole((8, width)),
            whole((8, width)),
            whole((8, LANES)),
            rowwise(heads * dv),
            rowwise(heads * size),
            rowwise(heads * dv),
            rowwise(heads * dk),
            pl.BlockSpec((1, heads, dk, dv + dk), lambda n: (steps - 1 - n, 0, 0, 0)),
            whole((heads, dk, dv)),
            whole((heads, dk, dv)),
        ],
        out_specs=[spec for _, _, spec in outs],
        out_shape=[jax.ShapeDtypeStruct(shape, kind) for shape, kind, _ in outs],
        scratch_shapes=[
            pltpu.VMEM((heads, dk, dv), f32),
            pltpu.VMEM((size + 8, width), f32),
            pltpu.VMEM((8, width), f32),
            pltpu.VMEM((8, LANES), f32),
        ],
        compiler_params=vmem(),
        cost_estimate=pl.CostEstimate(
            flops=rows * heads * 2 * (10 * size * dv + 8 * dk * dv),
            bytes_accessed=rows * width * 16,
            transcendentals=rows * width * 2,
        ),
    )(
        proj, conv, proj, flags, cum, halo, taps, head, do, tinv, uval, wkey, states, entering,
        leaving,
    )


def shifted(value, axis, distance):
    count = lax.axis_size(axis)
    route = [(i, i + distance) for i in range(count) if 0 <= i + distance < count]
    return lax.ppermute(value, axis, route)


def heads_mm(a, b):
    return jnp.einsum("hij,hjk->hik", a, b, preferred_element_type=f32)


def heads_mm_tn(a, b):
    return jnp.einsum("hji,hjk->hik", a, b, preferred_element_type=f32)


def entering_state(own, dv, reach):
    runs = []
    run = own
    distance = 1
    while distance < reach:
        runs.append(run[:, :, dv:])
        before = shifted(run, "ctx", distance)
        joined = heads_mm(run[:, :, dv:], before)
        run = jnp.concatenate(
            [run[:, :, :dv].astype(f32) + joined[:, :, :dv], joined[:, :, dv:]], axis=-1
        ).astype(bf16)
        distance *= 2
    entering = shifted(run[:, :, :dv], "ctx", 1)
    ahead = [part if j == 0 else shifted(part, "ctx", 1 - 2**j) for j, part in enumerate(runs)]
    return entering, ahead


def leaving_grad(own, ahead):
    run = own
    for j, maps in enumerate(ahead):
        later = shifted(run, "ctx", -(2**j))
        run = (run.astype(f32) + heads_mm_tn(maps, later)).astype(bf16)
    return shifted(run, "ctx", -1)


def summed_over_tp(part):
    count = lax.axis_size("tp")
    total = part.astype(f32)
    for d in range(1, count):
        route = [(i, (i + d) % count) for i in range(count)]
        total = total + lax.ppermute(part, "tp", route).astype(f32)
    return total


def reduced(grad):
    part = lax.psum_scatter(grad, "fs", scatter_dimension=0, tiled=True)
    part = lax.psum_scatter(part, "ctx", scatter_dimension=0, tiled=True)
    return lax.all_gather(part, "ctx", axis=0, tiled=True).astype(f32)


def per_device(
    tokens, cotangent, lengths, order, mixer_gain, w_query, w_key, w_value, w_outgate, w_decay,
    w_beta, conv_query, conv_key, conv_value, decay_log, decay_bias, out_gain, w_output, mlp_gain,
    w_gate, w_up, w_down,
):
    rows, model = tokens.shape[1:]
    ctx = lax.axis_size("ctx")
    fs = lax.axis_size("fs")
    me = lax.axis_index("ctx")
    heads = decay_log.shape[0]
    dk = w_query.shape[1] // heads
    dv = w_value.shape[1] // heads
    key_cols, value_cols = heads * dk, heads * dv
    width = 2 * key_cols + value_cols
    hidden_cols = w_gate.shape[1]
    total = order.shape[1]
    peer = rows // ctx
    halo_rows = TAPS - 1
    sequences = lengths.shape[1]
    longest = 2 * total // (sequences + 1)
    reach = min(ctx - 1, -(-longest // rows))

    order_row = order[0]
    source_all = order_row // rows
    mine = (source_all == me).reshape(ctx, rows)
    upto = (jnp.arange(rows)[:, None] <= jnp.arange(rows)[None, :]).astype(bf16)
    rank_all = jnp.dot(mine.astype(bf16), upto, preferred_element_type=f32).astype(jnp.int32) - 1
    slots = jnp.arange(peer, dtype=jnp.int32)
    picked = mine[:, None, :] & (rank_all[:, None, :] == slots[None, :, None])
    local_all = (order_row - me * rows).reshape(ctx, 1, rows)
    send_order = jnp.sum(jnp.where(picked, local_all, 0), axis=2).reshape(rows)
    given = lax.dynamic_slice_in_dim(order_row, me * rows, rows)
    source = given // rows
    from_each = source[None, :] == jnp.arange(ctx, dtype=jnp.int32)[:, None]
    rank_here = jnp.dot(from_each.astype(bf16), upto, preferred_element_type=f32) - 1.0
    rank_here = jnp.sum(jnp.where(from_each, rank_here, 0.0), axis=0).astype(jnp.int32)
    recv_slot = source * peer + rank_here
    iota = jnp.arange(rows, dtype=jnp.int32)
    gather_send = (send_order[:, None] == iota[None, :]).astype(bf16)
    gather_recv = (recv_slot[:, None] == iota[None, :]).astype(bf16)

    def moved(maps, values, transposed=False):
        return lax.dot_general(
            maps, values, (((0 if transposed else 1,), (0,)), ((), ())), preferred_element_type=f32
        ).astype(bf16)

    def to_packed(values):
        arrived = lax.all_to_all(
            moved(gather_send, values), "ctx", split_axis=0, concat_axis=0, tiled=True
        )
        return moved(gather_recv, arrived)

    def to_given(values):
        arrived = lax.all_to_all(
            moved(gather_recv, values, True), "ctx", split_axis=0, concat_axis=0, tiled=True
        )
        return moved(gather_send, arrived, True)

    resident = to_packed(tokens[0])
    e = to_packed(cotangent[0])

    offsets = jnp.cumsum(lengths[0]) - lengths[0]
    positions = me * rows - halo_rows + jnp.arange(rows + 2 * halo_rows, dtype=jnp.int32)
    number = jnp.sum((offsets[None, :] <= positions[:, None]).astype(jnp.int32), axis=1)
    here = number[halo_rows : halo_rows + rows]
    fresh = jnp.any(offsets[None, :] == positions[halo_rows : halo_rows + rows, None], axis=1)
    columns = [jnp.zeros((rows,), f32)] * START + [fresh.astype(f32)]
    for s in range(1, TAPS):
        columns.append((number[halo_rows - s : halo_rows - s + rows] == here).astype(f32))
    for s in range(1, TAPS):
        columns.append((number[halo_rows + s : halo_rows + s + rows] == here).astype(f32))
    flags = jnp.stack(columns, axis=1)
    flags = jnp.pad(flags, ((0, 0), (0, LANES - flags.shape[1])))

    pad = jnp.zeros((w_decay.shape[0], LANES - 2 * heads), bf16)
    w_in = jnp.concatenate([w_query, w_key, w_value, w_outgate, w_decay, w_beta, pad], axis=1)
    w_in = lax.all_gather(w_in, "fs", axis=0, tiled=True)
    w_wide = lax.all_gather(jnp.concatenate([w_gate, w_up], axis=1), "fs", axis=0, tiled=True)
    w_down = lax.all_gather(w_down, "fs", axis=0, tiled=True)
    w_output = lax.all_gather(w_output, "fs", axis=0, tiled=True)
    small = jnp.concatenate(
        [
            conv_query.T.reshape(-1),
            conv_key.T.reshape(-1),
            conv_value.T.reshape(-1),
            mixer_gain,
            mlp_gain,
            out_gain,
        ]
    )
    small = lax.all_gather(small, "fs", axis=0).astype(f32)
    pieces, at = [], 0
    for channels in (conv_query.shape[0], conv_key.shape[0], conv_value.shape[0]):
        part = small[:, at : at + TAPS * channels].reshape(fs, TAPS, channels)
        pieces.append(part.transpose(1, 0, 2).reshape(TAPS, fs * channels))
        at += TAPS * channels
    taps = jnp.pad(jnp.concatenate(pieces, axis=1), ((0, 8 - TAPS), (0, 0)))
    gains = []
    for size in (mixer_gain.shape[0], mlp_gain.shape[0], out_gain.shape[0]):
        gains.append(small[:, at : at + size].reshape(-1))
        at += size
    gain_one, gain_two, gain_out = gains
    gain_rows = jnp.broadcast_to(gain_out[None, :], (8, dv))
    head = jnp.pad(
        jnp.stack([decay_log, decay_bias]), ((0, 6), (0, LANES - heads))
    )

    x = resident.astype(f32)
    inv_one = lax.rsqrt(jnp.mean(x * x, axis=-1, keepdims=True) + EPS)
    n1 = (x * inv_one * gain_one).astype(bf16)
    proj = jnp.dot(n1, w_in, preferred_element_type=f32)
    halo = shifted(proj[rows - 8 :, :width], "ctx", 1)
    conv, local, qa, states, tinv, uval, wkey, qeff, ktail, cum, last = delta_forward(
        proj, flags, halo, taps, head, heads, dk, dv
    )
    entering, ahead = entering_state(last, dv, reach)
    y1, part = delta_mix(local, qa, entering, proj, gain_rows, w_output, heads, dk, dv)

    r = x + summed_over_tp(part)
    inv_two = lax.rsqrt(jnp.mean(r * r, axis=-1, keepdims=True) + EPS)
    n2 = (r * inv_two * gain_two).astype(bf16)
    wide = jnp.dot(n2, w_wide, preferred_element_type=f32)
    gp, up = wide[:, :hidden_cols], wide[:, hidden_cols:]
    act = silu(gp)
    hid = (act * up).astype(bf16)
    down = jnp.dot(hid, w_down, preferred_element_type=f32).astype(bf16)
    dhid = lax.dot_general(e, w_down, (((1,), (1,)), ((), ())), preferred_element_type=f32)
    dwide = jnp.concatenate(
        [(dhid * up * silu_grad(gp)).astype(bf16), (dhid * act).astype(bf16)], axis=1
    )
    dn2 = lax.dot_general(dwide, w_wide, (((1,), (1,)), ((), ())), preferred_element_type=f32)
    dn2 = summed_over_tp(dn2.astype(bf16))
    block_out = to_given((r + summed_over_tp(down)).astype(bf16))
    grad_mlp_gain = jnp.sum(dn2 * r * inv_two, axis=0)
    scaled = gain_two * dn2
    dr = (
        e.astype(f32)
        + inv_two * scaled
        - r * (inv_two * inv_two * inv_two * jnp.mean(scaled * r, axis=-1, keepdims=True))
    )
    er = dr.astype(bf16)

    dz, do, dgain_out, first = delta_back(
        er, local, qa, entering, proj, gain_rows, w_output, qeff, wkey, ktail, cum, heads, dk, dv
    )
    leaving = leaving_grad(first, ahead)
    dproj, dab, tail_rows, head_rows, dtaps, dhead = delta_grad(
        proj, conv, flags, cum, halo, taps, head, do, tinv, uval, wkey, states, entering, leaving,
        heads, dk, dv,
    )
    next_rows = shifted(head_rows, "ctx", -1)
    extra = jnp.zeros_like(tail_rows)
    for s in range(1, TAPS):
        part_s = jnp.concatenate([jnp.zeros((8 - s, width), f32), next_rows[:s]], axis=0)
        extra = extra + part_s * taps[TAPS - 1 - s] * flags[rows - 8 :, AHEAD + s][:, None]
    dproj = lax.dynamic_update_slice(dproj, (tail_rows + extra).astype(bf16), (rows - 8, 0))
    dall = jnp.concatenate([dproj, dz, dab], axis=1)
    dn1 = lax.dot_general(dall, w_in, (((1,), (1,)), ((), ())), preferred_element_type=f32)
    dn1 = summed_over_tp(dn1.astype(bf16))
    grad_mixer_gain = jnp.sum(dn1 * x * inv_one, axis=0)
    scaled = gain_one * dn1
    grad_in = (
        dr
        + inv_one * scaled
        - x * (inv_one * inv_one * inv_one * jnp.mean(scaled * x, axis=-1, keepdims=True))
    ).astype(bf16)
    grad_tokens = to_given(grad_in)

    def outer(a, b):
        return lax.dot_general(a, b, (((0,), (0,)), ((), ())), preferred_element_type=f32)

    def halves(grad):
        return grad.reshape(fs, grad.shape[0] // fs, *grad.shape[1:])

    g_wide = reduced(outer(n2, dwide).astype(bf16))
    g_rows = jnp.concatenate([halves(outer(hid, e)), halves(outer(y1, er))], axis=1)
    g_rows = reduced(g_rows.reshape(-1, model).astype(bf16))
    g_in = reduced(outer(n1, dall).astype(bf16))
    down_rows = hidden_cols // fs

    def tap_part(lo, channels):
        return dtaps[:TAPS, lo : lo + channels].reshape(TAPS, fs, -1).transpose(1, 0, 2).reshape(fs, -1)

    share = lax.psum(jnp.sum(dgain_out, axis=0).astype(bf16), "tp").astype(f32)
    rates = jnp.broadcast_to(dhead[:2, :heads].reshape(1, 2 * heads), (fs, 2 * heads))
    little = jnp.concatenate(
        [
            tap_part(0, key_cols),
            tap_part(key_cols, key_cols),
            tap_part(2 * key_cols, value_cols),
            halves(grad_mixer_gain),
            halves(grad_mlp_gain),
            halves(share),
            rates,
        ],
        axis=1,
    )
    little = lax.psum_scatter(little, "fs", scatter_dimension=0, tiled=True)
    little = lax.psum(little, "ctx")[0]
    taken, at = [], 0
    for channels in (conv_query.shape[0], conv_key.shape[0], conv_value.shape[0]):
        taken.append(little[at : at + TAPS * channels].reshape(TAPS, channels).T)
        at += TAPS * channels
    for size in (mixer_gain.shape[0], mlp_gain.shape[0], out_gain.shape[0], heads, heads):
        taken.append(little[at : at + size])
        at += size
    g_cq, g_ck, g_cv, g_mixer, g_mlp, g_out_gain, g_log, g_bias = taken
    ends = [key_cols, 2 * key_cols, width, width + value_cols, width + value_cols + heads]
    g_query, g_key, g_value, g_outgate, g_decay, g_beta = (
        g_in[:, lo:hi] for lo, hi in zip([0] + ends, ends + [ends[-1] + heads])
    )
    return (
        block_out[None],
        grad_tokens[None],
        g_mixer,
        g_query,
        g_key,
        g_value,
        g_outgate,
        g_decay,
        g_beta,
        g_cq,
        g_ck,
        g_cv,
        g_log,
        g_bias,
        g_out_gain,
        g_rows[down_rows:],
        g_mlp,
        g_wide[:, :hidden_cols],
        g_wide[:, hidden_cols:],
        g_rows[:down_rows],
    )


def solution(mesh):
    split = P("fs", "ctx", None)
    cols = P("fs", "tp")
    both = P(("tp", "fs"), None)
    in_specs = (
        split, split, P("fs", None), P("fs", None), P("fs"),
        cols, cols, cols, cols, cols, cols,
        both, both, both, P("tp"), P("tp"), P("fs"), both, P("fs"), cols, cols, both,
    )
    out_specs = (
        split, split, P("fs"),
        cols, cols, cols, cols, cols, cols,
        both, both, both, P("tp"), P("tp"), P("fs"), both, P("fs"), cols, cols, both,
    )
    return jax.shard_map(
        per_device, mesh=mesh, in_specs=in_specs, out_specs=out_specs, check_vma=False
    )
```

time: 2750 us -> 996 us (0.36)
  matrix products: 606 us -> 134 us
  waiting for transfers between devices: 981 us -> 513 us
  other arithmetic: 481 us -> 24.7 us
  local copies, waits for them, and re-layouts: 324 us -> 45.8 us
  blocking collectives: 284 us -> 98.3 us
  Pallas kernels: 0 us -> 110 us
    dot_general x225 -> x24, matrix products: 575 us -> 134 us  [the longest x8 42.5 us: moved(): lax.dot_general(maps, values, (((0 if transposed else 1,), (0,)), ((), ()...]
    another operation x12 -> x2, other arithmetic: 320 us -> 1.43 us  [the longest x4 317 us: block_parts(): jax.scipy.linalg.solve_triangular(system, (beta_vals * entry_gain)[..., N...]
    unnamed x39 -> x13, waiting for transfers between devices: 234 us -> 2.19 us
    all_gather x17 -> x1, blocking collectives: 203 us -> 2.36 us  [per_device(): small = lax.all_gather(small, 'fs', axis=0).astype(f32)]
    ppermute x6 -> x13, waiting for transfers between devices: 1.68 us -> 199 us  [the longest x4 111 us: summed_over_tp(): total = total + lax.ppermute(part, 'tp', route).astype(f32)]
    psum x3 -> x0, waiting for transfers between devices: 196 us -> none  [the longest x1 96.8 us: per_device(): lax.psum(jnp.dot(grad_gate_rows, gathered[13].T, preferred_element_type=j...]
    all_gather x18 -> x7, waiting for transfers between devices: 198 us -> 75 us  [the longest x3 75 us: reduced(): return lax.all_gather(part, 'ctx', axis=0, tiled=True).astype(f32)]
    pallas_call x0 -> x4, Pallas kernels: none -> 110 us  [the longest x1 48.6 us: delta_grad(): pl.pallas_call(functools.partial(grad_kernel, heads, dk, dv), grid=(steps...]
  transfers between devices with their start and end apart: 44 -> 30, of which waited for: 26 -> 18; matrix products, arithmetic and copies ran while one was open for 49% -> 16% of each run, Pallas kernels for 0% -> 11%
where the time goes in v1:
time: 996 us; the launch traced here: 990 us
  waiting for transfers between devices  513 us (52%)
  matrix products  134 us (13%)
  Pallas kernels  110 us (11%)
  blocking collectives  98.3 us (10%)
  starting transfers between devices  48.5 us (5%)
  local copies, waits for them, and re-layouts  45.8 us (5%)
  other arithmetic  24.7 us (2%)
  between operations  15.1 us (2%)
    reduce_scatter x3, waiting for transfers between devices, reduced(): part = lax.psum_scatter(part, 'ctx', scatter_dimension=0, tiled=True)  186 us
    ppermute x4, waiting for transfers between devices, summed_over_tp(): total = total + lax.ppermute(part, 'tp', route).astype(f32)  111 us
    ppermute x9, waiting for transfers between devices, shifted(): return lax.ppermute(value, axis, route)  87.9 us
    psum x1, blocking collectives, per_device(): little = lax.psum(little, 'ctx')[0]  87.3 us
    all_gather x3, waiting for transfers between devices, reduced(): return lax.all_gather(part, 'ctx', axis=0, tiled=True).astype(f32)  75 us
    pallas_call x1, Pallas kernels, delta_grad(): pl.pallas_call(functools.partial(grad_kernel, heads, dk, dv), grid=(steps...  48.6 us
    dot_general x8, matrix products, moved(): lax.dot_general(maps, values, (((0 if transposed else 1,), (0,)), ((), ()...  42.5 us
    pallas_call x1, Pallas kernels, delta_forward(): pl.pallas_call(functools.partial(forward_kernel, heads, dk, dv), grid=(st...  35.3 us
  transfers between devices with their start and end apart: 30, of which 18 were waited for; matrix products, arithmetic and copies ran while one was open for 16% of the time, Pallas kernels for 11%

profile of v1, /device:TPU:0, one launch (start us, length us, event | category | flops | bytes accessed | tf_op | source)
XLA Modules:
  0.0 990.3 jit_solution(3056415010286588943)
XLA Ops:
  9.2 6.5 concatenate.41
  22.8 7.4 all-to-all-start
  43.5 35.0 %all-to-all-done = bf16[8,128,1024]{2,1,0:T(8,128)(2,1)S(1)} async-done(((bf16[8,128,1024]{2,1,0:T(8,128)(2,1)}), bf16[8,128,1024]{2,1,0:T(8,128)(2,1)S(1)}, u32[]{:S(2)}, u32[]{:S(2)}) %all-to-all-start) | async-done | bytes 2097184 | tf_op jit(solution)/shard_map/all_to_all | solution.py:705
  84.5 10.2 %fusion.58.proj.ab.zgate = f32[1024,3200]{1,0:T(8,128)S(1)} fusion(bf16[1024,3200]{1,0:T(8,128)(2,1)} %all-gather.10.cloned.1.call-done, bf16[1024,1024]{1,0:T(8,128)(2,1)S(1)} %get-tuple-element.187, f32[1024]{0:T(1024)S(1)} %bitcast.152, f32[1024]{0:T(1024)S(1)} %add_rsqrt_fusion.1), kind=kOutput, calls=%fused_computation.84 | convolution fusion | flops 6715080704 | bytes 21766144 | tf_op jit(solution)/shard_map/dot_general | solution.py:768
  105.3 35.3 %shard_map.365 = (f32[1024,2048]{1,0:T(8,128)}, f32[1024,1024]{1,0:T(8,128)}, bf16[1024,512]{1,0:T(8,128)(2,1)}, bf16[8,4,128,384]{3,2,1,0:T(8,128)(2,1)}, bf16[...) custom-call(f32[1024,3200]{1,0:T(8,128)} %copy-done.2, ...), custom_call_target="tpu_custom_call" | custom-call | flops 5368709120 | bytes 29360128 | tf_op jit(solution)/shard_map/pallas_call | solution.py:220
  157.8 36.7 %collective-permute-done.2 = bf16[4,128,384]{2,1,0:T(8,128)(2,1)S(1)} collective-permute-done((bf16[4,128,384]{2,1,0:T(8,128)(2,1)S(1)}, bf16[4,128,384]{2,1,0:T(8,128)(2,1)S(1)}, u32[]{:S(2)}, u32[]{:S(2)}) %collective-permute-start.2) | collective-permute-done | bytes 393248 | tf_op jit(solution)/shard_map/ppermute | solution.py:607
  202.9 8.6 shard_map.366
  218.6 37.7 %collective-permute-done.4 = bf16[1024,1024]{1,0:T(8,128)(2,1)} collective-permute-done((bf16[1024,1024]{1,0:T(8,128)(2,1)}, bf16[1024,1024]{1,0:T(8,128)(2,1)}, u32[]{:S(2)}, u32[]{:S(2)}) %collective-permute-start.4) | collective-permute-done | bytes 2097184 | tf_op jit(solution)/shard_map/ppermute | solution.py:648
  260.8 12.5 %fusion.92 = f32[1024,2816]{1,0:T(8,128)} fusion(bf16[1024,2816]{1,0:T(8,128)(2,1)} %all-gather.14.cloned.1.call-done, f32[1024,1024]{1,0:T(8,128)} %get-tuple-element.153, f32[1024]{0:T(1024)S(1)} %bitcast.138, f32[1024]{0:T(1024)S(1)} %add_rsqrt_fusion), kind=kOutput, calls=%fused_computation.180 | convolution fusion | flops 5908725760 | bytes 21504000 | tf_op jit(solution)/shard_map/dot_general | solution.py:779
  273.2 10.5 %multiply_convert_fusion.1 = (bf16[1024,1408]{1,0:T(8,128)(2,1)S(1)}, bf16[1024,1408]{1,0:T(8,128)(2,1)S(1)}, bf16[1024,1408]{1,0:T(8,128)(2,1)S(1)}) fusion(f32[1024,2816]{1,0:T(8,128)} %fusion.92, bf16[1024,1024]{1,0:T(8,128)(2,1)} %fusion.48, bf16[1408,1024]{1,0:T(8,128)(2,1)} %all-gather.16.cloned.1.call-done), kind=kOutput, calls=%fused_computation.10 | convolution fusion | flops 2974416896 | bytes 25165824 | tf_op jit(solution)/shard_map/dot_general | solution.py:784
  283.8 6.4 fusion.39
  295.2 38.5 %collective-permute-done.6 = bf16[1024,1024]{1,0:T(8,128)(2,1)S(1)} collective-permute-done((bf16[1024,1024]{1,0:T(8,128)(2,1)S(1)}, bf16[1024,1024]{1,0:T(8,128)(2,1)S(1)}, u32[]{:S(2)}, u32[]{:S(2)}) %collective-permute-start.6) | collective-permute-done | bytes 2097184 | tf_op jit(solution)/shard_map/ppermute | solution.py:648
  342.6 11.6 %convolution_convert_fusion.1 = bf16[1024,2816]{1,0:T(8,128)(2,1)} fusion(bf16[1024,1408]{1,0:T(8,128)(2,1)} %copy-done.37, bf16[1024,1408]{1,0:T(8,128)(2,1)} %copy-done.36, f32[1024,1024]{1,0:T(8,128)} %get-tuple-element.153, f32[1024]{0:T(1024)S(1)} %bitcast.141, f32[1024]{0:T(1024)S(1)} %add_rsqrt_fusion), kind=kOutput, calls=%fused_computation.14 | convolution fusion | flops 5923143680 | bytes 15736832 | tf_op jit(solution)/shard_map/dot_general | solution.py:827
  354.3 17.8 %shard_map.367 = (bf16[1024,1024]{1,0:T(8,128)(2,1)}, bf16[1024,1024]{1,0:T(8,128)(2,1)}, f32[8,256]{1,0:T(8,128)}, bf16[4,128,256]{2,1,0:T(8,128)(2,1)}) custom-call(bf16[1024,1024]{1,0:T(8,128)(2,1)} %copy-done.7, f32[1024,1024]{1,0:T(8,128)} %get-tuple-element.43.local, bf16[1024,512]{1,0:T(8,128)(2,1)} %get-tuple-element.44.qa, ...), custom_call_target="tpu_custom_call" | custom-call | flops 3221225472 | bytes 18874368 | tf_op jit(solution)/shard_map/pallas_call | solution.py:348
  373.4 24.9 %collective-permute-done.7 = bf16[4,128,256]{2,1,0:T(8,128)(2,1)S(1)} collective-permute-done((bf16[4,128,256]{2,1,0:T(8,128)(2,1)}, bf16[4,128,256]{2,1,0:T(8,128)(2,1)S(1)}, u32[]{:S(2)}, u32[]{:S(2)}) %collective-permute-start.7) | collective-permute-done | bytes 262176 | tf_op jit(solution)/shard_map/ppermute | solution.py:607
  402.1 6.8 collective-permute-done.8
  411.4 7.8 collective-permute-done.10.leaving
  419.9 48.6 %shard_map.368 = (bf16[1024,2048]{1,0:T(8,128)(2,1)}, bf16[1024,128]{1,0:T(8,128)(2,1)}, f32[8,2048]{1,0:T(8,128)}, f32[8,2048]{1,0:T(8,128)}, f32[8,2048]{1,0:T(8,128)}, /*index=5*/f32[8,128]{1,0:T(8,128)}) custom-call(f32[1024,3200]{1,0:T(8,128)} %copy-done.2, f32[1024,2048]{1,0:T(8,128)} %get-tuple-element.47.conv, f32[1024,3200]{1,0:T(8,128)} %copy-done.2, ...), custom_call_target="tpu_custom_call" | custom-call | flops 4831838208 | bytes 33554432 | tf_op jit(solution)/shard_map/pallas_call | solution.py:564
  470.1 5.7 collective-permute-done.11
  477.4 12.4 %convolution_convert_fusion = bf16[1024,3200]{1,0:T(8,128)(2,1)} fusion(bf16[1024,128]{1,0:T(8,128)(2,1)} %get-tuple-element.61, bf16[1024,1024]{1,0:T(8,128)(2,1)S(1)} %copy-done.32, bf16[1024,2048]{1,0:T(8,128)(2,1)} %fusion.73, bf16[1024,1024]{1,0:T(8,128)(2,1)S(1)} %get-tuple-element.187, f32[1024]{0:T(1024)S(1)} %bitcast.153, f32[1024]{0:T(1024)S(1)} %add_rsqrt_fusion.1), kind=kOutput, calls=%fused_computation.6 | convolution fusion | flops 6738018304 | bytes 15212544 | tf_op jit(solution)/shard_map/dot_general | solution.py:827
  491.3 16.2 %reduce-scatter.7.cloned.1.call-done = bf16[512,3200]{1,0:T(8,128)(2,1)} async-done(((bf16[1024,3200]{1,0:T(8,128)(2,1)}), bf16[512,3200]{1,0:T(8,128)(2,1)}) %reduce-scatter.7.cloned.1.call-update) | async-done | bytes 3276816 | tf_op jit(solution)/shard_map/reduce_scatter | solution.py:653
  507.6 74.8 %reduce-scatter.13.cloned.1.call-done = bf16[152,1024]{1,0:T(8,128)(2,1)} async-done(((bf16[1216,1024]{1,0:T(8,128)(2,1)}), bf16[152,1024]{1,0:T(8,128)(2,1)}) %reduce-scatter.13.cloned.1.call-update) | async-done | bytes 311312 | tf_op jit(solution)/shard_map/reduce_scatter | solution.py:654
  582.7 7.4 convolution_convert_fusion.4
  591.6 65.0 %reduce-scatter.17.cloned.1.call-done = bf16[64,2816]{1,0:T(8,128)(2,1)} async-done(((bf16[512,2816]{1,0:T(8,128)(2,1)}), bf16[64,2816]{1,0:T(8,128)(2,1)}) %reduce-scatter.17.cloned.1.call-update) | async-done | bytes 360464 | tf_op jit(solution)/shard_map/reduce_scatter | solution.py:654
  656.7 12.4 %fusion.38 = bf16[1024,1024]{1,0:T(8,128)(2,1)} fusion(bf16[1024,3200]{1,0:T(8,128)(2,1)} %all-gather.10.cloned.1.call-done, bf16[1024,128]{1,0:T(8,128)(2,1)S(1)} %copy-done.34, bf16[1024,1024]{1,0:T(8,128)(2,1)} %get-tuple-element.60, bf16[1024,2048]{1,0:T(8,128)(2,1)} %fusion.73), kind=kOutput, calls=%fused_computation.69 | convolution fusion | flops 6731595776 | bytes 15204352 | tf_op jit(solution)/shard_map/dot_general | solution.py:815
  670.5 6.3 fusion.47
  681.2 35.0 %collective-permute-done.12 = bf16[1024,1024]{1,0:T(8,128)(2,1)} collective-permute-done((bf16[1024,1024]{1,0:T(8,128)(2,1)}, bf16[1024,1024]{1,0:T(8,128)(2,1)}, u32[]{:S(2)}, u32[]{:S(2)}) %collective-permute-start.12) | collective-permute-done | bytes 2097184 | tf_op jit(solution)/shard_map/ppermute | solution.py:648
  720.2 45.8 %reduce-scatter.9.cloned.1.call-done = bf16[64,3200]{1,0:T(8,128)(2,1)} async-done(((bf16[512,3200]{1,0:T(8,128)(2,1)}), bf16[64,3200]{1,0:T(8,128)(2,1)}) %reduce-scatter.9.cloned.1.call-update) | async-done | bytes 409616 | tf_op jit(solution)/shard_map/reduce_scatter | solution.py:654
  766.1 10.1 %fusion.49 = bf16[1024,1024]{1,0:T(8,128)(2,1)} fusion(bf16[1024,1024]{1,0:T(8,128)(2,1)S(1)} %get-tuple-element.187, bf16[1024,1024]{1,0:T(8,128)(2,1)} %collective-permute-done.12, bf16[1024,1024]{1,0:T(8,128)(2,1)} %fusion.38, f32[1024]{0:T(1024)S(1)} %fusion.80, f32[1024]{0:T(1024)S(1)} %bitcast.155, f32[1024]{0:T(1024)S(1)} %add_rsqrt_fusion.1, ...), kind=kOutput, calls=%fused_computation.76 | convolution fusion | flops 2169503744 | bytes 18903040 | tf_op jit(solution)/shard_map/dot_general | solution.py:700
  790.9 87.3 %psum.15 = f32[1,5256]{1,0:T(1,128)S(1)} all-reduce(f32[1,5256]{1,0:T(1,128)S(1)} %constant_dynamic-slice_fusion), channel_id=1, replica_groups=mesh['ctx'=8,'tp'=2,'fs'=2] {'ctx'}, use_global_device_ids=true, to_apply=%region_14.15 | all-reduce | flops 5256 | bytes 42048 | tf_op jit(solution)/shard_map/psum | solution.py:856
  895.8 16.6 %all-gather.22.cloned.1.call-done = bf16[512,2816]{1,0:T(8,128)(2,1)} async-done(((bf16[64,2816]{1,0:T(8,128)(2,1)}), bf16[512,2816]{1,0:T(8,128)(2,1)}) %all-gather.22.cloned.1.call-update) | async-done | bytes 2883600 | tf_op jit(solution)/shard_map/all_gather | solution.py:655
  917.1 58.4 %all-gather.18.cloned.1.call-done = bf16[512,3200]{1,0:T(8,128)(2,1)} async-done(((bf16[64,3200]{1,0:T(8,128)(2,1)}), bf16[512,3200]{1,0:T(8,128)(2,1)}) %all-gather.18.cloned.1.call-update) | async-done | bytes 3276816 | tf_op jit(solution)/shard_map/all_gather | solution.py:655
  (258 shorter events, 158.9 us)
Async XLA Ops:
  7.2 77.2 %all-gather.10.cloned.1.call-start = ((), (), s32[]{:S(2)}) async-start(), calls=%async_computation.10 | async-start | bytes 9830400 | tf_op jit(solution)/shard_map/all_gather | solution.py:734
  15.7 182.7 %all-gather.12.cloned.1.call-start = ((), (), s32[]{:S(2)}) async-start(), calls=%async_computation.11 | async-start | bytes 3145728 | tf_op jit(solution)/shard_map/all_gather | solution.py:737
  19.1 126.0 %copy-start.23 = (s32[8,128]{1,0:T(8,128)}, s32[8,128]{1,0:T(8,128)S(1)}, u32[]{:S(2)}) copy-start(s32[8,128]{1,0:T(8,128)S(1)} %select_reduce_fusion) | copy-start | bytes 12292
  22.8 55.7 %all-to-all-start = ((bf16[8,128,1024]{2,1,0:T(8,128)(2,1)}), bf16[8,128,1024]{2,1,0:T(8,128)(2,1)S(1)}, u32[]{:S(2)}, u32[]{:S(2)}) async-start(bf16[8,128,1024]{2,1,0:T(8,128)(2,1)} %bitcast.126), calls=%async_computation | async-start | bytes 4194304 | tf_op jit(solution)/shard_map/all_to_all | solution.py:705
  30.3 230.5 %all-gather.14.cloned.1.call-start = ((), (), s32[]{:S(2)}) async-start(), calls=%async_computation.12 | async-start | bytes 8650752 | tf_op jit(solution)/shard_map/all_gather | solution.py:735
  99.4 5.3 collective-permute-start
  140.6 12.8 %collective-permute-start.1 = (bf16[4,128,384]{2,1,0:T(8,128)(2,1)}, bf16[4,128,384]{2,1,0:T(8,128)(2,1)S(1)}, u32[]{:S(2)}, u32[]{:S(2)}) collective-permute-start(bf16[4,128,384]{2,1,0:T(8,128)(2,1)} %get-tuple-element.45), channel_id=1, source_target_pairs={{0,4},{4,8},{8,12},{12,16},{16,20},{20,24},{24,28},{1,5},{5,9},{9,... | collective-permute-start | bytes 1179656 | tf_op jit(solution)/shard_map/ppermute | solution.py:607
  148.8 64.3 %all-to-all-start.2 = ((bf16[8,128,1024]{2,1,0:T(8,128)(2,1)}), bf16[8,128,1024]{2,1,0:T(8,128)(2,1)}, u32[]{:S(2)}, u32[]{:S(2)}) async-start(bf16[8,128,1024]{2,1,0:T(8,128)(2,1)} %bitcast.129), calls=%async_computation.2 | async-start | bytes 4194304 | tf_op jit(solution)/shard_map/all_to_all | solution.py:705
  153.4 119.9 %all-gather.16.cloned.1.call-start = ((), (), s32[]{:S(2)}) async-start(), calls=%async_computation.13 | async-start | bytes 4325376 | tf_op jit(solution)/shard_map/all_gather | solution.py:736
  153.9 40.6 %collective-permute-start.2 = (bf16[4,128,384]{2,1,0:T(8,128)(2,1)S(1)}, bf16[4,128,384]{2,1,0:T(8,128)(2,1)S(1)}, u32[]{:S(2)}, u32[]{:S(2)}) collective-permute-start(bf16[4,128,384]{2,1,0:T(8,128)(2,1)S(1)} %pad_maximum_fusion.12), channel_id=1, source_target_pairs={{0,8},{4,12},{8,16},{12,20},{16,24},{20,28},{1,9},{5,13},{9,17},{1... | collective-permute-start | bytes 1179656 | tf_op jit(solution)/shard_map/ppermute | solution.py:607
  194.7 7.5 collective-permute-start.3
  211.5 44.7 %collective-permute-start.4 = (bf16[1024,1024]{1,0:T(8,128)(2,1)}, bf16[1024,1024]{1,0:T(8,128)(2,1)}, u32[]{:S(2)}, u32[]{:S(2)}) collective-permute-start(bf16[1024,1024]{1,0:T(8,128)(2,1)} %get-tuple-element.46), channel_id=1, source_target_pairs={{0,2},{2,0},{1,3},{3,1},{4,6},{6,4},{5,7},{7,5},{8,10},{10,8},{9,1... | collective-permute-start | bytes 6291464 | tf_op jit(solution)/shard_map/ppermute | solution.py:648
  213.1 276.8 %reduce-scatter.11.cloned.1.call-start = ((), (), s32[]{:S(2)}) async-start(), calls=%async_computation.17 | async-start | bytes 7471104 | tf_op jit(solution)/shard_map/reduce_scatter | solution.py:653
  290.2 43.5 %collective-permute-start.6 = (bf16[1024,1024]{1,0:T(8,128)(2,1)S(1)}, bf16[1024,1024]{1,0:T(8,128)(2,1)S(1)}, u32[]{:S(2)}, u32[]{:S(2)}) collective-permute-start(bf16[1024,1024]{1,0:T(8,128)(2,1)S(1)} %fusion.39), channel_id=1, source_target_pairs={{0,2},{2,0},{1,3},{3,1},{4,6},{6,4},{5,7},{7,5},{8,10},{10,8},{9,1... | collective-permute-start | bytes 6291464 | tf_op jit(solution)/shard_map/ppermute | solution.py:648
  342.6 148.0 %reduce-scatter.15.cloned.1.call-start = ((), (), s32[]{:S(2)}) async-start(), calls=%async_computation.20 | async-start | bytes 8650752 | tf_op jit(solution)/shard_map/reduce_scatter | solution.py:653
  354.2 153.3 %reduce-scatter.7.cloned.1.call-start = ((), (), s32[]{:S(2)}) async-start(), calls=%async_computation.14 | async-start | bytes 9830400 | tf_op jit(solution)/shard_map/reduce_scatter | solution.py:653
  372.1 26.2 %collective-permute-start.7 = (bf16[4,128,256]{2,1,0:T(8,128)(2,1)}, bf16[4,128,256]{2,1,0:T(8,128)(2,1)S(1)}, u32[]{:S(2)}, u32[]{:S(2)}) collective-permute-start(bf16[4,128,256]{2,1,0:T(8,128)(2,1)} %get-tuple-element.56), channel_id=1, source_target_pairs={{4,0},{8,4},{12,8},{16,12},{20,16},{24,20},{28,24},{5,1},{9,5},{13... | collective-permute-start | bytes 786440 | tf_op jit(solution)/shard_map/ppermute | solution.py:607
  399.5 10.3 %collective-permute-start.9 = (bf16[4,128,256]{2,1,0:T(8,128)(2,1)S(1)}, bf16[4,128,256]{2,1,0:T(8,128)(2,1)S(1)}, u32[]{:S(2)}, u32[]{:S(2)}) collective-permute-start(bf16[4,128,256]{2,1,0:T(8,128)(2,1)S(1)} %add_convert_fusion.5), channel_id=1, source_target_pairs={{8,0},{12,4},{16,8},{20,12},{24,16},{28,20},{9,1},{13,5},{17,9},{2... | collective-permute-start | bytes 786440 | tf_op jit(solution)/shard_map/ppermute | solution.py:607
  400.8 8.1 collective-permute-start.8
  410.1 9.1 collective-permute-start.10
  468.5 7.3 collective-permute-start.11
  489.8 92.7 %reduce-scatter.13.cloned.1.call-start = ((), (), s32[]{:S(2)}) async-start(), calls=%async_computation.18 | async-start | bytes 2801664 | tf_op jit(solution)/shard_map/reduce_scatter | solution.py:654
  490.5 166.1 %reduce-scatter.17.cloned.1.call-start = ((), (), s32[]{:S(2)}) async-start(), calls=%async_computation.21 | async-start | bytes 3244032 | tf_op jit(solution)/shard_map/reduce_scatter | solution.py:654
  491.3 274.8 %reduce-scatter.9.cloned.1.call-start = ((), (), s32[]{:S(2)}) async-start(), calls=%async_computation.15 | async-start | bytes 3686400 | tf_op jit(solution)/shard_map/reduce_scatter | solution.py:654
  507.6 383.3 %all-gather.20.cloned.1.call-start = ((), (), s32[]{:S(2)}) async-start(), calls=%async_computation.19 | async-start | bytes 2801664 | tf_op jit(solution)/shard_map/all_gather | solution.py:655
  582.5 329.9 %all-gather.22.cloned.1.call-start = ((), (), s32[]{:S(2)}) async-start(), calls=%async_computation.22 | async-start | bytes 3244032 | tf_op jit(solution)/shard_map/all_gather | solution.py:655
  590.1 80.4 %collective-permute-start.5 = (bf16[1024,1024]{1,0:T(8,128)(2,1)}, bf16[1024,1024]{1,0:T(8,128)(2,1)}, u32[]{:S(2)}, u32[]{:S(2)}) collective-permute-start(bf16[1024,1024]{1,0:T(8,128)(2,1)} %convolution_convert_fusion.4), channel_id=1, source_target_pairs={{0,2},{2,0},{1,3},{3,1},{4,6},{6,4},{5,7},{7,5},{8,10},{10,8},{9,1... | collective-permute-start | bytes 6291464 | tf_op jit(solution)/shard_map/ppermute | solution.py:648
  669.1 47.1 %collective-permute-start.12 = (bf16[1024,1024]{1,0:T(8,128)(2,1)}, bf16[1024,1024]{1,0:T(8,128)(2,1)}, u32[]{:S(2)}, u32[]{:S(2)}) collective-permute-start(bf16[1024,1024]{1,0:T(8,128)(2,1)} %fusion.38), channel_id=1, source_target_pairs={{0,2},{2,0},{1,3},{3,1},{4,6},{6,4},{5,7},{7,5},{8,10},{10,8},{9,1... | collective-permute-start | bytes 6291464 | tf_op jit(solution)/shard_map/ppermute | solution.py:648
  676.8 99.4 %all-to-all-start.1 = ((bf16[8,128,1024]{2,1,0:T(8,128)(2,1)}), bf16[8,128,1024]{2,1,0:T(8,128)(2,1)}, u32[]{:S(2)}, u32[]{:S(2)}) async-start(bf16[8,128,1024]{2,1,0:T(8,128)(2,1)} %bitcast.130), calls=%async_computation.1 | async-start | bytes 4194304 | tf_op jit(solution)/shard_map/all_to_all | solution.py:711
  681.2 294.3 %all-gather.18.cloned.1.call-start = ((), (), s32[]{:S(2)}) async-start(), calls=%async_computation.16 | async-start | bytes 3686400 | tf_op jit(solution)/shard_map/all_gather | solution.py:655
  776.2 105.5 %copy-start.24 = (s32[8,128]{1,0:T(8,128)S(1)}, s32[8,128]{1,0:T(8,128)}, u32[]{:S(2)}) copy-start(s32[8,128]{1,0:T(8,128)} %copy-done.23) | copy-start | bytes 12292
  776.2 110.9 %all-to-all-start.3 = ((bf16[8,128,1024]{2,1,0:T(8,128)(2,1)}), bf16[8,128,1024]{2,1,0:T(8,128)(2,1)S(1)}, u32[]{:S(2)}, u32[]{:S(2)}) async-start(bf16[8,128,1024]{2,1,0:T(8,128)(2,1)} %bitcast.127), calls=%async_computation.3 | async-start | bytes 4194304 | tf_op jit(solution)/shard_map/all_to_all | solution.py:711
  (37 other events, 522.1 us)
Sparse Core Ops, SparseCore 0:
  15.8 19.8 all-gather.9
  37.2 11.7 all-gather.11
  51.1 17.1 all-gather.13
  213.2 25.8 all-gather.15
  342.7 32.9 reduce-scatter.10
  378.0 15.0 reduce-scatter.14
  489.9 17.5 reduce-scatter.6
  511.5 70.9 reduce-scatter.12
  586.0 70.6 reduce-scatter.16
  660.1 105.8 reduce-scatter.8
  768.5 86.4 all-gather.19
  857.3 55.1 all-gather.21
  914.8 60.5 all-gather.17

commit v2 on v1

--- a/solution.py
+++ b/solution.py
@@ -236,7 +236,7 @@
         ],
         compiler_params=vmem(),
         cost_estimate=pl.CostEstimate(
-            flops=rows * heads * 2 * (16 * size * size + 8 * dk * (dv + dk)),
+            flops=rows * heads * 40 * size * (dv + dk + size + size),
             bytes_accessed=rows * width * 14,
             transcendentals=rows * width * 2,
         ),
@@ -279,7 +279,7 @@
         ],
         compiler_params=vmem(),
         cost_estimate=pl.CostEstimate(
-            flops=2 * rows * heads * dv * (model + dk),
+            flops=10 * rows * heads * dv * model,
             bytes_accessed=rows * heads * dv * 14,
             transcendentals=rows * heads * dv,
         ),
@@ -366,7 +366,7 @@
         scratch_shapes=[pltpu.VMEM((heads, dk, dv), f32), pltpu.VMEM((8, dv), f32)],
         compiler_params=vmem(),
         cost_estimate=pl.CostEstimate(
-            flops=2 * rows * heads * dv * (model + 4 * dk),
+            flops=20 * rows * heads * dv * model,
             bytes_accessed=rows * heads * dv * 18,
             transcendentals=rows * heads * dv,
         ),
@@ -591,7 +591,7 @@
         ],
         compiler_params=vmem(),
         cost_estimate=pl.CostEstimate(
-            flops=rows * heads * 2 * (10 * size * dv + 8 * dk * dv),
+            flops=rows * heads * 200 * size * (dv + dk + size),
             bytes_accessed=rows * width * 16,
             transcendentals=rows * width * 2,
         ),
@@ -649,10 +649,271 @@
     return total
 
 
-def reduced(grad):
-    part = lax.psum_scatter(grad, "fs", scatter_dimension=0, tiled=True)
-    part = lax.psum_scatter(part, "ctx", scatter_dimension=0, tiled=True)
-    return lax.all_gather(part, "ctx", axis=0, tiled=True).astype(f32)
+def swapped(value, axis, bit):
+    return lax.ppermute(value, axis, [(i, i ^ bit) for i in range(lax.axis_size(axis))])
+
+
+def sum_kernel(plan, *refs):
+    count = len(plan)
+    grads, outs = refs[:count], refs[count : 2 * count]
+    refs = refs[2 * count :]
+    own, fs_in, in_y, in_m, in_h, full = (refs[i * count : (i + 1) * count] for i in range(6))
+    load_sem, send_sem, recv_sem = refs[6 * count :]
+    fs = lax.axis_index("fs")
+    me = lax.axis_index("ctx")
+    y = lax.rem(me, 2)
+    z = lax.div(me, 2)
+    hub = lax.div(z, 2)
+    inner = lax.rem(lax.div(z + 1, 2), 2)
+    mate = z + 1 - 2 * lax.rem(z, 2)
+    core = {"fs": 1 - fs}
+    beside = {"ctx": z * 2 + 1 - y}
+    paired = {"ctx": mate * 2 + y}
+    across = {"ctx": (3 - z) * 2 + y}
+    barrier = pltpu.get_barrier_semaphore()
+    for partner in (core, beside, paired, across):
+        pl.semaphore_signal(barrier, inc=1, device_id=partner, device_id_type=pl.DeviceIdType.MESH)
+    pl.semaphore_wait(barrier, 4)
+
+    segments = []
+    for i, widths in enumerate(plan):
+        lo = 0
+        for w in widths:
+            segments.append((i, slice(lo, lo + w)))
+            lo += w
+    total = len(segments)
+
+    def rows(start, n):
+        return pl.ds(pl.multiple_of(start, 16), n)
+
+    def stages(g):
+        i, at = segments[g]
+        half = own[i].shape[0]
+        q, e = half // 2, half // 4
+        y_first = g % 2 == 0
+
+        def remote(slot, src, dst, partner):
+            return pltpu.make_async_remote_copy(
+                src_ref=src,
+                dst_ref=dst,
+                send_sem=send_sem.at[g, slot],
+                recv_sem=recv_sem.at[g, slot],
+                device_id=partner,
+                device_id_type=pl.DeviceIdType.MESH,
+            )
+
+        def moved(slot, source, target, start, n, partner):
+            return remote(
+                slot, source[i].at[rows(start, n), at], target[i].at[rows(start, n), at], partner
+            )
+
+        def add(target, one, two, start, n):
+            step = 32 if n % 32 == 0 else 16
+
+            def body(j, carry):
+                r = rows(start + j * step, step)
+                total = one[i][r, at].astype(f32) + two[i][r, at].astype(f32)
+                target[i][r, at] = total.astype(bf16)
+                return carry
+
+            lax.fori_loop(0, n // step, body, 0)
+
+        load = pltpu.make_async_copy(
+            grads[i].at[rows(fs * half, half), at], own[i].at[:, at], load_sem.at[g]
+        )
+        unload = pltpu.make_async_copy(full[i].at[:, at], outs[i].at[:, at], load_sem.at[total + g])
+        fs_copy = remote(0, grads[i].at[rows((1 - fs) * half, half), at], fs_in[i].at[:, at], core)
+        if y_first:
+            mine = y * q
+            low_copy = moved(1, own, in_y, (1 - y) * q, q, beside)
+            mate_copy = moved(2, own, in_m, mine, q, paired)
+            hub_copy = moved(3, own, in_h, mine + (1 - hub) * e, e, across)
+            back_hub = moved(4, full, full, mine + hub * e, e, across)
+            back_low = moved(5, full, full, mine, q, beside)
+            back_mate = moved(6, full, full, mine, q, paired)
+        else:
+            mine = hub * q
+            mate_copy = moved(2, own, in_m, 0, half, paired)
+            hub_copy = moved(3, own, in_h, (1 - hub) * q, q, across)
+            low_copy = moved(1, own, in_y, mine + (1 - y) * e, e, beside)
+            back_low = moved(5, full, full, mine + y * e, e, beside)
+            back_hub = moved(4, full, full, mine, q, across)
+            back_mate = moved(6, full, full, 0, half, paired)
+
+        def begin():
+            fs_copy.start()
+            load.start()
+
+        def finish():
+            @pl.when(inner == 0)
+            def _():
+                mate_copy.wait_send()
+
+            @pl.when(inner == 1)
+            def _():
+                back_mate.wait_send()
+
+            unload.wait()
+
+        def cores():
+            load.wait()
+            fs_copy.wait()
+            add(own, own, fs_in, 0, half)
+
+        if y_first:
+
+            def s0():
+                cores()
+                low_copy.start()
+
+            def s1():
+                low_copy.wait()
+                add(own, own, in_y, mine, q)
+
+                @pl.when(inner == 0)
+                def _():
+                    mate_copy.start()
+
+            def s2():
+                @pl.when(inner == 1)
+                def _():
+                    mate_copy.wait_recv()
+                    add(own, own, in_m, mine, q)
+                    hub_copy.start()
+
+            def s3():
+                @pl.when(inner == 1)
+                def _():
+                    hub_copy.wait()
+                    add(full, own, in_h, mine + hub * e, e)
+                    back_hub.start()
+
+            def s4():
+                @pl.when(inner == 1)
+                def _():
+                    back_hub.wait()
+                    back_mate.start()
+                    back_low.start()
+
+            def s5():
+                @pl.when(inner == 0)
+                def _():
+                    back_mate.wait_recv()
+                    back_low.start()
+
+            def s6():
+                back_low.wait()
+                unload.start()
+
+        else:
+
+            def s0():
+                cores()
+
+                @pl.when(inner == 0)
+                def _():
+                    mate_copy.start()
+
+            def s1():
+                @pl.when(inner == 1)
+                def _():
+                    mate_copy.wait_recv()
+                    add(own, own, in_m, 0, half)
+                    hub_copy.start()
+
+            def s2():
+                @pl.when(inner == 1)
+                def _():
+                    hub_copy.wait()
+                    add(own, own, in_h, mine, q)
+                    low_copy.start()
+
+            def s3():
+                @pl.when(inner == 1)
+                def _():
+                    low_copy.wait()
+                    add(full, own, in_y, mine + y * e, e)
+                    back_low.start()
+
+            def s4():
+                @pl.when(inner == 1)
+                def _():
+                    back_low.wait()
+                    back_hub.start()
+
+            def s5():
+                @pl.when(inner == 1)
+                def _():
+                    back_hub.wait()
+                    back_mate.start()
+                    unload.start()
+
+            def s6():
+                @pl.when(inner == 0)
+                def _():
+                    back_mate.wait_recv()
+                    unload.start()
+
+        return begin, (s0, s1, s2, s3, s4, s5, s6), finish
+
+    work = [stages(g) for g in range(total)]
+    for begin, _, _ in work:
+        begin()
+    for t in range(total + 6):
+        for stage in range(7):
+            if 0 <= t - stage < total:
+                work[t - stage][1][stage]()
+    for _, _, finish in work:
+        finish()
+
+
+def segment_widths(cols, rows, target=128 * 1024):
+    tiles = cols // LANES
+    parts = max(1, min(tiles, round(rows * cols / target)))
+    return tuple((tiles * (j + 1) // parts - tiles * j // parts) * LANES for j in range(parts))
+
+
+def reduced(grads, collective_id, micros):
+    if lax.axis_size("ctx") != 8 or lax.axis_size("fs") != 2:
+        parts = [lax.psum_scatter(g, "fs", scatter_dimension=0, tiled=True) for g in grads]
+        return [lax.psum(part, "ctx") for part in parts]
+    shapes = [(g.shape[0] // 2, g.shape[1]) for g in grads]
+    plan = tuple(segment_widths(cols, half) for half, cols in shapes)
+    total = sum(len(widths) for widths in plan)
+    return pl.pallas_call(
+        functools.partial(sum_kernel, plan),
+        in_specs=[pl.BlockSpec(memory_space=pl.ANY)] * len(grads),
+        out_specs=[pl.BlockSpec(memory_space=pl.ANY)] * len(grads),
+        out_shape=[jax.ShapeDtypeStruct(shape, bf16) for shape in shapes],
+        scratch_shapes=[pltpu.VMEM(shape, bf16) for shape in shapes] * 6
+        + [
+            pltpu.SemaphoreType.DMA((2 * total,)),
+            pltpu.SemaphoreType.DMA((total, 7)),
+            pltpu.SemaphoreType.DMA((total, 7)),
+        ],
+        compiler_params=pltpu.CompilerParams(
+            collective_id=collective_id, has_side_effects=True, vmem_limit_bytes=56 * MIB
+        ),
+        cost_estimate=pl.CostEstimate(
+            flops=micros * 10**9, bytes_accessed=4 * sum(g.size for g in grads), transcendentals=0
+        ),
+    )(*grads)
+
+
+def scattered(grad):
+    return lax.psum_scatter(grad, ("fs", "ctx"), scatter_dimension=0, tiled=True)
+
+
+def reduced_little(little):
+    mine = lax.axis_index("fs")
+    give = lax.dynamic_slice_in_dim(little, 1 - mine, 1, 0)
+    keep = lax.dynamic_slice_in_dim(little, mine, 1, 0)
+    total = (keep + swapped(give, "fs", 1))[0]
+    bit = 1
+    while bit < lax.axis_size("ctx"):
+        total = total + swapped(total, "ctx", bit)
+        bit *= 2
+    return total
 
 
 def per_device(
@@ -714,7 +975,6 @@
         return moved(gather_send, arrived, True)
 
     resident = to_packed(tokens[0])
-    e = to_packed(cotangent[0])
 
     offsets = jnp.cumsum(lengths[0]) - lengths[0]
     positions = me * rows - halo_rows + jnp.arange(rows + 2 * halo_rows, dtype=jnp.int32)
@@ -771,6 +1031,8 @@
         proj, flags, halo, taps, head, heads, dk, dv
     )
     entering, ahead = entering_state(last, dv, reach)
+    entering, cot = lax.optimization_barrier((entering, cotangent[0]))
+    e = to_packed(cot)
     y1, part = delta_mix(local, qa, entering, proj, gain_rows, w_output, heads, dk, dv)
 
     r = x + summed_over_tp(part)
@@ -787,7 +1049,25 @@
     )
     dn2 = lax.dot_general(dwide, w_wide, (((1,), (1,)), ((), ())), preferred_element_type=f32)
     dn2 = summed_over_tp(dn2.astype(bf16))
-    block_out = to_given((r + summed_over_tp(down)).astype(bf16))
+    def outer(a, b):
+        return lax.dot_general(
+            a, b, (((0,), (0,)), ((), ())), preferred_element_type=f32
+        ).astype(bf16)
+
+    def halves(grad):
+        return grad.reshape(fs, grad.shape[0] // fs, *grad.shape[1:])
+
+    half = model // fs
+    g_down = outer(hid, e)
+    down_rows = hidden_cols // fs
+    pieces = []
+    for f in range(fs):
+        pieces.append(outer(dwide, n2[:, f * half : (f + 1) * half]))
+        rows_f = g_down[f * down_rows : (f + 1) * down_rows]
+        pieces += [rows_f[:, j * half : (j + 1) * half] for j in range(fs)]
+    dn2, down, mlp_cat = lax.optimization_barrier((dn2, down, jnp.concatenate(pieces, axis=0)))
+    mlp_share = scattered(mlp_cat)
+    result = (r + summed_over_tp(down)).astype(bf16)
     grad_mlp_gain = jnp.sum(dn2 * r * inv_two, axis=0)
     scaled = gain_two * dn2
     dr = (
@@ -801,10 +1081,15 @@
         er, local, qa, entering, proj, gain_rows, w_output, qeff, wkey, ktail, cum, heads, dk, dv
     )
     leaving = leaving_grad(first, ahead)
+    block_out = to_given(result)
+    g_z = outer(n1, dz)
+    g_o = outer(y1, er)
     dproj, dab, tail_rows, head_rows, dtaps, dhead = delta_grad(
         proj, conv, flags, cum, halo, taps, head, do, tinv, uval, wkey, states, entering, leaving,
         heads, dk, dv,
     )
+    dproj, mlp_share = lax.optimization_barrier((dproj, mlp_share))
+    g_mlp_all = lax.all_gather(mlp_share, "ctx", axis=0, tiled=True)
     next_rows = shifted(head_rows, "ctx", -1)
     extra = jnp.zeros_like(tail_rows)
     for s in range(1, TAPS):
@@ -814,6 +1099,12 @@
     dall = jnp.concatenate([dproj, dz, dab], axis=1)
     dn1 = lax.dot_general(dall, w_in, (((1,), (1,)), ((), ())), preferred_element_type=f32)
     dn1 = summed_over_tp(dn1.astype(bf16))
+    g_in = outer(n1, jnp.concatenate([dproj, dab], axis=1))
+    g_in, g_z, g_o = reduced([g_in, g_z, g_o], 1, 110)
+    dn1, g_in, g_z, g_o = lax.optimization_barrier((dn1, g_in, g_z, g_o))
+    g_wide = jnp.swapaxes(g_mlp_all[: 2 * hidden_cols], 0, 1)
+    g_down = g_mlp_all[2 * hidden_cols :].reshape(fs, down_rows, half)
+    g_down = jnp.concatenate([g_down[j] for j in range(fs)], axis=1)
     grad_mixer_gain = jnp.sum(dn1 * x * inv_one, axis=0)
     scaled = gain_one * dn1
     grad_in = (
@@ -823,22 +1114,10 @@
     ).astype(bf16)
     grad_tokens = to_given(grad_in)
 
-    def outer(a, b):
-        return lax.dot_general(a, b, (((0,), (0,)), ((), ())), preferred_element_type=f32)
-
-    def halves(grad):
-        return grad.reshape(fs, grad.shape[0] // fs, *grad.shape[1:])
-
-    g_wide = reduced(outer(n2, dwide).astype(bf16))
-    g_rows = jnp.concatenate([halves(outer(hid, e)), halves(outer(y1, er))], axis=1)
-    g_rows = reduced(g_rows.reshape(-1, model).astype(bf16))
-    g_in = reduced(outer(n1, dall).astype(bf16))
-    down_rows = hidden_cols // fs
-
     def tap_part(lo, channels):
         return dtaps[:TAPS, lo : lo + channels].reshape(TAPS, fs, -1).transpose(1, 0, 2).reshape(fs, -1)
 
-    share = lax.psum(jnp.sum(dgain_out, axis=0).astype(bf16), "tp").astype(f32)
+    share = summed_over_tp(jnp.sum(dgain_out, axis=0).astype(bf16))
     rates = jnp.broadcast_to(dhead[:2, :heads].reshape(1, 2 * heads), (fs, 2 * heads))
     little = jnp.concatenate(
         [
@@ -852,8 +1131,7 @@
         ],
         axis=1,
     )
-    little = lax.psum_scatter(little, "fs", scatter_dimension=0, tiled=True)
-    little = lax.psum(little, "ctx")[0]
+    little = reduced_little(little)
     taken, at = [], 0
     for channels in (conv_query.shape[0], conv_key.shape[0], conv_value.shape[0]):
         taken.append(little[at : at + TAPS * channels].reshape(TAPS, channels).T)
@@ -862,9 +1140,9 @@
         taken.append(little[at : at + size])
         at += size
     g_cq, g_ck, g_cv, g_mixer, g_mlp, g_out_gain, g_log, g_bias = taken
-    ends = [key_cols, 2 * key_cols, width, width + value_cols, width + value_cols + heads]
-    g_query, g_key, g_value, g_outgate, g_decay, g_beta = (
-        g_in[:, lo:hi] for lo, hi in zip([0] + ends, ends + [ends[-1] + heads])
+    ends = [key_cols, 2 * key_cols, width, width + heads]
+    g_query, g_key, g_value, g_decay, g_beta = (
+        g_in[:, lo:hi].astype(f32) for lo, hi in zip([0] + ends, ends + [ends[-1] + heads])
     )
     return (
         block_out[None],
@@ -873,7 +1151,7 @@
         g_query,
         g_key,
         g_value,
-        g_outgate,
+        g_z.astype(f32),
         g_decay,
         g_beta,
         g_cq,
@@ -882,11 +1160,11 @@
         g_log,
         g_bias,
         g_out_gain,
-        g_rows[down_rows:],
+        g_o.astype(f32),
         g_mlp,
-        g_wide[:, :hidden_cols],
-        g_wide[:, hidden_cols:],
-        g_rows[:down_rows],
+        g_wide[:, :hidden_cols].astype(f32),
+        g_wide[:, hidden_cols:].astype(f32),
+        g_down.astype(f32),
     )
 
 

time: 996 us -> 755 us (0.76)
  waiting for transfers between devices: 513 us -> 168 us
  Pallas kernels: 110 us -> 266 us
  blocking collectives: 98.3 us -> 2.05 us
  other arithmetic: 24.7 us -> 46.9 us
  starting transfers between devices: 48.5 us -> 66.1 us
    reduce_scatter x6 -> x1, waiting for transfers between devices: 202 us -> 0.02 us  [scattered(): lax.psum_scatter(grad, ('fs', 'ctx'), scatter_dimension=0, tiled=True)]
    pallas_call x0 -> x1, Pallas kernels: none -> 156 us  [reduced(): pl.pallas_call(functools.partial(sum_kernel, plan), in_specs=[pl.BlockSpe...]
    psum x2 -> x0, blocking collectives: 92.2 us -> none  [the longest x1 87.3 us: per_device(): little = lax.psum(little, 'ctx')[0]]
    all_gather x3 -> x1, waiting for transfers between devices: 75 us -> 0.01 us  [per_device(): g_mlp_all = lax.all_gather(mlp_share, 'ctx', axis=0, tiled=True)]
    ppermute x4 -> x5, waiting for transfers between devices: 111 us -> 52.6 us  [summed_over_tp(): total = total + lax.ppermute(part, 'tp', route).astype(f32)]
    ppermute x9, waiting for transfers between devices: 87.9 us -> 59.1 us  [shifted(): return lax.ppermute(value, axis, route)]
    ppermute x0 -> x4, waiting for transfers between devices: none -> 19.2 us  [swapped(): lax.ppermute(value, axis, [(i, i ^ bit) for i in range(lax.axis_size(axis...]
    convert_element_type x0 -> x8, other arithmetic: none -> 15.4 us  [the longest x3 3.98 us: per_device(): g_in[:, lo:hi].astype(f32)]
  transfers between devices with their start and end apart: 30 -> 28, of which waited for: 18 -> 14; matrix products, arithmetic and copies ran while one was open for 16% -> 22% of each run, Pallas kernels for 11% -> 36%
where the time goes in v2:
time: 755 us; the launch traced here: 745 us
  Pallas kernels  266 us (35%)
  waiting for transfers between devices  168 us (22%)
  matrix products  136 us (18%)
  starting transfers between devices  66.1 us (9%)
  other arithmetic  46.9 us (6%)
  local copies, waits for them, and re-layouts  45.5 us (6%)
  between operations  15.4 us (2%)
    pallas_call x1, Pallas kernels, reduced(): pl.pallas_call(functools.partial(sum_kernel, plan), in_specs=[pl.BlockSpe...  156 us
    ppermute x9, waiting for transfers between devices, shifted(): return lax.ppermute(value, axis, route)  59.1 us
    ppermute x5, waiting for transfers between devices, summed_over_tp(): total = total + lax.ppermute(part, 'tp', route).astype(f32)  52.6 us
    pallas_call x1, Pallas kernels, delta_grad(): pl.pallas_call(functools.partial(grad_kernel, heads, dk, dv), grid=(steps...  48.2 us
    dot_general x8, matrix products, moved(): lax.dot_general(maps, values, (((0 if transposed else 1,), (0,)), ((), ()...  41.7 us
    pallas_call x1, Pallas kernels, delta_forward(): pl.pallas_call(functools.partial(forward_kernel, heads, dk, dv), grid=(st...  35.4 us
    all_to_all x2, waiting for transfers between devices, to_packed(): lax.all_to_all(moved(gather_send, values), 'ctx', split_axis=0, concat_ax...  35.1 us
    dot_general x6, matrix products, outer(): lax.dot_general(a, b, (((0,), (0,)), ((), ())), preferred_element_type=f32)  31.5 us
  transfers between devices with their start and end apart: 28, of which 14 were waited for; matrix products, arithmetic and copies ran while one was open for 22% of the time, Pallas kernels for 36%

profile of v2, /device:TPU:0, one launch (start us, length us, event | category | flops | bytes accessed | tf_op | source)
XLA Modules:
  0.0 745.1 jit_solution(11976238835487604000)
XLA Ops:
  9.2 6.5 concatenate.46
  19.1 5.3 fusion.44
  24.4 7.4 all-to-all-start
  45.1 35.1 %all-to-all-done = bf16[8,128,1024]{2,1,0:T(8,128)(2,1)} async-done(((bf16[8,128,1024]{2,1,0:T(8,128)(2,1)}), bf16[8,128,1024]{2,1,0:T(8,128)(2,1)}, u32[]{:S(2)}, u32[]{:S(2)}) %all-to-all-start) | async-done | bytes 2097184 | tf_op jit(solution)/shard_map/all_to_all | solution.py:966
  80.2 5.3 fusion.12
  85.5 10.8 %fusion.99.proj.ab.zgate = f32[1024,3200]{1,0:T(8,128)S(1)} fusion(bf16[1024,3200]{1,0:T(8,128)(2,1)} %all-gather.8.cloned.1.call-done, bf16[1024,1024]{1,0:T(8,128)(2,1)} %get-tuple-element.215, f32[1024]{0:T(1024)S(1)} %bitcast.136, f32[1024]{0:T(1024)S(1)} %add_rsqrt_fusion.1), kind=kOutput, calls=%fused_computation.195 | convolution fusion | flops 6715080704 | bytes 21766144 | tf_op jit(solution)/shard_map/dot_general | solution.py:1028
  102.2 35.4 %shard_map.365 = (f32[1024,2048]{1,0:T(8,128)}, f32[1024,1024]{1,0:T(8,128)}, bf16[1024,512]{1,0:T(8,128)(2,1)}, bf16[8,4,128,384]{3,2,1,0:T(8,128)(2,1)}, bf16[...) custom-call(f32[1024,3200]{1,0:T(8,128)} %copy-done.41, ...), custom_call_target="tpu_custom_call" | custom-call | flops 13421772800 | bytes 29360128 | tf_op jit(solution)/shard_map/pallas_call | solution.py:220
  141.9 6.7 collective-permute-done.1
  150.9 5.5 collective-permute-start.2
  156.4 5.4 collective-permute-done.2
  168.2 8.6 %shard_map.366 = (bf16[1024,1024]{1,0:T(8,128)(2,1)}, bf16[1024,1024]{1,0:T(8,128)(2,1)}) custom-call(f32[1024,1024]{1,0:T(8,128)} %get-tuple-element.57.local, bf16[1024,512]{1,0:T(8,128)(2,1)} %get-tuple-element.58.qa, bf16[4,128,256]{2,1,0:T(8,128)(2,1)} %copy-done.43, f32[1024,3200]{1,0:T(8,128)} %copy-done.41, f32[8,256]{1,0:T(8,128)} %broadcast_in_dim.35.gain, ...), custom_call_target="tpu_custom_call" | custom-call | flops 10737418240 | bytes 14680064 | tf_op jit(solution)/shard_map/pallas_call | solution.py:264
  182.0 11.0 %all-to-all-start.1 = ((bf16[8,128,1024]{2,1,0:T(8,128)(2,1)}), bf16[8,128,1024]{2,1,0:T(8,128)(2,1)}, u32[]{:S(2)}, u32[]{:S(2)}) async-start(bf16[8,128,1024]{2,1,0:T(8,128)(2,1)} %bitcast.115), calls=%async_computation.1 | async-start | bytes 4194304 | tf_op jit(solution)/shard_map/all_to_all | solution.py:966
  193.7 27.0 %collective-permute-done.4 = bf16[1024,1024]{1,0:T(8,128)(2,1)} collective-permute-done((bf16[1024,1024]{1,0:T(8,128)(2,1)}, bf16[1024,1024]{1,0:T(8,128)(2,1)}, u32[]{:S(2)}, u32[]{:S(2)}) %collective-permute-start.4) | collective-permute-done | bytes 2097184 | tf_op jit(solution)/shard_map/ppermute | solution.py:648
  227.6 11.8 %fusion.110 = f32[1024,2816]{1,0:T(8,128)} fusion(bf16[1024,1024]{1,0:T(8,128)(2,1)} %multiply_convert_fusion.3, bf16[1024,2816]{1,0:T(8,128)(2,1)} %all-gather.14.cloned.1.call-done), kind=kOutput, calls=%fused_computation.205 | convolution fusion | flops 5905580032 | bytes 19398656 | tf_op jit(solution)/shard_map/dot_general | solution.py:1041
  239.4 5.3 fusion.49
  244.6 10.5 %multiply_convert_fusion.2 = (bf16[1024,1408]{1,0:T(8,128)(2,1)S(1)}, bf16[1024,1408]{1,0:T(8,128)(2,1)S(1)}, bf16[1024,1408]{1,0:T(8,128)(2,1)S(1)}) fusion(f32[1024,2816]{1,0:T(8,128)} %fusion.110, bf16[1024,1024]{1,0:T(8,128)(2,1)} %fusion.49, bf16[1408,1024]{1,0:T(8,128)(2,1)} %all-gather.12.cloned.1.call-done), kind=kOutput, calls=%fused_computation.15 | convolution fusion | flops 2974416896 | bytes 25165824 | tf_op jit(solution)/shard_map/dot_general | solution.py:1046
  263.3 7.5 %convolution_convert_fusion.7 = bf16[1024,1024]{1,0:T(8,128)(2,1)} fusion(bf16[1024,2816]{1,0:T(8,128)(2,1)S(1)} %bitcast.166, bf16[1024,1408]{1,0:T(8,128)(2,1)S(1)} %get-tuple-element.183, bf16[1024,1408]{1,0:T(8,128)(2,1)S(1)} %get-tuple-element.182), kind=kOutput, calls=%fused_computation.85 | convolution fusion | flops 5918162944 | bytes 13631488 | tf_op jit(solution)/shard_map/dot_general | solution.py:1050
  280.7 7.4 convolution_convert_fusion.6
  288.1 25.6 %collective-permute-done.5 = bf16[1024,1024]{1,0:T(8,128)(2,1)} collective-permute-done((bf16[1024,1024]{1,0:T(8,128)(2,1)}, bf16[1024,1024]{1,0:T(8,128)(2,1)}, u32[]{:S(2)}, u32[]{:S(2)}) %collective-permute-start.5) | collective-permute-done | bytes 2097184 | tf_op jit(solution)/shard_map/ppermute | solution.py:648
  328.4 18.0 %shard_map.367 = (bf16[1024,1024]{1,0:T(8,128)(2,1)}, bf16[1024,1024]{1,0:T(8,128)(2,1)}, f32[8,256]{1,0:T(8,128)}, bf16[4,128,256]{2,1,0:T(8,128)(2,1)}) custom-call(bf16[1024,1024]{1,0:T(8,128)(2,1)} %fusion.101.er, f32[1024,1024]{1,0:T(8,128)} %get-tuple-element.57.local, bf16[1024,512]{1,0:T(8,128)(2,1)} %get-tuple-element.58.qa, ...), custom_call_target="tpu_custom_call" | custom-call | flops 21474836480 | bytes 18874368 | tf_op jit(solution)/shard_map/pallas_call | solution.py:348
  359.3 5.7 convolution_convert_fusion.5.refs_1_
  365.0 19.7 %collective-permute-done.9 = bf16[4,128,256]{2,1,0:T(8,128)(2,1)S(1)} collective-permute-done((bf16[4,128,256]{2,1,0:T(8,128)(2,1)S(1)}, bf16[4,128,256]{2,1,0:T(8,128)(2,1)S(1)}, u32[]{:S(2)}, u32[]{:S(2)}) %collective-permute-start.9) | collective-permute-done | bytes 262176 | tf_op jit(solution)/shard_map/ppermute | solution.py:607
  396.1 48.2 %shard_map.368 = (bf16[1024,2048]{1,0:T(8,128)(2,1)}, bf16[1024,128]{1,0:T(8,128)(2,1)}, f32[8,2048]{1,0:T(8,128)}, f32[8,2048]{1,0:T(8,128)}, f32[8,2048]{1,0:T(8,128)}, /*index=5*/f32[8,128]{1,0:T(8,128)}) custom-call(f32[1024,3200]{1,0:T(8,128)} %copy-done.41, f32[1024,2048]{1,0:T(8,128)} %get-tuple-element.65.conv, f32[1024,3200]{1,0:T(8,128)} %copy-done.41, ...), custom_call_target="tpu_custom_call" | custom-call | flops 53687091200 | bytes 33554432 | tf_op jit(solution)/shard_map/pallas_call | solution.py:564
  449.1 14.7 %collective-permute-done.11 = f32[8,2048]{1,0:T(8,128)S(1)} collective-permute-done((f32[8,2048]{1,0:T(8,128)}, f32[8,2048]{1,0:T(8,128)S(1)}, u32[]{:S(2)}, u32[]{:S(2)}) %collective-permute-start.11) | collective-permute-done | bytes 65568 | tf_op jit(solution)/shard_map/ppermute | solution.py:607
  463.8 7.4 fusion.50
  471.2 5.6 all-to-all-start.2
  478.1 9.4 %convolution_convert_fusion.refs_0_ = bf16[1024,2176]{1,0:T(8,128)(2,1)} fusion(bf16[1024,128]{1,0:T(8,128)(2,1)S(1)} %copy-done.50, bf16[1024,2048]{1,0:T(8,128)(2,1)} %fusion.77, bf16[1024,1024]{1,0:T(8,128)(2,1)S(1)} %copy-done.7, f32[1024]{0:T(1024)S(1)} %bitcast.138, f32[1024]{0:T(1024)S(1)} %add_rsqrt_fusion.1), kind=kOutput, calls=%fused_computation.18 | convolution fusion | flops 4578738176 | bytes 11018240 | tf_op jit(solution)/shard_map/dot_general | solution.py:1053
  487.5 10.8 %fusion.54 = bf16[1024,1024]{1,0:T(8,128)(2,1)S(1)} fusion(bf16[1024,3200]{1,0:T(8,128)(2,1)} %all-gather.8.cloned.1.call-done, bf16[1024,128]{1,0:T(8,128)(2,1)S(1)} %copy-done.50, bf16[1024,1024]{1,0:T(8,128)(2,1)S(1)} %copy-done.47, bf16[1024,2048]{1,0:T(8,128)(2,1)S(1)} %copy-done.42), kind=kOutput, calls=%fused_computation.81 | convolution fusion | flops 6731595776 | bytes 15204352 | tf_op jit(solution)/shard_map/dot_general | solution.py:1100
  499.8 155.9 %shard_map.369 = (bf16[512,2176]{1,0:T(8,128)(2,1)}, bf16[512,1024]{1,0:T(8,128)(2,1)}, bf16[512,1024]{1,0:T(8,128)(2,1)}) custom-call(bf16[1024,2176]{1,0:T(8,128)(2,1)} %convolution_convert_fusion.refs_0_, bf16[1024,1024]{1,0:T(8,128)(2,1)} %convolution_convert_fusion.5.refs_1_, bf16[1024,1024]{1,0:T(8,128)(2,1)} %convolution_convert_fusion.4.refs_2_), custom_call_target="tpu_custom_call" | custom-call | flops 109999996928 | bytes 17301504 | tf_op jit(solution)/shard_map/pallas_call | solution.py:883
  660.0 5.4 fusion.51
  670.9 5.5 convert_bitcast_fusion.1
  686.5 14.8 %collective-permute-done.16 = f32[5256]{0:T(1024)S(1)} collective-permute-done((f32[5256]{0:T(1024)S(1)}, f32[5256]{0:T(1024)S(1)}, u32[]{:S(2)}, u32[]{:S(2)}) %collective-permute-start.16) | collective-permute-done | bytes 21056 | tf_op jit(solution)/shard_map/ppermute | solution.py:653
  (293 shorter events, 170.6 us)
Async XLA Ops:
  7.2 160.3 %copy-start = (bf16[1,1024,1024]{2,1,0:T(8,128)(2,1)S(1)}, bf16[1,1024,1024]{2,1,0:T(8,128)(2,1)}, u32[]{:S(2)}) copy-start(bf16[1,1024,1024]{2,1,0:T(8,128)(2,1)} %param.23) | copy-start | bytes 6291460
  7.2 78.3 %all-gather.8.cloned.1.call-start = ((), (), s32[]{:S(2)}) async-start(), calls=%async_computation.5 | async-start | bytes 9830400 | tf_op jit(solution)/shard_map/all_gather | solution.py:994
  15.7 151.8 %all-gather.10.cloned.1.call-start = ((), (), s32[]{:S(2)}) async-start(), calls=%async_computation.6 | async-start | bytes 3145728 | tf_op jit(solution)/shard_map/all_gather | solution.py:997
  19.1 159.2 %copy-start.32 = (s32[8,128]{1,0:T(8,128)}, s32[8,128]{1,0:T(8,128)S(1)}, u32[]{:S(2)}) copy-start(s32[8,128]{1,0:T(8,128)S(1)} %select_reduce_fusion) | copy-start | bytes 12292
  24.4 55.8 %all-to-all-start = ((bf16[8,128,1024]{2,1,0:T(8,128)(2,1)}), bf16[8,128,1024]{2,1,0:T(8,128)(2,1)}, u32[]{:S(2)}, u32[]{:S(2)}) async-start(bf16[8,128,1024]{2,1,0:T(8,128)(2,1)} %bitcast.112), calls=%async_computation | async-start | bytes 4194304 | tf_op jit(solution)/shard_map/all_to_all | solution.py:966
  31.9 195.7 %all-gather.14.cloned.1.call-start = ((), (), s32[]{:S(2)}) async-start(), calls=%async_computation.8 | async-start | bytes 8650752 | tf_op jit(solution)/shard_map/all_gather | solution.py:995
  45.1 194.3 %copy-start.34 = (s32[1024]{0:T(1024)}, s32[1024]{0:T(1024)S(1)}, u32[]{:S(2)}) copy-start(s32[1024]{0:T(1024)S(1)} %fusion.82) | copy-start | bytes 12292
  96.3 5.3 collective-permute-start
  137.6 11.0 %collective-permute-start.1 = (bf16[4,128,384]{2,1,0:T(8,128)(2,1)}, bf16[4,128,384]{2,1,0:T(8,128)(2,1)S(1)}, u32[]{:S(2)}, u32[]{:S(2)}) collective-permute-start(bf16[4,128,384]{2,1,0:T(8,128)(2,1)} %get-tuple-element.59), channel_id=1, source_target_pairs={{0,4},{4,8},{8,12},{12,16},{16,20},{20,24},{24,28},{1,5},{5,9},{9,... | collective-permute-start | bytes 1179656 | tf_op jit(solution)/shard_map/ppermute | solution.py:607
  150.9 11.0 %collective-permute-start.2 = (bf16[4,128,384]{2,1,0:T(8,128)(2,1)S(1)}, bf16[4,128,384]{2,1,0:T(8,128)(2,1)S(1)}, u32[]{:S(2)}, u32[]{:S(2)}) collective-permute-start(bf16[4,128,384]{2,1,0:T(8,128)(2,1)S(1)} %pad_maximum_fusion.5), channel_id=1, source_target_pairs={{0,8},{4,12},{8,16},{12,20},{16,24},{20,28},{1,9},{5,13},{9,17},{1... | collective-permute-start | bytes 1179656 | tf_op jit(solution)/shard_map/ppermute | solution.py:607
  162.1 5.5 collective-permute-start.3
  176.9 43.8 %collective-permute-start.4 = (bf16[1024,1024]{1,0:T(8,128)(2,1)}, bf16[1024,1024]{1,0:T(8,128)(2,1)}, u32[]{:S(2)}, u32[]{:S(2)}) collective-permute-start(bf16[1024,1024]{1,0:T(8,128)(2,1)} %get-tuple-element.61), channel_id=1, source_target_pairs={{0,2},{2,0},{1,3},{3,1},{4,6},{6,4},{5,7},{7,5},{8,10},{10,8},{9,1... | collective-permute-start | bytes 6291464 | tf_op jit(solution)/shard_map/ppermute | solution.py:648
  182.0 57.3 %all-to-all-start.1 = ((bf16[8,128,1024]{2,1,0:T(8,128)(2,1)}), bf16[8,128,1024]{2,1,0:T(8,128)(2,1)}, u32[]{:S(2)}, u32[]{:S(2)}) async-start(bf16[8,128,1024]{2,1,0:T(8,128)(2,1)} %bitcast.115), calls=%async_computation.1 | async-start | bytes 4194304 | tf_op jit(solution)/shard_map/all_to_all | solution.py:966
  193.0 51.6 %all-gather.12.cloned.1.call-start = ((), (), s32[]{:S(2)}) async-start(), calls=%async_computation.7 | async-start | bytes 4325376 | tf_op jit(solution)/shard_map/all_gather | solution.py:996
  193.6 283.5 %reduce-scatter.2.cloned.1.call-start = ((), (), s32[]{:S(2)}) async-start(), calls=%async_computation.9 | async-start | bytes 9191424 | tf_op jit(solution)/shard_map/reduce_scatter | solution.py:904
  193.6 130.0 %copy-start.18 = (f32[1,4,2,128]{3,1,2,0:T(4,128)}, f32[1,4,2,128]{3,1,2,0:T(4,128)S(1)}, u32[]{:S(2)}) copy-start(f32[1,4,2,128]{3,1,2,0:T(4,128)S(1)} %copy.104) | copy-start | bytes 12292
  270.8 42.9 %collective-permute-start.5 = (bf16[1024,1024]{1,0:T(8,128)(2,1)}, bf16[1024,1024]{1,0:T(8,128)(2,1)}, u32[]{:S(2)}, u32[]{:S(2)}) collective-permute-start(bf16[1024,1024]{1,0:T(8,128)(2,1)} %convolution_convert_fusion.7), channel_id=1, source_target_pairs={{0,2},{2,0},{1,3},{3,1},{4,6},{6,4},{5,7},{7,5},{8,10},{10,8},{9,1... | collective-permute-start | bytes 6291464 | tf_op jit(solution)/shard_map/ppermute | solution.py:648
  346.5 10.1 %collective-permute-start.7 = (bf16[4,128,256]{2,1,0:T(8,128)(2,1)}, bf16[4,128,256]{2,1,0:T(8,128)(2,1)S(1)}, u32[]{:S(2)}, u32[]{:S(2)}) collective-permute-start(bf16[4,128,256]{2,1,0:T(8,128)(2,1)} %get-tuple-element.74), channel_id=1, source_target_pairs={{4,0},{8,4},{12,8},{16,12},{20,16},{24,20},{28,24},{5,1},{9,5},{13... | collective-permute-start | bytes 786440 | tf_op jit(solution)/shard_map/ppermute | solution.py:607
  347.8 17.2 %collective-permute-start.8 = (bf16[4,128,128]{2,1,0:T(8,128)(2,1)S(1)}, bf16[4,128,128]{2,1,0:T(8,128)(2,1)S(1)}, u32[]{:S(2)}, u32[]{:S(2)}) collective-permute-start(bf16[4,128,128]{2,1,0:T(8,128)(2,1)S(1)} %slice.387), channel_id=1, source_target_pairs={{4,0},{8,4},{12,8},{16,12},{20,16},{24,20},{28,24},{5,1},{9,5},{13... | collective-permute-start | bytes 393224 | tf_op jit(solution)/shard_map/ppermute | solution.py:607
  350.9 319.2 %collective-permute-start.13 = (bf16[256]{0:T(256)(128)(2,1)}, bf16[256]{0:T(256)(128)(2,1)}, u32[]{:S(2)}, u32[]{:S(2)}) collective-permute-start(bf16[256]{0:T(256)(128)(2,1)} %reduce_sum.99), channel_id=1, source_target_pairs={{0,2},{2,0},{1,3},{3,1},{4,6},{6,4},{5,7},{7,5},{8,10},{10,8},{9,1... | collective-permute-start | bytes 1544 | tf_op jit(solution)/shard_map/ppermute | solution.py:648
  358.0 26.7 %collective-permute-start.9 = (bf16[4,128,256]{2,1,0:T(8,128)(2,1)S(1)}, bf16[4,128,256]{2,1,0:T(8,128)(2,1)S(1)}, u32[]{:S(2)}, u32[]{:S(2)}) collective-permute-start(bf16[4,128,256]{2,1,0:T(8,128)(2,1)S(1)} %add_convert_fusion.5), channel_id=1, source_target_pairs={{8,0},{12,4},{16,8},{20,12},{24,16},{28,20},{9,1},{13,5},{17,9},{2... | collective-permute-start | bytes 786440 | tf_op jit(solution)/shard_map/ppermute | solution.py:607
  385.0 10.4 %collective-permute-start.10 = (bf16[4,128,256]{2,1,0:T(8,128)(2,1)S(1)}, bf16[4,128,256]{2,1,0:T(8,128)(2,1)S(1)}, u32[]{:S(2)}, u32[]{:S(2)}) collective-permute-start(bf16[4,128,256]{2,1,0:T(8,128)(2,1)S(1)} %add_convert_fusion.4), channel_id=1, source_target_pairs={{4,0},{8,4},{12,8},{16,12},{20,16},{24,20},{28,24},{5,1},{9,5},{13... | collective-permute-start | bytes 786440 | tf_op jit(solution)/shard_map/ppermute | solution.py:607
  390.2 73.6 %collective-permute-start.6 = (bf16[1024,1024]{1,0:T(8,128)(2,1)}, bf16[1024,1024]{1,0:T(8,128)(2,1)}, u32[]{:S(2)}, u32[]{:S(2)}) collective-permute-start(bf16[1024,1024]{1,0:T(8,128)(2,1)} %convolution_convert_fusion.6), channel_id=1, source_target_pairs={{0,2},{2,0},{1,3},{3,1},{4,6},{6,4},{5,7},{7,5},{8,10},{10,8},{9,1... | collective-permute-start | bytes 6291464 | tf_op jit(solution)/shard_map/ppermute | solution.py:648
  447.8 16.0 %collective-permute-start.11 = (f32[8,2048]{1,0:T(8,128)}, f32[8,2048]{1,0:T(8,128)S(1)}, u32[]{:S(2)}, u32[]{:S(2)}) collective-permute-start(f32[8,2048]{1,0:T(8,128)} %get-tuple-element.79), channel_id=1, source_target_pairs={{4,0},{8,4},{12,8},{16,12},{20,16},{24,20},{28,24},{5,1},{9,5},{13... | collective-permute-start | bytes 196616 | tf_op jit(solution)/shard_map/ppermute | solution.py:607
  471.2 194.3 %all-to-all-start.2 = ((bf16[8,128,1024]{2,1,0:T(8,128)(2,1)}), bf16[8,128,1024]{2,1,0:T(8,128)(2,1)}, u32[]{:S(2)}, u32[]{:S(2)}) async-start(bf16[8,128,1024]{2,1,0:T(8,128)(2,1)} %bitcast.114), calls=%async_computation.2 | async-start | bytes 4194304 | tf_op jit(solution)/shard_map/all_to_all | solution.py:972
  476.8 245.6 %all-gather.16.cloned.1.call-start = ((), (), s32[]{:S(2)}) async-start(), calls=%async_computation.10 | async-start | bytes 4866048 | tf_op jit(solution)/shard_map/all_gather | solution.py:1092
  498.4 157.3 %collective-permute-start.12 = (bf16[1024,1024]{1,0:T(8,128)(2,1)S(1)}, bf16[1024,1024]{1,0:T(8,128)(2,1)S(1)}, u32[]{:S(2)}, u32[]{:S(2)}) collective-permute-start(bf16[1024,1024]{1,0:T(8,128)(2,1)S(1)} %fusion.54), channel_id=1, source_target_pairs={{0,2},{2,0},{1,3},{3,1},{4,6},{6,4},{5,7},{7,5},{8,10},{10,8},{9,1... | collective-permute-start | bytes 6291464 | tf_op jit(solution)/shard_map/ppermute | solution.py:648
  665.5 53.1 %all-to-all-start.3 = ((bf16[8,128,1024]{2,1,0:T(8,128)(2,1)}), bf16[8,128,1024]{2,1,0:T(8,128)(2,1)S(1)}, u32[]{:S(2)}, u32[]{:S(2)}) async-start(bf16[8,128,1024]{2,1,0:T(8,128)(2,1)} %bitcast.111), calls=%async_computation.4 | async-start | bytes 4194304 | tf_op jit(solution)/shard_map/all_to_all | solution.py:972
  670.8 5.6 collective-permute-start.14
  676.6 5.7 collective-permute-start.15
  682.2 19.0 %collective-permute-start.16 = (f32[5256]{0:T(1024)S(1)}, f32[5256]{0:T(1024)S(1)}, u32[]{:S(2)}, u32[]{:S(2)}) collective-permute-start(f32[5256]{0:T(1024)S(1)} %add.172), channel_id=1, source_target_pairs={{0,8},{4,12},{8,0},{12,4},{16,24},{20,28},{24,16},{28,20},{1,9},{5... | collective-permute-start | bytes 63080 | tf_op jit(solution)/shard_map/ppermute | solution.py:653
  701.3 13.8 %collective-permute-start.17 = (f32[5256]{0:T(1024)S(1)}, f32[5256]{0:T(1024)S(1)}, u32[]{:S(2)}, u32[]{:S(2)}) collective-permute-start(f32[5256]{0:T(1024)S(1)} %add.173), channel_id=1, source_target_pairs={{0,16},{4,20},{8,24},{12,28},{16,0},{20,4},{24,8},{28,12},{1,17},{... | collective-permute-start | bytes 63080 | tf_op jit(solution)/shard_map/ppermute | solution.py:653
  (52 other events, 563.1 us)
Sparse Core Ops, SparseCore 0:
  15.8 19.8 all-gather.7
  37.3 11.7 all-gather.9
  51.2 17.1 all-gather.13
  195.1 12.2 all-gather.11
  318.9 126.2 reduce-scatter.1
  479.5 113.5 all-gather.15

commit v3 on v2

--- a/solution.py
+++ b/solution.py
@@ -243,47 +243,182 @@
     )(proj, proj, flags, halo, taps, head)
 
 
-def mix_kernel(heads, dk, dv, local, qa, entering, zgate, gain, wout, y_out, part_out):
-    for h in range(heads):
-        at = slice(h * dv, (h + 1) * dv)
-        o = local[:, at] + mm(qa[:, h * dk : (h + 1) * dk], entering[h])
-        so = lax.rsqrt(jnp.mean(o * o, axis=-1, keepdims=True) + EPS)
-        y_out[:, at] = (o * so * gain[0:1, :] * silu(zgate[:, at])).astype(bf16)
-    part_out[...] = mm(y_out[...], wout[...]).astype(part_out.dtype)
-
-
-def delta_mix(local, qa, entering, proj, gain, wout, heads, dk, dv):
-    rows = local.shape[0]
-    size = 2 * CHUNK
-    model = wout.shape[1]
+def block_kernel(
+    heads, dk, dv, tiles,
+    local, qa, entering, zgate, gain, wout, res, e_now, gain_two, wwide, wdown, e_late,
+    y_out, down_out, r_out, dr_out, er_out, gain_grad, grads_out,
+    part_own, part_in, dn_own, dn_in, r_keep, hid_out, dwide_out, grads, stage, gain_sum,
+    part_sems, dn_sems, out_sems,
+):
+    step = pl.program_id(0)
+    hidden = wdown.shape[0]
+    partner = {"tp": 1 - lax.axis_index("tp")}
+
+    def swap(own, arrived, sems, t):
+        return pltpu.make_async_remote_copy(
+            src_ref=own.at[t],
+            dst_ref=arrived.at[t],
+            send_sem=sems.at[0, t],
+            recv_sem=sems.at[1, t],
+            device_id=partner,
+            device_id_type=pl.DeviceIdType.MESH,
+        )
+
+    @pl.when(step == 0)
+    def _():
+        barrier = pltpu.get_barrier_semaphore()
+        pl.semaphore_signal(barrier, inc=1, device_id=partner, device_id_type=pl.DeviceIdType.MESH)
+        pl.semaphore_wait(barrier, 1)
+        gain_sum[...] = jnp.zeros_like(gain_sum)
+
+        def clear(i, carry):
+            grads[pl.ds(pl.multiple_of(i * 128, 128), 128), :] = jnp.zeros((128, grads.shape[1]), f32)
+            return carry
+
+        lax.fori_loop(0, grads.shape[0] // 128, clear, 0)
+
+    @pl.when(step < tiles)
+    def _():
+        for h in range(heads):
+            at = slice(h * dv, (h + 1) * dv)
+            o = local[:, at] + mm(qa[:, h * dk : (h + 1) * dk], entering[h])
+            so = lax.rsqrt(jnp.mean(o * o, axis=-1, keepdims=True) + EPS)
+            y_out[:, at] = (o * so * gain[0:1, :] * silu(zgate[:, at])).astype(bf16)
+        part_own[step] = mm(y_out[...], wout[...]).astype(bf16)
+        swap(part_own, part_in, part_sems, step).start()
+
+    @pl.when((step >= 1) & (step <= tiles))
+    def _():
+        t = step - 1
+        swap(part_own, part_in, part_sems, t).wait()
+        r = res[...].astype(f32) + part_own[t].astype(f32) + part_in[t].astype(f32)
+        r_keep[t] = r
+        r_out[...] = r
+        inv = lax.rsqrt(jnp.mean(r * r, axis=-1, keepdims=True) + EPS)
+        n2 = (r * inv * gain_two[0:1, :]).astype(bf16)
+        gp = mm(n2, wwide[:, 0:hidden])
+        up = mm(n2, wwide[:, hidden : 2 * hidden])
+        dhid = mm_nt(e_now[...], wdown[...])
+        sig = jax.nn.sigmoid(gp)
+        act = gp * sig
+        hid_out[...] = (act * up).astype(bf16)
+        dwide_out[:, 0:hidden] = (dhid * up * (sig * (1.0 + gp * (1.0 - sig)))).astype(bf16)
+        dwide_out[:, hidden : 2 * hidden] = (dhid * act).astype(bf16)
+        dn_own[t] = mm_nt(dwide_out[...], wwide[...]).astype(bf16)
+        swap(dn_own, dn_in, dn_sems, t).start()
+        down_out[...] = mm(hid_out[...], wdown[...]).astype(bf16)
+        for lo in range(0, 2 * hidden, 2 * LANES):
+            at = slice(lo, lo + 2 * LANES)
+            grads[at, :] += mm_tn(dwide_out[:, at], n2)
+        for lo in range(0, hidden, LANES):
+            at = slice(lo, lo + LANES)
+            grads[2 * hidden + lo : 2 * hidden + lo + LANES, :] += mm_tn(hid_out[:, at], e_now[...])
+
+    @pl.when(step >= 2)
+    def _():
+        t = step - 2
+        swap(dn_own, dn_in, dn_sems, t).wait()
+        dn2 = dn_own[t].astype(f32) + dn_in[t].astype(f32)
+        r = r_keep[t]
+        inv = lax.rsqrt(jnp.mean(r * r, axis=-1, keepdims=True) + EPS)
+        scaled = gain_two[0:1, :] * dn2
+        gain_sum[0:1, :] += jnp.sum(dn2 * r * inv, axis=0, keepdims=True)
+        dr = (
+            e_late[...].astype(f32)
+            + inv * scaled
+            - r * (inv * inv * inv * jnp.mean(scaled * r, axis=-1, keepdims=True))
+        )
+        dr_out[...] = dr
+        er_out[...] = dr.astype(bf16)
+        gain_grad[...] = gain_sum[...]
+
+    @pl.when(step == tiles + 1)
+    def _():
+        long, cols = hidden // 2, grads.shape[1] // 2
+        chunks = []
+        for f in range(2):
+            chunks += [(j * long, f * cols) for j in range(4)]
+            chunks += [(2 * hidden + f * long, j * cols) for j in range(2)]
+
+        def out_copy(c):
+            return pltpu.make_async_copy(
+                stage.at[c % 2], grads_out.at[pl.ds(c * long, long), :], out_sems.at[c % 2]
+            )
+
+        for c, (row, col) in enumerate(chunks):
+            if c >= 2:
+                out_copy(c - 2).wait()
+            stage[c % 2] = grads[row : row + long, col : col + cols].astype(bf16)
+            out_copy(c).start()
+        for c in (len(chunks) - 2, len(chunks) - 1):
+            out_copy(c).wait()
+
+
+def block_rest(
+    local, qa, entering, proj, gain, wout, res, e, gain_two, wwide, wdown, heads, dk, dv, collective_id
+):
+    rows, model = res.shape
+    size = CHUNK
+    tiles = rows // size
+    hidden = wdown.shape[0]
     z_at = (2 * heads * dk + heads * dv) // (heads * dv)
 
-    def rowwise(cols, at=0):
-        return pl.BlockSpec((size, cols), lambda n: (n, at))
-
+    def rowwise(cols, lag, at=0):
+        return pl.BlockSpec((size, cols), lambda n: (jnp.clip(n - lag, 0, tiles - 1), at))
+
+    def kept(shape):
+        return pl.BlockSpec(shape, lambda n: (0,) * len(shape), pipeline_mode=pl.Buffered(1))
+
+    outs = [
+        ((rows, heads * dv), bf16, rowwise(heads * dv, 0)),
+        ((rows, model), bf16, rowwise(model, 1)),
+        ((rows, model), f32, rowwise(model, 1)),
+        ((rows, model), f32, rowwise(model, 2)),
+        ((rows, model), bf16, rowwise(model, 2)),
+        ((8, model), f32, whole((8, model))),
+        ((6 * hidden, model // 2), bf16, pl.BlockSpec(memory_space=pl.ANY)),
+    ]
     return pl.pallas_call(
-        functools.partial(mix_kernel, heads, dk, dv),
-        grid=(rows // size,),
+        functools.partial(block_kernel, heads, dk, dv, tiles),
+        grid=(tiles + 2,),
         in_specs=[
-            rowwise(heads * dv),
-            rowwise(heads * dk),
-            whole((heads, dk, dv)),
-            rowwise(heads * dv, z_at),
-            whole((8, dv)),
-            whole(wout.shape),
+            rowwise(heads * dv, 0),
+            rowwise(heads * dk, 0),
+            kept((heads, dk, dv)),
+            rowwise(heads * dv, 0, z_at),
+            kept((8, dv)),
+            kept(wout.shape),
+            rowwise(model, 1),
+            rowwise(model, 1),
+            kept((8, model)),
+            kept(wwide.shape),
+            kept(wdown.shape),
+            rowwise(model, 2),
         ],
-        out_specs=[rowwise(heads * dv), rowwise(model)],
-        out_shape=[
-            jax.ShapeDtypeStruct((rows, heads * dv), bf16),
-            jax.ShapeDtypeStruct((rows, model), bf16),
+        out_specs=[spec for _, _, spec in outs],
+        out_shape=[jax.ShapeDtypeStruct(shape, kind) for shape, kind, _ in outs],
+        scratch_shapes=[pltpu.VMEM((tiles, size, model), bf16)] * 4
+        + [
+            pltpu.VMEM((tiles, size, model), f32),
+            pltpu.VMEM((size, hidden), bf16),
+            pltpu.VMEM((size, 2 * hidden), bf16),
+            pltpu.VMEM((3 * hidden, model), f32),
+            pltpu.VMEM((2, hidden // 2, model // 2), bf16),
+            pltpu.VMEM((8, model), f32),
+            pltpu.SemaphoreType.DMA((2, tiles)),
+            pltpu.SemaphoreType.DMA((2, tiles)),
+            pltpu.SemaphoreType.DMA((2,)),
         ],
-        compiler_params=vmem(),
+        compiler_params=pltpu.CompilerParams(
+            collective_id=collective_id,
+            has_side_effects=True,
+            vmem_limit_bytes=60 * MIB,
+            dimension_semantics=("arbitrary",),
+        ),
         cost_estimate=pl.CostEstimate(
-            flops=10 * rows * heads * dv * model,
-            bytes_accessed=rows * heads * dv * 14,
-            transcendentals=rows * heads * dv,
+            flops=100 * 10**9, bytes_accessed=rows * model * 40, transcendentals=rows * hidden
         ),
-    )(local, qa, entering, proj, gain, wout)
+    )(local, qa, entering, proj, gain, wout, res, e, gain_two, wwide, wdown, e)
 
 
 def back_kernel(
@@ -607,37 +742,128 @@
     return lax.ppermute(value, axis, route)
 
 
-def heads_mm(a, b):
-    return jnp.einsum("hij,hjk->hik", a, b, preferred_element_type=f32)
-
-
-def heads_mm_tn(a, b):
-    return jnp.einsum("hji,hjk->hik", a, b, preferred_element_type=f32)
+def chain_kernel(forward, levels, *refs):
+    if forward:
+        own, out, mats, runs, arrived, send_sem, recv_sem = refs
+    else:
+        own, maps, out, runs, arrived, send_sem, recv_sem = refs
+    heads, dk = own.shape[:2]
+    dv = out.shape[2]
+    count = lax.axis_size("ctx")
+    me = lax.axis_index("ctx")
+    place = me if forward else count - 1 - me
+    way = 1 if forward else -1
+    distances = [2**j for j in range(levels)] + [1]
+    reaches = sorted(set(distances))
+    barrier = pltpu.get_barrier_semaphore()
+    known = jnp.int32(0)
+    for d in reaches:
+        for sign in (1, -1):
+            there = (me + sign * d >= 0) & (me + sign * d < count)
+            known = known + there.astype(jnp.int32)
+
+            @pl.when(there)
+            def _(sign=sign, d=d):
+                pl.semaphore_signal(
+                    barrier, inc=1, device_id={"ctx": me + sign * d},
+                    device_id_type=pl.DeviceIdType.MESH,
+                )
+
+    pl.semaphore_wait(barrier, known)
+
+    def copy(j, h):
+        width = dv if j >= levels - 1 else own.shape[2]
+        source = own if j == 0 else runs.at[j - 1]
+        return pltpu.make_async_remote_copy(
+            src_ref=source.at[h, :, pl.ds(0, width)],
+            dst_ref=arrived.at[j, h, :, pl.ds(0, width)],
+            send_sem=send_sem.at[j, h],
+            recv_sem=recv_sem.at[j, h],
+            device_id={"ctx": me + way * distances[j]},
+            device_id_type=pl.DeviceIdType.MESH,
+        )
+
+    def send(j, h):
+        @pl.when(place + distances[j] < count)
+        def _():
+            copy(j, h).start()
+
+    for h in range(heads):
+        send(0, h)
+    for j in range(levels + 1):
+        for h in range(heads):
+
+            @pl.when(place >= distances[j])
+            def _(j=j, h=h):
+                copy(j, h).wait_recv()
+
+            @pl.when(place < distances[j])
+            def _(j=j, h=h):
+                arrived[j, h] = jnp.zeros(arrived.shape[2:], bf16)
+
+            if j == levels:
+                out[h] = arrived[j, h, :, 0:dv]
+                continue
+            run = own[h] if j == 0 else runs[j - 1, h]
+            if forward:
+                matrix = run[:, dv:]
+                width = dv if j == levels - 1 else dv + dk
+                joined = mm(matrix, arrived[j, h, :, 0:width])
+                runs[j, h, :, 0:dv] = (run[:, 0:dv].astype(f32) + joined[:, 0:dv]).astype(bf16)
+                if j < levels - 1:
+                    runs[j, h, :, dv : dv + dk] = joined[:, dv:].astype(bf16)
+                    mats[j, h] = joined[:, dv:].astype(bf16)
+            else:
+                joined = mm_tn(maps[j, h], arrived[j, h])
+                runs[j, h] = (run.astype(f32) + joined).astype(bf16)
+            send(j + 1, h)
+    for j in range(levels + 1):
+        for h in range(heads):
+
+            @pl.when(place + distances[j] < count)
+            def _(j=j, h=h):
+                copy(j, h).wait_send()
+
+
+def chained(own, maps, dv, levels, collective_id):
+    heads, dk, width = own.shape
+    forward = maps is None
+    spec = pl.BlockSpec(memory_space=pltpu.VMEM)
+    shapes = [(heads, dk, dv)] + ([(max(levels - 1, 1), heads, dk, dk)] if forward else [])
+    return pl.pallas_call(
+        functools.partial(chain_kernel, forward, levels),
+        in_specs=[spec] * (1 if forward else 2),
+        out_specs=[spec] * len(shapes),
+        out_shape=[jax.ShapeDtypeStruct(shape, bf16) for shape in shapes],
+        scratch_shapes=[
+            pltpu.VMEM((levels, heads, dk, width), bf16),
+            pltpu.VMEM((levels + 1, heads, dk, width), bf16),
+            pltpu.SemaphoreType.DMA((levels + 1, heads)),
+            pltpu.SemaphoreType.DMA((levels + 1, heads)),
+        ],
+        compiler_params=pltpu.CompilerParams(
+            collective_id=collective_id, has_side_effects=True, vmem_limit_bytes=24 * MIB
+        ),
+        cost_estimate=pl.CostEstimate(flops=25 * 10**9, bytes_accessed=own.size * 16, transcendentals=0),
+    )(*([own] if forward else [own, maps]))
+
+
+def levels_of(reach):
+    levels = 1
+    while 2**levels < reach:
+        levels += 1
+    return levels
 
 
 def entering_state(own, dv, reach):
-    runs = []
-    run = own
-    distance = 1
-    while distance < reach:
-        runs.append(run[:, :, dv:])
-        before = shifted(run, "ctx", distance)
-        joined = heads_mm(run[:, :, dv:], before)
-        run = jnp.concatenate(
-            [run[:, :, :dv].astype(f32) + joined[:, :, :dv], joined[:, :, dv:]], axis=-1
-        ).astype(bf16)
-        distance *= 2
-    entering = shifted(run[:, :, :dv], "ctx", 1)
-    ahead = [part if j == 0 else shifted(part, "ctx", 1 - 2**j) for j, part in enumerate(runs)]
-    return entering, ahead
+    levels = levels_of(reach)
+    entering, mats = chained(own, None, dv, levels, 3)
+    ahead = [own[:, :, dv:]] + [shifted(mats[j - 1], "ctx", 1 - 2**j) for j in range(1, levels)]
+    return entering, jnp.stack(ahead)
 
 
 def leaving_grad(own, ahead):
-    run = own
-    for j, maps in enumerate(ahead):
-        later = shifted(run, "ctx", -(2**j))
-        run = (run.astype(f32) + heads_mm_tn(maps, later)).astype(bf16)
-    return shifted(run, "ctx", -1)
+    return chained(own, ahead, own.shape[2], ahead.shape[0], 4)[0]
 
 
 def summed_over_tp(part):
@@ -962,19 +1188,16 @@
             maps, values, (((0 if transposed else 1,), (0,)), ((), ())), preferred_element_type=f32
         ).astype(bf16)
 
-    def to_packed(values):
-        arrived = lax.all_to_all(
-            moved(gather_send, values), "ctx", split_axis=0, concat_axis=0, tiled=True
-        )
-        return moved(gather_recv, arrived)
-
-    def to_given(values):
-        arrived = lax.all_to_all(
-            moved(gather_recv, values, True), "ctx", split_axis=0, concat_axis=0, tiled=True
-        )
-        return moved(gather_send, arrived, True)
-
-    resident = to_packed(tokens[0])
+    def exchanged(values):
+        return lax.all_to_all(values, "ctx", split_axis=0, concat_axis=0, tiled=True)
+
+    def sent_to_packed(values):
+        return exchanged(moved(gather_send, values))
+
+    def sent_to_given(values):
+        return exchanged(moved(gather_recv, values, True))
+
+    resident = moved(gather_recv, sent_to_packed(tokens[0]))
 
     offsets = jnp.cumsum(lengths[0]) - lengths[0]
     positions = me * rows - halo_rows + jnp.arange(rows + 2 * halo_rows, dtype=jnp.int32)
@@ -1030,25 +1253,15 @@
     conv, local, qa, states, tinv, uval, wkey, qeff, ktail, cum, last = delta_forward(
         proj, flags, halo, taps, head, heads, dk, dv
     )
+    last, arrived = lax.optimization_barrier((last, sent_to_packed(cotangent[0])))
+    e = moved(gather_recv, arrived)
     entering, ahead = entering_state(last, dv, reach)
-    entering, cot = lax.optimization_barrier((entering, cotangent[0]))
-    e = to_packed(cot)
-    y1, part = delta_mix(local, qa, entering, proj, gain_rows, w_output, heads, dk, dv)
-
-    r = x + summed_over_tp(part)
-    inv_two = lax.rsqrt(jnp.mean(r * r, axis=-1, keepdims=True) + EPS)
-    n2 = (r * inv_two * gain_two).astype(bf16)
-    wide = jnp.dot(n2, w_wide, preferred_element_type=f32)
-    gp, up = wide[:, :hidden_cols], wide[:, hidden_cols:]
-    act = silu(gp)
-    hid = (act * up).astype(bf16)
-    down = jnp.dot(hid, w_down, preferred_element_type=f32).astype(bf16)
-    dhid = lax.dot_general(e, w_down, (((1,), (1,)), ((), ())), preferred_element_type=f32)
-    dwide = jnp.concatenate(
-        [(dhid * up * silu_grad(gp)).astype(bf16), (dhid * act).astype(bf16)], axis=1
-    )
-    dn2 = lax.dot_general(dwide, w_wide, (((1,), (1,)), ((), ())), preferred_element_type=f32)
-    dn2 = summed_over_tp(dn2.astype(bf16))
+    y1, down, r, dr, er, mlp_gain_sum, mlp_cat = block_rest(
+        local, qa, entering, proj, gain_rows, w_output, resident, e,
+        jnp.broadcast_to(gain_two[None, :], (8, model)), w_wide, w_down, heads, dk, dv, 2,
+    )
+    grad_mlp_gain = mlp_gain_sum[0]
+
     def outer(a, b):
         return lax.dot_general(
             a, b, (((0,), (0,)), ((), ())), preferred_element_type=f32
@@ -1058,37 +1271,24 @@
         return grad.reshape(fs, grad.shape[0] // fs, *grad.shape[1:])
 
     half = model // fs
-    g_down = outer(hid, e)
     down_rows = hidden_cols // fs
-    pieces = []
-    for f in range(fs):
-        pieces.append(outer(dwide, n2[:, f * half : (f + 1) * half]))
-        rows_f = g_down[f * down_rows : (f + 1) * down_rows]
-        pieces += [rows_f[:, j * half : (j + 1) * half] for j in range(fs)]
-    dn2, down, mlp_cat = lax.optimization_barrier((dn2, down, jnp.concatenate(pieces, axis=0)))
     mlp_share = scattered(mlp_cat)
     result = (r + summed_over_tp(down)).astype(bf16)
-    grad_mlp_gain = jnp.sum(dn2 * r * inv_two, axis=0)
-    scaled = gain_two * dn2
-    dr = (
-        e.astype(f32)
-        + inv_two * scaled
-        - r * (inv_two * inv_two * inv_two * jnp.mean(scaled * r, axis=-1, keepdims=True))
-    )
-    er = dr.astype(bf16)
 
     dz, do, dgain_out, first = delta_back(
         er, local, qa, entering, proj, gain_rows, w_output, qeff, wkey, ktail, cum, heads, dk, dv
     )
     leaving = leaving_grad(first, ahead)
-    block_out = to_given(result)
     g_z = outer(n1, dz)
     g_o = outer(y1, er)
     dproj, dab, tail_rows, head_rows, dtaps, dhead = delta_grad(
         proj, conv, flags, cum, halo, taps, head, do, tinv, uval, wkey, states, entering, leaving,
         heads, dk, dv,
     )
-    dproj, mlp_share = lax.optimization_barrier((dproj, mlp_share))
+    dproj, mlp_share, arrived = lax.optimization_barrier(
+        (dproj, mlp_share, sent_to_given(result))
+    )
+    block_out = moved(gather_send, arrived, True)
     g_mlp_all = lax.all_gather(mlp_share, "ctx", axis=0, tiled=True)
     next_rows = shifted(head_rows, "ctx", -1)
     extra = jnp.zeros_like(tail_rows)
@@ -1112,7 +1312,7 @@
         + inv_one * scaled
         - x * (inv_one * inv_one * inv_one * jnp.mean(scaled * x, axis=-1, keepdims=True))
     ).astype(bf16)
-    grad_tokens = to_given(grad_in)
+    grad_tokens = moved(gather_send, sent_to_given(grad_in), True)
 
     def tap_part(lo, channels):
         return dtaps[:TAPS, lo : lo + channels].reshape(TAPS, fs, -1).transpose(1, 0, 2).reshape(fs, -1)

time: 755 us -> 725 us (0.960)
  Pallas kernels: 266 us -> 440 us
  waiting for transfers between devices: 168 us -> 64.7 us
  matrix products: 136 us -> 78.5 us
  other arithmetic: 46.9 us -> 28.3 us
  starting transfers between devices: 66.1 us -> 47.5 us
    pallas_call x1 -> x3, Pallas kernels: 8.62 us -> 198 us  [the longest x1 107 us: block_rest(): pl.pallas_call(functools.partial(block_kernel, heads, dk, dv, tiles), gri...]
    ppermute x9 -> x3, waiting for transfers between devices: 59.1 us -> 5.92 us  [shifted(): return lax.ppermute(value, axis, route)]
    ppermute x5 -> x3, waiting for transfers between devices: 52.6 us -> 0.01 us  [summed_over_tp(): total = total + lax.ppermute(part, 'tp', route).astype(f32)]
    dot_general x8 -> x0, matrix products: 40.2 us -> none  [the longest x1 11.8 us: per_device(): wide = jnp.dot(n2, w_wide, preferred_element_type=f32)]
    ppermute x9 -> x3, starting transfers between devices: 21.4 us -> 6.91 us  [shifted(): return lax.ppermute(value, axis, route)]
    pallas_call x1, Pallas kernels: 156 us -> 141 us  [reduced(): pl.pallas_call(functools.partial(sum_kernel, plan), in_specs=[pl.BlockSpe...]
    dot_general x6 -> x3, matrix products: 31.5 us -> 20.1 us  [outer(): lax.dot_general(a, b, (((0,), (0,)), ((), ())), preferred_element_type=f32)]
    reduce_sum x2 -> x0, other arithmetic: 7.85 us -> none  [the longest x1 4.61 us: per_device(): grad_mlp_gain = jnp.sum(dn2 * r * inv_two, axis=0)]
  transfers between devices with their start and end apart: 28 -> 20, of which waited for: 14 -> 7; matrix products, arithmetic and copies ran while one was open for 22% -> 16% of each run, Pallas kernels for 36% -> 47%
where the time goes in v3:
time: 725 us; the launch traced here: 717 us
  Pallas kernels  440 us (61%)
  matrix products  78.5 us (11%)
  waiting for transfers between devices  64.7 us (9%)
  starting transfers between devices  47.5 us (7%)
  local copies, waits for them, and re-layouts  40.8 us (6%)
  other arithmetic  28.3 us (4%)
  between operations  15.3 us (2%)
    pallas_call x1, Pallas kernels, reduced(): pl.pallas_call(functools.partial(sum_kernel, plan), in_specs=[pl.BlockSpe...  141 us
    pallas_call x1, Pallas kernels, block_rest(): pl.pallas_call(functools.partial(block_kernel, heads, dk, dv, tiles), gri...  107 us
    pallas_call x2, Pallas kernels, chained(): pl.pallas_call(functools.partial(chain_kernel, forward, levels), in_specs...  91.1 us
    pallas_call x1, Pallas kernels, delta_grad(): pl.pallas_call(functools.partial(grad_kernel, heads, dk, dv), grid=(steps...  48.2 us
    dot_general x8, matrix products, moved(): lax.dot_general(maps, values, (((0 if transposed else 1,), (0,)), ((), ()...  36.5 us
    all_to_all x4, waiting for transfers between devices, exchanged(): lax.all_to_all(values, 'ctx', split_axis=0, concat_axis=0, tiled=True)  36.3 us
    pallas_call x1, Pallas kernels, delta_forward(): pl.pallas_call(functools.partial(forward_kernel, heads, dk, dv), grid=(st...  35.3 us
    all_to_all x4, starting transfers between devices, exchanged(): lax.all_to_all(values, 'ctx', split_axis=0, concat_axis=0, tiled=True)  27.8 us
  transfers between devices with their start and end apart: 20, of which 7 were waited for; matrix products, arithmetic and copies ran while one was open for 16% of the time, Pallas kernels for 47%

profile of v3, /device:TPU:0, one launch (start us, length us, event | category | flops | bytes accessed | tf_op | source)
XLA Modules:
  0.0 717.5 jit_solution(196373477301749496)
XLA Ops:
  9.2 6.5 concatenate.34
  19.9 3.7 fusion.42
  23.6 7.4 %all-to-all-start = ((bf16[8,128,1024]{2,1,0:T(8,128)(2,1)}), bf16[8,128,1024]{2,1,0:T(8,128)(2,1)S(1)}, u32[]{:S(2)}, u32[]{:S(2)}) async-start(bf16[8,128,1024]{2,1,0:T(8,128)(2,1)} %bitcast.106), calls=%async_computation | async-start | bytes 4194304 | tf_op jit(solution)/shard_map/all_to_all | solution.py:1192
  45.0 5.5 fusion.45
  50.6 28.7 %all-to-all-done = bf16[8,128,1024]{2,1,0:T(8,128)(2,1)S(1)} async-done(((bf16[8,128,1024]{2,1,0:T(8,128)(2,1)}), bf16[8,128,1024]{2,1,0:T(8,128)(2,1)S(1)}, u32[]{:S(2)}, u32[]{:S(2)}) %all-to-all-start) | async-done | bytes 2097184 | tf_op jit(solution)/shard_map/all_to_all | solution.py:1192
  79.2 4.4 all-to-all-start.1
  84.2 4.0 fusion.9
  88.3 10.8 %fusion.82.proj.ab.zgate = f32[1024,3200]{1,0:T(8,128)S(1)} fusion(bf16[1024,3200]{1,0:T(8,128)(2,1)} %all-gather.8.cloned.1.call-done, bf16[1024,1024]{1,0:T(8,128)(2,1)S(1)} %get-tuple-element.218.res, f32[1024]{0:T(1024)S(1)} %bitcast.127, f32[1024]{0:T(1024)S(1)} %add_rsqrt_fusion), kind=kOutput, calls=%fused_computation.154 | convolution fusion | flops 6715080704 | bytes 21766144 | tf_op jit(solution)/shard_map/dot_general | solution.py:1251
  99.2 3.9 collective-permute-start
  105.6 35.3 %shard_map.365 = (f32[1024,2048]{1,0:T(8,128)}, f32[1024,1024]{1,0:T(8,128)}, bf16[1024,512]{1,0:T(8,128)(2,1)}, bf16[8,4,128,384]{3,2,1,0:T(8,128)(2,1)}, bf16[...) custom-call(f32[1024,3200]{1,0:T(8,128)} %copy-done.36, ...), custom_call_target="tpu_custom_call" | custom-call | flops 13421772800 | bytes 29360128 | tf_op jit(solution)/shard_map/pallas_call | solution.py:220
  141.0 5.3 fusion.49.e_now.e_late
  146.3 30.1 %shard_map.366 = (bf16[4,128,256]{2,1,0:T(8,128)(2,1)S(1)}, bf16[1,4,128,128]{3,2,1,0:T(8,128)(2,1)S(1)}) custom-call(bf16[4,128,384]{2,1,0:T(8,128)(2,1)S(1)} %copy-done.2), custom_call_target="tpu_custom_call" | custom-call | flops 24999999488 | bytes 3145728 | tf_op jit(solution)/shard_map/pallas_call | solution.py:833
  178.3 106.6 %shard_map.367 = (bf16[1024,1024]{1,0:T(8,128)(2,1)}, bf16[1024,1024]{1,0:T(8,128)(2,1)}, f32[1024,1024]{1,0:T(8,128)}, f32[1024,1024]{1,0:T(8,128)}, bf16[1024,...) custom-call(f32[1024,1024]{1,0:T(8,128)} %get-tuple-element.64.local, ...), custom_call_target="tpu_custom_call" | custom-call | flops 99999997952 | bytes 41943040 | tf_op jit(solution)/shard_map/pallas_call | solution.py:381
  288.9 17.7 %shard_map.368 = (bf16[1024,1024]{1,0:T(8,128)(2,1)}, bf16[1024,1024]{1,0:T(8,128)(2,1)}, f32[8,256]{1,0:T(8,128)}, bf16[4,128,256]{2,1,0:T(8,128)(2,1)}) custom-call(bf16[1024,1024]{1,0:T(8,128)(2,1)} %get-tuple-element.70.er, f32[1024,1024]{1,0:T(8,128)} %get-tuple-element.64.local, bf16[1024,512]{1,0:T(8,128)(2,1)} %get-tuple-element.65.qa, ...), custom_call_target="tpu_custom_call" | custom-call | flops 21474836480 | bytes 18874368 | tf_op jit(solution)/shard_map/pallas_call | solution.py:483
  311.3 6.6 convolution_convert_fusion.1.refs_2_
  317.9 4.0 convolution_convert_fusion.2.refs_1_
  322.0 61.0 %shard_map.369.leaving = bf16[4,128,256]{2,1,0:T(8,128)(2,1)S(1)} custom-call(bf16[4,128,256]{2,1,0:T(8,128)(2,1)S(1)} %copy-done.4, bf16[2,4,128,128]{3,2,1,0:T(8,128)(2,1)S(1)} %pad_maximum_fusion.1.refs_1_), custom_call_target="tpu_custom_call" | custom-call | flops 24999999488 | bytes 2097152 | tf_op jit(solution)/shard_map/pallas_call | solution.py:833
  383.8 4.0 fusion.50
  387.9 11.3 %all-to-all-start.2 = ((bf16[8,128,1024]{2,1,0:T(8,128)(2,1)}), bf16[8,128,1024]{2,1,0:T(8,128)(2,1)}, u32[]{:S(2)}, u32[]{:S(2)}) async-start(bf16[8,128,1024]{2,1,0:T(8,128)(2,1)} %bitcast.32), calls=%async_computation.3 | async-start | bytes 4194304 | tf_op jit(solution)/shard_map/all_to_all | solution.py:1192
  399.4 48.2 %shard_map.370 = (bf16[1024,2048]{1,0:T(8,128)(2,1)}, bf16[1024,128]{1,0:T(8,128)(2,1)}, f32[8,2048]{1,0:T(8,128)}, f32[8,2048]{1,0:T(8,128)}, f32[8,2048]{1,0:T(8,128)}, /*index=5*/f32[8,128]{1,0:T(8,128)}) custom-call(f32[1024,3200]{1,0:T(8,128)} %copy-done.36, f32[1024,2048]{1,0:T(8,128)} %get-tuple-element.62.conv, f32[1024,3200]{1,0:T(8,128)} %copy-done.36, ...), custom_call_target="tpu_custom_call" | custom-call | flops 53687091200 | bytes 33554432 | tf_op jit(solution)/shard_map/pallas_call | solution.py:699
  451.3 5.1 collective-permute-done.3
  456.4 7.6 %all-to-all-done.2 = bf16[8,128,1024]{2,1,0:T(8,128)(2,1)} async-done(((bf16[8,128,1024]{2,1,0:T(8,128)(2,1)}), bf16[8,128,1024]{2,1,0:T(8,128)(2,1)}, u32[]{:S(2)}, u32[]{:S(2)}) %all-to-all-start.2) | async-done | bytes 2097184 | tf_op jit(solution)/shard_map/all_to_all | solution.py:1192
  465.6 9.5 %convolution_convert_fusion.refs_0_ = bf16[1024,2176]{1,0:T(8,128)(2,1)} fusion(bf16[1024,128]{1,0:T(8,128)(2,1)} %get-tuple-element.90, bf16[1024,2048]{1,0:T(8,128)(2,1)} %fusion.64, bf16[1024,1024]{1,0:T(8,128)(2,1)S(1)} %copy-done.9, f32[1024]{0:T(1024)S(1)} %bitcast.129, f32[1024]{0:T(1024)S(1)} %copy-done.19), kind=kOutput, calls=%fused_computation.11 | convolution fusion | flops 4578738176 | bytes 11018240 | tf_op jit(solution)/shard_map/dot_general | solution.py:1266
  475.1 10.4 %fusion.54 = bf16[1024,1024]{1,0:T(8,128)(2,1)S(1)} fusion(bf16[1024,3200]{1,0:T(8,128)(2,1)} %all-gather.8.cloned.1.call-done, bf16[1024,128]{1,0:T(8,128)(2,1)S(1)} %copy-done.44, bf16[1024,1024]{1,0:T(8,128)(2,1)S(1)} %copy-done.43, bf16[1024,2048]{1,0:T(8,128)(2,1)S(1)} %copy-done.37), kind=kOutput, calls=%fused_computation.64 | convolution fusion | flops 6731595776 | bytes 15204352 | tf_op jit(solution)/shard_map/dot_general | solution.py:1300
  487.1 141.4 %shard_map.371 = (bf16[512,2176]{1,0:T(8,128)(2,1)}, bf16[512,1024]{1,0:T(8,128)(2,1)}, bf16[512,1024]{1,0:T(8,128)(2,1)}) custom-call(bf16[1024,2176]{1,0:T(8,128)(2,1)} %convolution_convert_fusion.refs_0_, bf16[1024,1024]{1,0:T(8,128)(2,1)} %convolution_convert_fusion.2.refs_1_, bf16[1024,1024]{1,0:T(8,128)(2,1)} %convolution_convert_fusion.1.refs_2_), custom_call_target="tpu_custom_call" | custom-call | flops 109999996928 | bytes 17301504 | tf_op jit(solution)/shard_map/pallas_call | solution.py:1109
  631.7 4.6 fusion.51
  636.3 4.8 all-to-all-start.3
  641.9 5.5 convert_bitcast_fusion.1
  651.2 4.7 collective-permute-done.7
  658.8 13.9 %collective-permute-done.8 = f32[5256]{0:T(1024)S(1)} collective-permute-done((f32[5256]{0:T(1024)S(1)}, f32[5256]{0:T(1024)S(1)}, u32[]{:S(2)}, u32[]{:S(2)}) %collective-permute-start.8) | collective-permute-done | bytes 21056 | tf_op jit(solution)/shard_map/ppermute | solution.py:879
  672.7 4.7 collective-permute-start.9
  690.9 3.8 convert_bitcast_fusion
  (238 shorter events, 81.0 us)
Async XLA Ops:
  7.2 12.7 %copy-start = (bf16[1,1024,1024]{2,1,0:T(8,128)(2,1)S(1)}, bf16[1,1024,1024]{2,1,0:T(8,128)(2,1)}, u32[]{:S(2)}) copy-start(bf16[1,1024,1024]{2,1,0:T(8,128)(2,1)} %param.22) | copy-start | bytes 6291460
  7.2 81.1 %all-gather.8.cloned.1.call-start = ((), (), s32[]{:S(2)}) async-start(), calls=%async_computation.5 | async-start | bytes 9830400 | tf_op jit(solution)/shard_map/all_gather | solution.py:1217
  15.7 161.4 %all-gather.10.cloned.1.call-start = ((), (), s32[]{:S(2)}) async-start(), calls=%async_computation.6 | async-start | bytes 3145728 | tf_op jit(solution)/shard_map/all_gather | solution.py:1220
  16.4 160.7 %all-gather.14.cloned.1.call-start = ((), (), s32[]{:S(2)}) async-start(), calls=%async_computation.8 | async-start | bytes 4325376 | tf_op jit(solution)/shard_map/all_gather | solution.py:1219
  19.9 25.2 %copy-start.26 = (s32[8,128]{1,0:T(8,128)}, s32[8,128]{1,0:T(8,128)S(1)}, u32[]{:S(2)}) copy-start(s32[8,128]{1,0:T(8,128)S(1)} %select_reduce_fusion) | copy-start | bytes 12292
  23.6 55.7 %all-to-all-start = ((bf16[8,128,1024]{2,1,0:T(8,128)(2,1)}), bf16[8,128,1024]{2,1,0:T(8,128)(2,1)S(1)}, u32[]{:S(2)}, u32[]{:S(2)}) async-start(bf16[8,128,1024]{2,1,0:T(8,128)(2,1)} %bitcast.106), calls=%async_computation | async-start | bytes 4194304 | tf_op jit(solution)/shard_map/all_to_all | solution.py:1192
  31.0 146.1 %all-gather.12.cloned.1.call-start = ((), (), s32[]{:S(2)}) async-start(), calls=%async_computation.7 | async-start | bytes 8650752 | tf_op jit(solution)/shard_map/all_gather | solution.py:1218
  40.7 47.6 %copy-start.16 = (f32[1,4,2,128]{3,1,2,0:T(4,128)}, f32[1,4,2,128]{3,1,2,0:T(4,128)S(1)}, u32[]{:S(2)}) copy-start(f32[1,4,2,128]{3,1,2,0:T(4,128)S(1)} %copy.90) | copy-start | bytes 12292
  45.0 95.9 %copy-start.28 = (s32[1024]{0:T(1024)}, s32[1024]{0:T(1024)S(1)}, u32[]{:S(2)}) copy-start(s32[1024]{0:T(1024)S(1)} %fusion.69) | copy-start | bytes 12292
  79.2 61.7 %all-to-all-start.1 = ((bf16[8,128,1024]{2,1,0:T(8,128)(2,1)}), bf16[8,128,1024]{2,1,0:T(8,128)(2,1)}, u32[]{:S(2)}, u32[]{:S(2)}) async-start(bf16[8,128,1024]{2,1,0:T(8,128)(2,1)} %bitcast.109), calls=%async_computation.1 | async-start | bytes 4194304 | tf_op jit(solution)/shard_map/all_to_all | solution.py:1192
  83.6 380.4 %reduce-scatter.2.cloned.1.call-start = ((), (), s32[]{:S(2)}) async-start(), calls=%async_computation.9 | async-start | bytes 9191424 | tf_op jit(solution)/shard_map/reduce_scatter | solution.py:1130
  88.2 11.0 %copy-start.7 = (bf16[1024,1024]{1,0:T(8,128)(2,1)}, bf16[1024,1024]{1,0:T(8,128)(2,1)S(1)}, u32[]{:S(2)}) copy-start(bf16[1024,1024]{1,0:T(8,128)(2,1)S(1)} %get-tuple-element.218.res) | copy-start | bytes 6291460
  88.3 14.9 %copy-start.34 = (f32[4]{0:T(128)S(1)}, f32[4]{0:T(128)}, u32[]{:S(2)}) copy-start(f32[4]{0:T(128)} %param.37) | copy-start | bytes 52
  88.3 14.9 %copy-start.35 = (f32[4]{0:T(128)S(1)}, f32[4]{0:T(128)}, u32[]{:S(2)}) copy-start(f32[4]{0:T(128)} %param.36) | copy-start | bytes 52
  99.2 5.7 collective-permute-start
  287.2 34.7 %collective-permute-start.1 = (bf16[4,128,128]{2,1,0:T(8,128)(2,1)S(1)}, bf16[4,128,128]{2,1,0:T(8,128)(2,1)S(1)}, u32[]{:S(2)}, u32[]{:S(2)}) collective-permute-start(bf16[4,128,128]{2,1,0:T(8,128)(2,1)S(1)} %bitcast.104), channel_id=1, source_target_pairs={{4,0},{8,4},{12,8},{16,12},{20,16},{24,20},{28,24},{5,1},{9,5},{13... | collective-permute-start | bytes 393224 | tf_op jit(solution)/shard_map/ppermute | solution.py:742
  309.2 331.9 %collective-permute-start.5 = (bf16[256]{0:T(256)(128)(2,1)}, bf16[256]{0:T(256)(128)(2,1)}, u32[]{:S(2)}, u32[]{:S(2)}) collective-permute-start(bf16[256]{0:T(256)(128)(2,1)} %reduce_sum.69), channel_id=1, source_target_pairs={{0,2},{2,0},{1,3},{3,1},{4,6},{6,4},{5,7},{7,5},{8,10},{10,8},{9,1... | collective-permute-start | bytes 1544 | tf_op jit(solution)/shard_map/ppermute | solution.py:874
  309.2 74.6 %collective-permute-start.2 = (bf16[1024,1024]{1,0:T(8,128)(2,1)}, bf16[1024,1024]{1,0:T(8,128)(2,1)S(1)}, u32[]{:S(2)}, u32[]{:S(2)}) collective-permute-start(bf16[1024,1024]{1,0:T(8,128)(2,1)} %get-tuple-element.83), channel_id=1, source_target_pairs={{0,2},{2,0},{1,3},{3,1},{4,6},{6,4},{5,7},{7,5},{8,10},{10,8},{9,1... | collective-permute-start | bytes 6291464 | tf_op jit(solution)/shard_map/ppermute | solution.py:874
  322.0 61.8 %copy-start.29 = (s32[1024]{0:T(1024)S(1)}, s32[1024]{0:T(1024)}, u32[]{:S(2)}) copy-start(s32[1024]{0:T(1024)} %copy-done.28) | copy-start | bytes 12292
  322.0 61.8 %copy-start.38 = (bf16[1024,1024]{1,0:T(8,128)(2,1)S(1)}, bf16[1024,1024]{1,0:T(8,128)(2,1)}, u32[]{:S(2)}) copy-start(bf16[1024,1024]{1,0:T(8,128)(2,1)} %get-tuple-element.83) | copy-start | bytes 6291460
  322.0 61.8 %copy-start.41 = (f32[1024,1024]{1,0:T(8,128)S(1)}, f32[1024,1024]{1,0:T(8,128)}, u32[]{:S(2)}) copy-start(f32[1024,1024]{1,0:T(8,128)} %get-tuple-element.82) | copy-start | bytes 12582916
  387.9 76.1 %all-to-all-start.2 = ((bf16[8,128,1024]{2,1,0:T(8,128)(2,1)}), bf16[8,128,1024]{2,1,0:T(8,128)(2,1)}, u32[]{:S(2)}, u32[]{:S(2)}) async-start(bf16[8,128,1024]{2,1,0:T(8,128)(2,1)} %bitcast.32), calls=%async_computation.3 | async-start | bytes 4194304 | tf_op jit(solution)/shard_map/all_to_all | solution.py:1192
  399.1 295.6 %all-gather.16.cloned.1.call-start = ((), (), s32[]{:S(2)}) async-start(), calls=%async_computation.10 | async-start | bytes 4866048 | tf_op jit(solution)/shard_map/all_gather | solution.py:1292
  399.3 66.2 %copy-start.9 = (bf16[1024,1024]{1,0:T(8,128)(2,1)S(1)}, bf16[1024,1024]{1,0:T(8,128)(2,1)}, u32[]{:S(2)}) copy-start(bf16[1024,1024]{1,0:T(8,128)(2,1)} %copy-done.7) | copy-start | bytes 6291460
  449.9 6.4 collective-permute-start.3
  485.5 143.1 %collective-permute-start.4 = (bf16[1024,1024]{1,0:T(8,128)(2,1)S(1)}, bf16[1024,1024]{1,0:T(8,128)(2,1)S(1)}, u32[]{:S(2)}, u32[]{:S(2)}) collective-permute-start(bf16[1024,1024]{1,0:T(8,128)(2,1)S(1)} %fusion.54), channel_id=1, source_target_pairs={{0,2},{2,0},{1,3},{3,1},{4,6},{6,4},{5,7},{7,5},{8,10},{10,8},{9,1... | collective-permute-start | bytes 6291464 | tf_op jit(solution)/shard_map/ppermute | solution.py:874
  636.3 54.6 %all-to-all-start.3 = ((bf16[8,128,1024]{2,1,0:T(8,128)(2,1)}), bf16[8,128,1024]{2,1,0:T(8,128)(2,1)S(1)}, u32[]{:S(2)}, u32[]{:S(2)}) async-start(bf16[8,128,1024]{2,1,0:T(8,128)(2,1)} %bitcast.107), calls=%async_computation.4 | async-start | bytes 4194304 | tf_op jit(solution)/shard_map/all_to_all | solution.py:1192
  641.8 5.6 collective-permute-start.6
  647.5 8.3 %collective-permute-start.7 = (f32[5256]{0:T(1024)S(1)}, f32[5256]{0:T(1024)S(1)}, u32[]{:S(2)}, u32[]{:S(2)}) collective-permute-start(f32[5256]{0:T(1024)S(1)} %add_reduce_fusion), channel_id=1, source_target_pairs={{0,4},{4,0},{8,12},{12,8},{16,20},{20,16},{24,28},{28,24},{1,5},{5... | collective-permute-start | bytes 63080 | tf_op jit(solution)/shard_map/ppermute | solution.py:879
  651.2 32.2 %copy-start.12 = (bf16[512,1024]{1,0:T(8,128)(2,1)S(1)}, bf16[512,1024]{1,0:T(8,128)(2,1)}, u32[]{:S(2)}) copy-start(bf16[512,1024]{1,0:T(8,128)(2,1)} %get-tuple-element.102) | copy-start | bytes 3145732
  655.9 16.8 %collective-permute-start.8 = (f32[5256]{0:T(1024)S(1)}, f32[5256]{0:T(1024)S(1)}, u32[]{:S(2)}, u32[]{:S(2)}) collective-permute-start(f32[5256]{0:T(1024)S(1)} %add.123), channel_id=1, source_target_pairs={{0,8},{4,12},{8,0},{12,4},{16,24},{20,28},{24,16},{28,20},{1,9},{5... | collective-permute-start | bytes 63080 | tf_op jit(solution)/shard_map/ppermute | solution.py:879
  672.7 14.7 %collective-permute-start.9 = (f32[5256]{0:T(1024)S(1)}, f32[5256]{0:T(1024)S(1)}, u32[]{:S(2)}, u32[]{:S(2)}) collective-permute-start(f32[5256]{0:T(1024)S(1)} %add.124), channel_id=1, source_target_pairs={{0,16},{4,20},{8,24},{12,28},{16,0},{20,4},{24,8},{28,12},{1,17},{... | collective-permute-start | bytes 63080 | tf_op jit(solution)/shard_map/ppermute | solution.py:879
  (33 other events, 156.3 us)
Sparse Core Ops, SparseCore 0:
  15.8 19.8 all-gather.7
  37.2 11.7 all-gather.9
  50.6 12.8 all-gather.13
  65.5 17.1 all-gather.11
  285.1 171.8 reduce-scatter.1
  464.1 102.7 all-gather.15

commit v4 on v3

--- a/solution.py
+++ b/solution.py
@@ -246,9 +246,11 @@
 def block_kernel(
     heads, dk, dv, tiles,
     local, qa, entering, zgate, gain, wout, res, e_now, gain_two, wwide, wdown, e_late,
+    local_late, qa_late, zgate_late, qeff, wkey, ktail, cum,
     y_out, down_out, r_out, dr_out, er_out, gain_grad, grads_out,
+    dz_out, do_out, out_gain_grad, first,
     part_own, part_in, dn_own, dn_in, r_keep, hid_out, dwide_out, grads, stage, gain_sum,
-    part_sems, dn_sems, out_sems,
+    state, out_gain_sum, part_sems, dn_sems, out_sems,
 ):
     step = pl.program_id(0)
     hidden = wdown.shape[0]
@@ -331,6 +333,11 @@
         dr_out[...] = dr
         er_out[...] = dr.astype(bf16)
         gain_grad[...] = gain_sum[...]
+        back_step(
+            heads, dk, dv, step == 2,
+            er_out, local_late, qa_late, entering, zgate_late, gain, wout, qeff, wkey, ktail, cum,
+            dz_out, do_out, out_gain_grad, first, state, out_gain_sum,
+        )
 
     @pl.when(step == tiles + 1)
     def _():
@@ -355,7 +362,8 @@
 
 
 def block_rest(
-    local, qa, entering, proj, gain, wout, res, e, gain_two, wwide, wdown, heads, dk, dv, collective_id
+    local, qa, entering, proj, gain, wout, res, e, gain_two, wwide, wdown, qeff, wkey, ktail, cum,
+    heads, dk, dv, collective_id,
 ):
     rows, model = res.shape
     size = CHUNK
@@ -364,7 +372,7 @@
     z_at = (2 * heads * dk + heads * dv) // (heads * dv)
 
     def rowwise(cols, lag, at=0):
-        return pl.BlockSpec((size, cols), lambda n: (jnp.clip(n - lag, 0, tiles - 1), at))
+        return pl.BlockSpec((size, cols), lambda n: (tiles - 1 - jnp.clip(n - lag, 0, tiles - 1), at))
 
     def kept(shape):
         return pl.BlockSpec(shape, lambda n: (0,) * len(shape), pipeline_mode=pl.Buffered(1))
@@ -377,6 +385,10 @@
         ((rows, model), bf16, rowwise(model, 2)),
         ((8, model), f32, whole((8, model))),
         ((6 * hidden, model // 2), bf16, pl.BlockSpec(memory_space=pl.ANY)),
+        ((rows, heads * dv), bf16, rowwise(heads * dv, 2)),
+        ((rows, heads * dv), bf16, rowwise(heads * dv, 2)),
+        ((8, dv), f32, whole((8, dv))),
+        ((heads, dk, dv), bf16, whole((heads, dk, dv))),
     ]
     return pl.pallas_call(
         functools.partial(block_kernel, heads, dk, dv, tiles),
@@ -394,6 +406,13 @@
             kept(wwide.shape),
             kept(wdown.shape),
             rowwise(model, 2),
+            rowwise(heads * dv, 2),
+            rowwise(heads * dk, 2),
+            rowwise(heads * dv, 2, z_at),
+            rowwise(heads * dk, 2),
+            rowwise(heads * dk, 2),
+            rowwise(heads * dk, 2),
+            rowwise(LANES, 2),
         ],
         out_specs=[spec for _, _, spec in outs],
         out_shape=[jax.ShapeDtypeStruct(shape, kind) for shape, kind, _ in outs],
@@ -405,6 +424,8 @@
             pltpu.VMEM((3 * hidden, model), f32),
             pltpu.VMEM((2, hidden // 2, model // 2), bf16),
             pltpu.VMEM((8, model), f32),
+            pltpu.VMEM((heads, dk, dv), f32),
+            pltpu.VMEM((8, dv), f32),
             pltpu.SemaphoreType.DMA((2, tiles)),
             pltpu.SemaphoreType.DMA((2, tiles)),
             pltpu.SemaphoreType.DMA((2,)),
@@ -412,24 +433,26 @@
         compiler_params=pltpu.CompilerParams(
             collective_id=collective_id,
             has_side_effects=True,
-            vmem_limit_bytes=60 * MIB,
+            vmem_limit_bytes=61 * MIB,
             dimension_semantics=("arbitrary",),
         ),
         cost_estimate=pl.CostEstimate(
             flops=100 * 10**9, bytes_accessed=rows * model * 40, transcendentals=rows * hidden
         ),
-    )(local, qa, entering, proj, gain, wout, res, e, gain_two, wwide, wdown, e)
-
-
-def back_kernel(
-    heads, dk, dv,
+    )(
+        local, qa, entering, proj, gain, wout, res, e, gain_two, wwide, wdown, e,
+        local, qa, proj, qeff, wkey, ktail, cum,
+    )
+
+
+def back_step(
+    heads, dk, dv, begins,
     er, local, qa, entering, zgate, gain, wout, qeff, wkey, ktail, cum,
     dz_out, do_out, gain_out, first, state, gain_sum,
 ):
-    step = pl.program_id(0)
     size = er.shape[0]
 
-    @pl.when(step == 0)
+    @pl.when(begins)
     def _():
         state[...] = jnp.zeros_like(state)
         gain_sum[...] = jnp.zeros_like(gain_sum)
@@ -463,49 +486,6 @@
         state[h] = now
         first[h] = now.astype(bf16)
     gain_out[...] = gain_sum[...]
-
-
-def delta_back(er, local, qa, entering, proj, gain, wout, qeff, wkey, ktail, cum, heads, dk, dv):
-    rows, model = er.shape
-    size = CHUNK
-    steps = rows // size
-    z_at = (2 * heads * dk + heads * dv) // (heads * dv)
-
-    def rowwise(cols, at=0):
-        return pl.BlockSpec((size, cols), lambda n: (steps - 1 - n, at))
-
-    outs = [
-        ((rows, heads * dv), bf16, rowwise(heads * dv)),
-        ((rows, heads * dv), bf16, rowwise(heads * dv)),
-        ((8, dv), f32, whole((8, dv))),
-        ((heads, dk, dv), bf16, whole((heads, dk, dv))),
-    ]
-    return pl.pallas_call(
-        functools.partial(back_kernel, heads, dk, dv),
-        grid=(steps,),
-        in_specs=[
-            rowwise(model),
-            rowwise(heads * dv),
-            rowwise(heads * dk),
-            whole((heads, dk, dv)),
-            rowwise(heads * dv, z_at),
-            whole((8, dv)),
-            whole(wout.shape),
-            rowwise(heads * dk),
-            rowwise(heads * dk),
-            rowwise(heads * dk),
-            rowwise(LANES),
-        ],
-        out_specs=[spec for _, _, spec in outs],
-        out_shape=[jax.ShapeDtypeStruct(shape, kind) for shape, kind, _ in outs],
-        scratch_shapes=[pltpu.VMEM((heads, dk, dv), f32), pltpu.VMEM((8, dv), f32)],
-        compiler_params=vmem(),
-        cost_estimate=pl.CostEstimate(
-            flops=20 * rows * heads * dv * model,
-            bytes_accessed=rows * heads * dv * 18,
-            transcendentals=rows * heads * dv,
-        ),
-    )(er, local, qa, entering, proj, gain, wout, qeff, wkey, ktail, cum)
 
 
 def grad_kernel(
@@ -744,7 +724,7 @@
 
 def chain_kernel(forward, levels, *refs):
     if forward:
-        own, out, mats, runs, arrived, send_sem, recv_sem = refs
+        own, out, mats, runs, arrived, kept, send_sem, recv_sem, mat_sems = refs
     else:
         own, maps, out, runs, arrived, send_sem, recv_sem = refs
     heads, dk = own.shape[:2]
@@ -754,7 +734,8 @@
     place = me if forward else count - 1 - me
     way = 1 if forward else -1
     distances = [2**j for j in range(levels)] + [1]
-    reaches = sorted(set(distances))
+    behind = [2 ** (j + 1) - 1 for j in range(levels - 1)] if forward else []
+    reaches = sorted(set(distances + behind))
     barrier = pltpu.get_barrier_semaphore()
     known = jnp.int32(0)
     for d in reaches:
@@ -788,6 +769,16 @@
         def _():
             copy(j, h).start()
 
+    def mat_copy(j, h):
+        return pltpu.make_async_remote_copy(
+            src_ref=kept.at[j, h],
+            dst_ref=kept.at[levels + j, h],
+            send_sem=mat_sems.at[0, j, h],
+            recv_sem=mat_sems.at[1, j, h],
+            device_id={"ctx": me - behind[j]},
+            device_id_type=pl.DeviceIdType.MESH,
+        )
+
     for h in range(heads):
         send(0, h)
     for j in range(levels + 1):
@@ -812,7 +803,11 @@
                 runs[j, h, :, 0:dv] = (run[:, 0:dv].astype(f32) + joined[:, 0:dv]).astype(bf16)
                 if j < levels - 1:
                     runs[j, h, :, dv : dv + dk] = joined[:, dv:].astype(bf16)
-                    mats[j, h] = joined[:, dv:].astype(bf16)
+                    kept[j, h] = joined[:, dv:].astype(bf16)
+
+                    @pl.when(me >= behind[j])
+                    def _(j=j, h=h):
+                        mat_copy(j, h).start()
             else:
                 joined = mm_tn(maps[j, h], arrived[j, h])
                 runs[j, h] = (run.astype(f32) + joined).astype(bf16)
@@ -823,13 +818,31 @@
             @pl.when(place + distances[j] < count)
             def _(j=j, h=h):
                 copy(j, h).wait_send()
+    if forward:
+        for h in range(heads):
+            mats[0, h] = own[h, :, dv:]
+        for j, d in enumerate(behind):
+            for h in range(heads):
+
+                @pl.when(me + d < count)
+                def _(j=j, h=h):
+                    mat_copy(j, h).wait_recv()
+                    mats[j + 1, h] = kept[levels + j, h]
+
+                @pl.when(me + d >= count)
+                def _(j=j, h=h):
+                    mats[j + 1, h] = jnp.zeros(mats.shape[2:], bf16)
+
+                @pl.when(me >= d)
+                def _(j=j, h=h):
+                    mat_copy(j, h).wait_send()
 
 
 def chained(own, maps, dv, levels, collective_id):
     heads, dk, width = own.shape
     forward = maps is None
     spec = pl.BlockSpec(memory_space=pltpu.VMEM)
-    shapes = [(heads, dk, dv)] + ([(max(levels - 1, 1), heads, dk, dk)] if forward else [])
+    shapes = [(heads, dk, dv)] + ([(levels, heads, dk, dk)] if forward else [])
     return pl.pallas_call(
         functools.partial(chain_kernel, forward, levels),
         in_specs=[spec] * (1 if forward else 2),
@@ -838,9 +851,13 @@
         scratch_shapes=[
             pltpu.VMEM((levels, heads, dk, width), bf16),
             pltpu.VMEM((levels + 1, heads, dk, width), bf16),
+        ]
+        + ([pltpu.VMEM((2 * levels, heads, dk, dk), bf16)] if forward else [])
+        + [
             pltpu.SemaphoreType.DMA((levels + 1, heads)),
             pltpu.SemaphoreType.DMA((levels + 1, heads)),
-        ],
+        ]
+        + ([pltpu.SemaphoreType.DMA((2, levels, heads))] if forward else []),
         compiler_params=pltpu.CompilerParams(
             collective_id=collective_id, has_side_effects=True, vmem_limit_bytes=24 * MIB
         ),
@@ -857,9 +874,7 @@
 
 def entering_state(own, dv, reach):
     levels = levels_of(reach)
-    entering, mats = chained(own, None, dv, levels, 3)
-    ahead = [own[:, :, dv:]] + [shifted(mats[j - 1], "ctx", 1 - 2**j) for j in range(1, levels)]
-    return entering, jnp.stack(ahead)
+    return chained(own, None, dv, levels, 3)
 
 
 def leaving_grad(own, ahead):
@@ -867,11 +882,19 @@
 
 
 def summed_over_tp(part):
+    return added(part, over_tp(part))
+
+
+def over_tp(part):
     count = lax.axis_size("tp")
+    routes = [[(i, (i + d) % count) for i in range(count)] for d in range(1, count)]
+    return [lax.ppermute(part, "tp", route) for route in routes]
+
+
+def added(part, others):
     total = part.astype(f32)
-    for d in range(1, count):
-        route = [(i, (i + d) % count) for i in range(count)]
-        total = total + lax.ppermute(part, "tp", route).astype(f32)
+    for other in others:
+        total = total + other.astype(f32)
     return total
 
 
@@ -939,7 +962,7 @@
             def body(j, carry):
                 r = rows(start + j * step, step)
                 total = one[i][r, at].astype(f32) + two[i][r, at].astype(f32)
-                target[i][r, at] = total.astype(bf16)
+                target[i][r, at] = total.astype(target[i].dtype)
                 return carry
 
             lax.fori_loop(0, n // step, body, 0)
@@ -1110,8 +1133,8 @@
         functools.partial(sum_kernel, plan),
         in_specs=[pl.BlockSpec(memory_space=pl.ANY)] * len(grads),
         out_specs=[pl.BlockSpec(memory_space=pl.ANY)] * len(grads),
-        out_shape=[jax.ShapeDtypeStruct(shape, bf16) for shape in shapes],
-        scratch_shapes=[pltpu.VMEM(shape, bf16) for shape in shapes] * 6
+        out_shape=[jax.ShapeDtypeStruct(shape, g.dtype) for shape, g in zip(shapes, grads)],
+        scratch_shapes=[pltpu.VMEM(shape, g.dtype) for shape, g in zip(shapes, grads)] * 6
         + [
             pltpu.SemaphoreType.DMA((2 * total,)),
             pltpu.SemaphoreType.DMA((total, 7)),
@@ -1128,18 +1151,6 @@
 
 def scattered(grad):
     return lax.psum_scatter(grad, ("fs", "ctx"), scatter_dimension=0, tiled=True)
-
-
-def reduced_little(little):
-    mine = lax.axis_index("fs")
-    give = lax.dynamic_slice_in_dim(little, 1 - mine, 1, 0)
-    keep = lax.dynamic_slice_in_dim(little, mine, 1, 0)
-    total = (keep + swapped(give, "fs", 1))[0]
-    bit = 1
-    while bit < lax.axis_size("ctx"):
-        total = total + swapped(total, "ctx", bit)
-        bit *= 2
-    return total
 
 
 def per_device(
@@ -1191,14 +1202,7 @@
     def exchanged(values):
         return lax.all_to_all(values, "ctx", split_axis=0, concat_axis=0, tiled=True)
 
-    def sent_to_packed(values):
-        return exchanged(moved(gather_send, values))
-
-    def sent_to_given(values):
-        return exchanged(moved(gather_recv, values, True))
-
-    resident = moved(gather_recv, sent_to_packed(tokens[0]))
-
+    sent = moved(gather_send, tokens[0])
     offsets = jnp.cumsum(lengths[0]) - lengths[0]
     positions = me * rows - halo_rows + jnp.arange(rows + 2 * halo_rows, dtype=jnp.int32)
     number = jnp.sum((offsets[None, :] <= positions[:, None]).astype(jnp.int32), axis=1)
@@ -1214,7 +1218,9 @@
 
     pad = jnp.zeros((w_decay.shape[0], LANES - 2 * heads), bf16)
     w_in = jnp.concatenate([w_query, w_key, w_value, w_outgate, w_decay, w_beta, pad], axis=1)
+    sent, w_in = lax.optimization_barrier((sent, w_in))
     w_in = lax.all_gather(w_in, "fs", axis=0, tiled=True)
+    resident = moved(gather_recv, exchanged(sent))
     w_wide = lax.all_gather(jnp.concatenate([w_gate, w_up], axis=1), "fs", axis=0, tiled=True)
     w_down = lax.all_gather(w_down, "fs", axis=0, tiled=True)
     w_output = lax.all_gather(w_output, "fs", axis=0, tiled=True)
@@ -1253,12 +1259,13 @@
     conv, local, qa, states, tinv, uval, wkey, qeff, ktail, cum, last = delta_forward(
         proj, flags, halo, taps, head, heads, dk, dv
     )
-    last, arrived = lax.optimization_barrier((last, sent_to_packed(cotangent[0])))
+    last, arrived = lax.optimization_barrier((last, exchanged(moved(gather_send, cotangent[0]))))
     e = moved(gather_recv, arrived)
     entering, ahead = entering_state(last, dv, reach)
-    y1, down, r, dr, er, mlp_gain_sum, mlp_cat = block_rest(
+    y1, down, r, dr, er, mlp_gain_sum, mlp_cat, dz, do, dgain_out, first = block_rest(
         local, qa, entering, proj, gain_rows, w_output, resident, e,
-        jnp.broadcast_to(gain_two[None, :], (8, model)), w_wide, w_down, heads, dk, dv, 2,
+        jnp.broadcast_to(gain_two[None, :], (8, model)), w_wide, w_down, qeff, wkey, ktail, cum,
+        heads, dk, dv, 2,
     )
     grad_mlp_gain = mlp_gain_sum[0]
 
@@ -1273,23 +1280,13 @@
     half = model // fs
     down_rows = hidden_cols // fs
     mlp_share = scattered(mlp_cat)
-    result = (r + summed_over_tp(down)).astype(bf16)
-
-    dz, do, dgain_out, first = delta_back(
-        er, local, qa, entering, proj, gain_rows, w_output, qeff, wkey, ktail, cum, heads, dk, dv
-    )
+
     leaving = leaving_grad(first, ahead)
-    g_z = outer(n1, dz)
-    g_o = outer(y1, er)
     dproj, dab, tail_rows, head_rows, dtaps, dhead = delta_grad(
         proj, conv, flags, cum, halo, taps, head, do, tinv, uval, wkey, states, entering, leaving,
         heads, dk, dv,
     )
-    dproj, mlp_share, arrived = lax.optimization_barrier(
-        (dproj, mlp_share, sent_to_given(result))
-    )
-    block_out = moved(gather_send, arrived, True)
-    g_mlp_all = lax.all_gather(mlp_share, "ctx", axis=0, tiled=True)
+    dproj, down_other = lax.optimization_barrier((dproj, over_tp(down)))
     next_rows = shifted(head_rows, "ctx", -1)
     extra = jnp.zeros_like(tail_rows)
     for s in range(1, TAPS):
@@ -1298,40 +1295,62 @@
     dproj = lax.dynamic_update_slice(dproj, (tail_rows + extra).astype(bf16), (rows - 8, 0))
     dall = jnp.concatenate([dproj, dz, dab], axis=1)
     dn1 = lax.dot_general(dall, w_in, (((1,), (1,)), ((), ())), preferred_element_type=f32)
-    dn1 = summed_over_tp(dn1.astype(bf16))
+    dn1_own, dz, y1, down_other = lax.optimization_barrier(
+        (dn1.astype(bf16), dz, y1, down_other)
+    )
+    dn1_other = over_tp(dn1_own)
     g_in = outer(n1, jnp.concatenate([dproj, dab], axis=1))
-    g_in, g_z, g_o = reduced([g_in, g_z, g_o], 1, 110)
-    dn1, g_in, g_z, g_o = lax.optimization_barrier((dn1, g_in, g_z, g_o))
-    g_wide = jnp.swapaxes(g_mlp_all[: 2 * hidden_cols], 0, 1)
+    g_z = outer(n1, dz)
+    g_o = outer(y1, er)
+    g_in, mlp_share = lax.optimization_barrier((g_in, mlp_share))
+    g_mlp_all = lax.all_gather(mlp_share, "ctx", axis=0, tiled=True)
+    result = (r + added(down, down_other)).astype(bf16)
+    block_rows = exchanged(moved(gather_recv, result, True))
+    def tap_part(lo, channels):
+        return dtaps[:TAPS, lo : lo + channels].reshape(TAPS, fs, -1).transpose(1, 0, 2).reshape(fs, -1)
+
+    share = jnp.sum(dgain_out, axis=0)
+    rates = jnp.broadcast_to(dhead[:2, :heads].reshape(1, 2 * heads), (fs, 2 * heads))
+    own_mixer_gain = jnp.sum(dn1_own.astype(f32) * x * inv_one, axis=0)
+    little = jnp.concatenate(
+        [
+            tap_part(0, key_cols),
+            tap_part(key_cols, key_cols),
+            tap_part(2 * key_cols, value_cols),
+            halves(own_mixer_gain),
+            halves(grad_mlp_gain),
+            halves(share),
+            rates,
+        ],
+        axis=1,
+    )
+    little_rows = -(-little.shape[1] // (64 * LANES)) * 64
+    little = jnp.pad(little, ((0, 0), (0, little_rows * LANES - little.shape[1])))
+    little = little.reshape(fs * little_rows, LANES)
+    little, g_in, g_z, g_o = reduced([little, g_in, g_z, g_o], 1, 110)
+    dn1_other, block_rows, little, g_in, g_z, g_o = lax.optimization_barrier(
+        (dn1_other, block_rows, little, g_in, g_z, g_o)
+    )
+    dn1 = added(dn1_own, dn1_other)
+    little = little.reshape(-1)
+    unit = jnp.eye(hidden_cols, dtype=bf16)
+    g_gate, g_up = (
+        lax.dot_general(
+            g_mlp_all[lo : lo + hidden_cols], unit, (((0,), (0,)), ((), ())),
+            preferred_element_type=f32,
+        )
+        for lo in (0, hidden_cols)
+    )
     g_down = g_mlp_all[2 * hidden_cols :].reshape(fs, down_rows, half)
     g_down = jnp.concatenate([g_down[j] for j in range(fs)], axis=1)
-    grad_mixer_gain = jnp.sum(dn1 * x * inv_one, axis=0)
     scaled = gain_one * dn1
     grad_in = (
         dr
         + inv_one * scaled
         - x * (inv_one * inv_one * inv_one * jnp.mean(scaled * x, axis=-1, keepdims=True))
     ).astype(bf16)
-    grad_tokens = moved(gather_send, sent_to_given(grad_in), True)
-
-    def tap_part(lo, channels):
-        return dtaps[:TAPS, lo : lo + channels].reshape(TAPS, fs, -1).transpose(1, 0, 2).reshape(fs, -1)
-
-    share = summed_over_tp(jnp.sum(dgain_out, axis=0).astype(bf16))
-    rates = jnp.broadcast_to(dhead[:2, :heads].reshape(1, 2 * heads), (fs, 2 * heads))
-    little = jnp.concatenate(
-        [
-            tap_part(0, key_cols),
-            tap_part(key_cols, key_cols),
-            tap_part(2 * key_cols, value_cols),
-            halves(grad_mixer_gain),
-            halves(grad_mlp_gain),
-            halves(share),
-            rates,
-        ],
-        axis=1,
-    )
-    little = reduced_little(little)
+    token_rows = exchanged(moved(gather_recv, grad_in, True))
+
     taken, at = [], 0
     for channels in (conv_query.shape[0], conv_key.shape[0], conv_value.shape[0]):
         taken.append(little[at : at + TAPS * channels].reshape(TAPS, channels).T)
@@ -1340,13 +1359,14 @@
         taken.append(little[at : at + size])
         at += size
     g_cq, g_ck, g_cv, g_mixer, g_mlp, g_out_gain, g_log, g_bias = taken
+    ends_tp = summed_over_tp(jnp.concatenate([g_mixer, g_out_gain]))
+    g_mixer, g_out_gain = ends_tp[: g_mixer.shape[0]], ends_tp[g_mixer.shape[0] :]
     ends = [key_cols, 2 * key_cols, width, width + heads]
     g_query, g_key, g_value, g_decay, g_beta = (
         g_in[:, lo:hi].astype(f32) for lo, hi in zip([0] + ends, ends + [ends[-1] + heads])
     )
-    return (
-        block_out[None],
-        grad_tokens[None],
+    outs = (
+        moved(gather_send, block_rows, True)[None],
         g_mixer,
         g_query,
         g_key,
@@ -1362,10 +1382,13 @@
         g_out_gain,
         g_o.astype(f32),
         g_mlp,
-        g_wide[:, :hidden_cols].astype(f32),
-        g_wide[:, hidden_cols:].astype(f32),
+        g_gate,
+        g_up,
         g_down.astype(f32),
     )
+    token_rows, outs = lax.optimization_barrier((token_rows, outs))
+    grad_tokens = moved(gather_send, token_rows, True)[None]
+    return (outs[0], grad_tokens) + outs[1:]
 
 
 def solution(mesh):

time: 725 us -> 685 us (0.945)
  starting transfers between devices: 47.5 us -> 29.3 us
  matrix products: 78.5 us -> 92.7 us
  waiting for transfers between devices: 64.7 us -> 51.7 us
  local copies, waits for them, and re-layouts: 40.8 us -> 30.4 us
  Pallas kernels: 440 us -> 432 us
    pallas_call x1, Pallas kernels: 141 us -> 170 us  [reduced(): pl.pallas_call(functools.partial(sum_kernel, plan), in_specs=[pl.BlockSpe...]
    pallas_call x2, Pallas kernels: 91.1 us -> 68.4 us  [chained(): pl.pallas_call(functools.partial(chain_kernel, forward, levels), in_specs...]
    ppermute x7 -> x3, waiting for transfers between devices: 21 us -> 0.01 us  [over_tp(): return [lax.ppermute(part, 'tp', route) for route in routes]]
    pallas_call x1 -> x0, Pallas kernels: 17.7 us -> none  [delta_back(): pl.pallas_call(functools.partial(back_kernel, heads, dk, dv), grid=(steps...]
    ppermute x7 -> x3, starting transfers between devices: 11.9 us -> 2.33 us  [over_tp(): return [lax.ppermute(part, 'tp', route) for route in routes]]
    unnamed x120 -> x117, local copies, waits for them, and re-layouts: 17.6 us -> 8.38 us
    all_to_all x4, waiting for transfers between devices: 36.3 us -> 45.2 us  [exchanged(): lax.all_to_all(values, 'ctx', split_axis=0, concat_axis=0, tiled=True)]
    dot_general x0 -> x2, matrix products: none -> 8.11 us  [per_device(): lax.dot_general(g_mlp_all[lo:lo + hidden_cols], unit, (((0,), (0,)), ((),...]
  transfers between devices with their start and end apart: 20 -> 15, of which waited for: 7 -> 4; matrix products, arithmetic and copies ran while one was open for 16% -> 18% of each run, Pallas kernels for 47% -> 48%
where the time goes in v4:
time: 685 us; the launch traced here: 678 us
  Pallas kernels  432 us (63%)
  matrix products  92.7 us (14%)
  waiting for transfers between devices  51.7 us (8%)
  local copies, waits for them, and re-layouts  30.4 us (4%)
  starting transfers between devices  29.3 us (4%)
  other arithmetic  24.9 us (4%)
  between operations  15.1 us (2%)
    pallas_call x1, Pallas kernels, reduced(): pl.pallas_call(functools.partial(sum_kernel, plan), in_specs=[pl.BlockSpe...  170 us
    pallas_call x1, Pallas kernels, block_rest(): pl.pallas_call(functools.partial(block_kernel, heads, dk, dv, tiles), gri...  110 us
    pallas_call x2, Pallas kernels, chained(): pl.pallas_call(functools.partial(chain_kernel, forward, levels), in_specs...  68.4 us
    pallas_call x1, Pallas kernels, delta_grad(): pl.pallas_call(functools.partial(grad_kernel, heads, dk, dv), grid=(steps...  48.5 us
    all_to_all x4, waiting for transfers between devices, exchanged(): lax.all_to_all(values, 'ctx', split_axis=0, concat_axis=0, tiled=True)  45.2 us
    dot_general x8, matrix products, moved(): lax.dot_general(maps, values, (((0 if transposed else 1,), (0,)), ((), ()...  43.9 us
    pallas_call x1, Pallas kernels, delta_forward(): pl.pallas_call(functools.partial(forward_kernel, heads, dk, dv), grid=(st...  35.4 us
    all_to_all x4, starting transfers between devices, exchanged(): lax.all_to_all(values, 'ctx', split_axis=0, concat_axis=0, tiled=True)  21.1 us
  transfers between devices with their start and end apart: 15, of which 4 were waited for; matrix products, arithmetic and copies ran while one was open for 18% of the time, Pallas kernels for 48%

profile of v4, /device:TPU:0, one launch (start us, length us, event | category | flops | bytes accessed | tf_op | source)
XLA Modules:
  0.0 677.6 jit_solution(17406428885371220295)
XLA Ops:
  12.5 3.7 fusion.51
  16.2 6.4 concatenate.36
  24.2 7.3 %all-to-all-start = ((bf16[8,128,1024]{2,1,0:T(8,128)(2,1)}), bf16[8,128,1024]{2,1,0:T(8,128)(2,1)S(1)}, u32[]{:S(2)}, u32[]{:S(2)}) async-start(bf16[8,128,1024]{2,1,0:T(8,128)(2,1)} %bitcast.4), calls=%async_computation | async-start | bytes 4194304 | tf_op jit(solution)/shard_map/all_to_all | solution.py:1203
  31.5 3.4 pad_maximum_fusion
  46.5 5.3 fusion.54
  51.8 27.9 %all-to-all-done = bf16[8,128,1024]{2,1,0:T(8,128)(2,1)S(1)} async-done(((bf16[8,128,1024]{2,1,0:T(8,128)(2,1)}), bf16[8,128,1024]{2,1,0:T(8,128)(2,1)S(1)}, u32[]{:S(2)}, u32[]{:S(2)}) %all-to-all-start) | async-done | bytes 2097184 | tf_op jit(solution)/shard_map/all_to_all | solution.py:1203
  79.7 4.4 all-to-all-start.1
  84.4 4.3 fusion.12
  89.3 10.3 %fusion.88.proj.ab.zgate.zgate_late = f32[1024,3200]{1,0:T(8,128)S(1)} fusion(bf16[1024,3200]{1,0:T(8,128)(2,1)} %all-gather.8.cloned.1.call-done, bf16[1024,1024]{1,0:T(8,128)(2,1)S(1)} %get-tuple-element.274.res, f32[1024]{0:T(1024)S(1)} %bitcast.125, f32[1024]{0:T(1024)S(1)} %add_rsqrt_fusion), kind=kOutput, calls=%fused_computation.158 | convolution fusion | flops 6715080704 | bytes 21766144 | tf_op jit(solution)/shard_map/dot_general | solution.py:1257
  99.6 4.0 collective-permute-start
  106.0 35.4 %shard_map.365 = (f32[1024,2048]{1,0:T(8,128)}, f32[1024,1024]{1,0:T(8,128)}, bf16[1024,512]{1,0:T(8,128)(2,1)}, bf16[8,4,128,384]{3,2,1,0:T(8,128)(2,1)}, bf16[...) custom-call(f32[1024,3200]{1,0:T(8,128)} %copy-done.38, ...), custom_call_target="tpu_custom_call" | custom-call | flops 13421772800 | bytes 29360128 | tf_op jit(solution)/shard_map/pallas_call | solution.py:220
  141.4 5.3 fusion.46.e_now.e_late
  146.7 32.3 %shard_map.366 = (bf16[4,128,256]{2,1,0:T(8,128)(2,1)S(1)}, bf16[2,4,128,128]{3,2,1,0:T(8,128)(2,1)S(1)}) custom-call(bf16[4,128,384]{2,1,0:T(8,128)(2,1)S(1)} %copy-done.2), custom_call_target="tpu_custom_call" | custom-call | flops 24999999488 | bytes 3145728 | tf_op jit(solution)/shard_map/pallas_call | solution.py:846
  181.0 109.8 %shard_map.367 = (bf16[1024,1024]{1,0:T(8,128)(2,1)}, bf16[1024,1024]{1,0:T(8,128)(2,1)}, f32[1024,1024]{1,0:T(8,128)}, f32[1024,1024]{1,0:T(8,128)}, bf16[1024,...) custom-call(f32[1024,1024]{1,0:T(8,128)} %get-tuple-element.94.local, ...), custom_call_target="tpu_custom_call" | custom-call | flops 99999997952 | bytes 41943040 | tf_op jit(solution)/shard_map/pallas_call | solution.py:393
  291.8 36.1 %shard_map.368.leaving = bf16[4,128,256]{2,1,0:T(8,128)(2,1)S(1)} custom-call(bf16[4,128,256]{2,1,0:T(8,128)(2,1)S(1)} %copy-done.3, bf16[2,4,128,128]{3,2,1,0:T(8,128)(2,1)S(1)} %get-tuple-element.111.refs_1_), custom_call_target="tpu_custom_call" | custom-call | flops 24999999488 | bytes 2097152 | tf_op jit(solution)/shard_map/pallas_call | solution.py:846
  328.7 48.5 %shard_map.369 = (bf16[1024,2048]{1,0:T(8,128)(2,1)}, bf16[1024,128]{1,0:T(8,128)(2,1)}, f32[8,2048]{1,0:T(8,128)}, f32[8,2048]{1,0:T(8,128)}, f32[8,2048]{1,0:T(8,128)}, /*index=5*/f32[8,128]{1,0:T(8,128)}) custom-call(f32[1024,3200]{1,0:T(8,128)} %copy-done.38, f32[1024,2048]{1,0:T(8,128)} %get-tuple-element.105.conv, f32[1024,3200]{1,0:T(8,128)} %copy-done.38, ...), custom_call_target="tpu_custom_call" | custom-call | flops 53687091200 | bytes 33554432 | tf_op jit(solution)/shard_map/pallas_call | solution.py:679
  381.6 4.2 collective-permute-done.2
  387.5 12.5 %fusion.57 = bf16[1024,1024]{1,0:T(8,128)(2,1)} fusion(bf16[1024,3200]{1,0:T(8,128)(2,1)} %all-gather.8.cloned.1.call-done, bf16[1024,128]{1,0:T(8,128)(2,1)} %get-tuple-element.118, bf16[1024,1024]{1,0:T(8,128)(2,1)} %get-tuple-element.130, bf16[1024,2048]{1,0:T(8,128)(2,1)} %fusion.69), kind=kOutput, calls=%fused_computation.67 | convolution fusion | flops 6731595776 | bytes 15204352 | tf_op jit(solution)/shard_map/dot_general | solution.py:1297
  403.6 7.4 %fusion.47 = bf16[1024,1024]{1,0:T(8,128)(2,1)} fusion(f32[1024,1024]{1,0:T(8,128)} %get-tuple-element.122, bf16[1024,1024]{1,0:T(8,128)(2,1)} %collective-permute-done.1, bf16[1024,1024]{1,0:T(8,128)(2,1)} %get-tuple-element.113, s32[1024]{0:T(1024)S(1)} %copy-done.29), kind=kOutput, calls=%fused_computation.63 | convolution fusion | flops 2154823680 | bytes 10489856 | tf_op jit(solution)/shard_map/dot_general | solution.py:1198
  411.0 4.6 all-to-all-start.2
  416.4 6.1 convolution_convert_fusion.1.refs_3_
  422.5 4.0 convolution_convert_fusion.2.refs_2_
  426.5 7.3 %convolution_convert_fusion.refs_1_ = bf16[1024,2176]{1,0:T(8,128)(2,1)} fusion(bf16[1024,128]{1,0:T(8,128)(2,1)S(1)} %copy-done.43, bf16[1024,2048]{1,0:T(8,128)(2,1)S(1)} %copy-done.39, bf16[1024,1024]{1,0:T(8,128)(2,1)S(1)} %copy-done.7, f32[1024]{0:T(1024)S(1)} %bitcast.127, f32[1024]{0:T(1024)S(1)} %copy-done.23), kind=kOutput, calls=%fused_computation.14 | convolution fusion | flops 4578738176 | bytes 11018240 | tf_op jit(solution)/shard_map/dot_general | solution.py:1273
  433.8 169.6 %shard_map.370 = (f32[64,128]{1,0:T(8,128)}, bf16[512,2176]{1,0:T(8,128)(2,1)}, bf16[512,1024]{1,0:T(8,128)(2,1)}, bf16[512,1024]{1,0:T(8,128)(2,1)}) custom-call(f32[128,128]{1,0:T(8,128)} %reshape.269.refs_0_, bf16[1024,2176]{1,0:T(8,128)(2,1)} %convolution_convert_fusion.refs_1_, bf16[1024,1024]{1,0:T(8,128)(2,1)} %convolution_convert_fusion.2.refs_2_, ...), custom_call_target="tpu_custom_call" | custom-call | flops 109999996928 | bytes 17367040 | tf_op jit(solution)/shard_map/pallas_call | solution.py:1132
  603.5 3.4 fusion.17
  606.9 7.0 %fusion.48 = bf16[1024,1024]{1,0:T(8,128)(2,1)} fusion(bf16[1024,1024]{1,0:T(8,128)(2,1)S(1)} %copy-done.7, f32[1024,1024]{1,0:T(8,128)S(1)} %copy-done.41, bf16[1024,1024]{1,0:T(8,128)(2,1)} %collective-permute-done.3, bf16[1024,1024]{1,0:T(8,128)(2,1)} %fusion.57, f32[1024]{0:T(1024)S(1)} %fusion.75, f32[1024]{0:T(1024)S(1)} %bitcast.129, ...), kind=kOutput, calls=%fused_computation.64 | convolution fusion | flops 2160066560 | bytes 12599296 | tf_op jit(solution)/shard_map/dot_general | solution.py:1198
  613.9 4.9 all-to-all-start.3
  622.8 5.5 convert_bitcast_fusion.1
  638.5 4.1 fusion
  642.5 4.1 fusion.1
  646.6 17.2 %all-to-all-done.3 = bf16[8,128,1024]{2,1,0:T(8,128)(2,1)} async-done(((bf16[8,128,1024]{2,1,0:T(8,128)(2,1)}), bf16[8,128,1024]{2,1,0:T(8,128)(2,1)}, u32[]{:S(2)}, u32[]{:S(2)}) %all-to-all-start.3) | async-done | bytes 2097184 | tf_op jit(solution)/shard_map/all_to_all | solution.py:1203
  665.3 5.4 convert_bitcast_fusion
  (222 shorter events, 51.1 us)
Async XLA Ops:
  7.2 82.1 %all-gather.8.cloned.1.call-start = ((), (), s32[]{:S(2)}) async-start(), calls=%async_computation.5 | async-start | bytes 9830400 | tf_op jit(solution)/shard_map/all_gather | solution.py:1222
  12.5 34.0 %copy-start.26 = (s32[8,128]{1,0:T(8,128)}, s32[8,128]{1,0:T(8,128)S(1)}, u32[]{:S(2)}) copy-start(s32[8,128]{1,0:T(8,128)S(1)} %select_reduce_fusion) | copy-start | bytes 12292
  22.7 157.1 %all-gather.10.cloned.1.call-start = ((), (), s32[]{:S(2)}) async-start(), calls=%async_computation.6 | async-start | bytes 3145728 | tf_op jit(solution)/shard_map/all_gather | solution.py:1226
  23.4 156.4 %all-gather.14.cloned.1.call-start = ((), (), s32[]{:S(2)}) async-start(), calls=%async_computation.8 | async-start | bytes 4325376 | tf_op jit(solution)/shard_map/all_gather | solution.py:1225
  24.2 55.5 %all-to-all-start = ((bf16[8,128,1024]{2,1,0:T(8,128)(2,1)}), bf16[8,128,1024]{2,1,0:T(8,128)(2,1)S(1)}, u32[]{:S(2)}, u32[]{:S(2)}) async-start(bf16[8,128,1024]{2,1,0:T(8,128)(2,1)} %bitcast.4), calls=%async_computation | async-start | bytes 4194304 | tf_op jit(solution)/shard_map/all_to_all | solution.py:1203
  31.5 148.3 %all-gather.12.cloned.1.call-start = ((), (), s32[]{:S(2)}) async-start(), calls=%async_computation.7 | async-start | bytes 8650752 | tf_op jit(solution)/shard_map/all_gather | solution.py:1224
  42.9 46.4 %copy-start.18 = (f32[1,4,2,128]{3,1,2,0:T(4,128)}, f32[1,4,2,128]{3,1,2,0:T(4,128)S(1)}, u32[]{:S(2)}) copy-start(f32[1,4,2,128]{3,1,2,0:T(4,128)S(1)} %copy.82) | copy-start | bytes 12292
  45.8 95.5 %copy-start.28 = (s32[1024]{0:T(1024)}, s32[1024]{0:T(1024)S(1)}, u32[]{:S(2)}) copy-start(s32[1024]{0:T(1024)S(1)} %fusion.74) | copy-start | bytes 12292
  79.7 61.7 %all-to-all-start.1 = ((bf16[8,128,1024]{2,1,0:T(8,128)(2,1)}), bf16[8,128,1024]{2,1,0:T(8,128)(2,1)}, u32[]{:S(2)}, u32[]{:S(2)}) async-start(bf16[8,128,1024]{2,1,0:T(8,128)(2,1)} %bitcast.108), calls=%async_computation.1 | async-start | bytes 4194304 | tf_op jit(solution)/shard_map/all_to_all | solution.py:1203
  84.1 349.7 %reduce-scatter.2.cloned.1.call-start = ((), (), s32[]{:S(2)}) async-start(), calls=%async_computation.9 | async-start | bytes 9191424 | tf_op jit(solution)/shard_map/reduce_scatter | solution.py:1153
  88.7 10.9 %copy-start.6 = (bf16[1024,1024]{1,0:T(8,128)(2,1)}, bf16[1024,1024]{1,0:T(8,128)(2,1)S(1)}, u32[]{:S(2)}) copy-start(bf16[1024,1024]{1,0:T(8,128)(2,1)S(1)} %get-tuple-element.274.res) | copy-start | bytes 6291460
  89.3 10.3 %copy-start.22 = (f32[1024]{0:T(1024)}, f32[1024]{0:T(1024)S(1)}, u32[]{:S(2)}) copy-start(f32[1024]{0:T(1024)S(1)} %add_rsqrt_fusion) | copy-start | bytes 12292
  89.3 14.4 %copy-start.36 = (f32[4]{0:T(128)S(1)}, f32[4]{0:T(128)}, u32[]{:S(2)}) copy-start(f32[4]{0:T(128)} %param.37) | copy-start | bytes 52
  89.3 14.4 %copy-start.37 = (f32[4]{0:T(128)S(1)}, f32[4]{0:T(128)}, u32[]{:S(2)}) copy-start(f32[4]{0:T(128)} %param.36) | copy-start | bytes 52
  99.6 5.7 collective-permute-start
  290.8 95.1 %collective-permute-start.1 = (bf16[1024,1024]{1,0:T(8,128)(2,1)}, bf16[1024,1024]{1,0:T(8,128)(2,1)}, u32[]{:S(2)}, u32[]{:S(2)}) collective-permute-start(bf16[1024,1024]{1,0:T(8,128)(2,1)} %get-tuple-element.113), channel_id=1, source_target_pairs={{0,2},{2,0},{1,3},{3,1},{4,6},{6,4},{5,7},{7,5},{8,10},{10,8},{9,1... | collective-permute-start | bytes 6291464 | tf_op jit(solution)/shard_map/ppermute | solution.py:891
  328.6 49.3 %copy-start.25 = (f32[8,256]{1,0:T(8,128)S(1)}, f32[8,256]{1,0:T(8,128)}, u32[]{:S(2)}) copy-start(f32[8,256]{1,0:T(8,128)} %get-tuple-element.126) | copy-start | bytes 24580
  328.6 57.3 %copy-start.15 = (f32[1,2048]{1,0:T(1,128)S(1)}, f32[1,2048]{1,0:T(1,128)}, u32[]{:S(2)}) copy-start(f32[1,2048]{1,0:T(1,128)} %get-tuple-element.264) | copy-start | bytes 24580
  328.6 57.3 %copy-start.16 = (f32[1,2048]{1,0:T(1,128)S(1)}, f32[1,2048]{1,0:T(1,128)}, u32[]{:S(2)}) copy-start(f32[1,2048]{1,0:T(1,128)} %get-tuple-element.265) | copy-start | bytes 24580
  328.6 57.3 %copy-start.17 = (f32[1,2048]{1,0:T(1,128)S(1)}, f32[1,2048]{1,0:T(1,128)}, u32[]{:S(2)}) copy-start(f32[1,2048]{1,0:T(1,128)} %get-tuple-element.266) | copy-start | bytes 24580
  328.6 57.3 %copy-start.33 = (f32[8]{0:T(128)S(1)}, f32[8]{0:T(128)}, u32[]{:S(2)}) copy-start(f32[8]{0:T(128)} %slice.196) | copy-start | bytes 100
  328.6 57.3 %copy-start.34 = (f32[8]{0:T(128)S(1)}, f32[8]{0:T(128)}, u32[]{:S(2)}) copy-start(f32[8]{0:T(128)} %slice.193) | copy-start | bytes 100
  328.7 57.3 %copy-start.35 = (f32[8]{0:T(128)S(1)}, f32[8]{0:T(128)}, u32[]{:S(2)}) copy-start(f32[8]{0:T(128)} %slice.190) | copy-start | bytes 100
  379.5 6.4 collective-permute-start.2
  387.5 13.8 %copy-start.7 = (bf16[1024,1024]{1,0:T(8,128)(2,1)S(1)}, bf16[1024,1024]{1,0:T(8,128)(2,1)}, u32[]{:S(2)}) copy-start(bf16[1024,1024]{1,0:T(8,128)(2,1)} %copy-done.6) | copy-start | bytes 6291460
  387.5 13.8 %copy-start.23 = (f32[1024]{0:T(1024)S(1)}, f32[1024]{0:T(1024)}, u32[]{:S(2)}) copy-start(f32[1024]{0:T(1024)} %copy-done.22) | copy-start | bytes 12292
  400.0 203.5 %collective-permute-start.3 = (bf16[1024,1024]{1,0:T(8,128)(2,1)}, bf16[1024,1024]{1,0:T(8,128)(2,1)}, u32[]{:S(2)}, u32[]{:S(2)}) collective-permute-start(bf16[1024,1024]{1,0:T(8,128)(2,1)} %fusion.57), channel_id=1, source_target_pairs={{0,2},{2,0},{1,3},{3,1},{4,6},{6,4},{5,7},{7,5},{8,10},{10,8},{9,1... | collective-permute-start | bytes 6291464 | tf_op jit(solution)/shard_map/ppermute | solution.py:891
  411.0 192.4 %all-to-all-start.2 = ((bf16[8,128,1024]{2,1,0:T(8,128)(2,1)}), bf16[8,128,1024]{2,1,0:T(8,128)(2,1)}, u32[]{:S(2)}, u32[]{:S(2)}) async-start(bf16[8,128,1024]{2,1,0:T(8,128)(2,1)} %bitcast.107), calls=%async_computation.2 | async-start | bytes 4194304 | tf_op jit(solution)/shard_map/all_to_all | solution.py:1203
  415.6 219.4 %all-gather.16.cloned.1.call-start = ((), (), s32[]{:S(2)}) async-start(), calls=%async_computation.10 | async-start | bytes 4866048 | tf_op jit(solution)/shard_map/all_gather | solution.py:1306
  613.9 50.0 %all-to-all-start.3 = ((bf16[8,128,1024]{2,1,0:T(8,128)(2,1)}), bf16[8,128,1024]{2,1,0:T(8,128)(2,1)}, u32[]{:S(2)}, u32[]{:S(2)}) async-start(bf16[8,128,1024]{2,1,0:T(8,128)(2,1)} %bitcast.106), calls=%async_computation.4 | async-start | bytes 4194304 | tf_op jit(solution)/shard_map/all_to_all | solution.py:1203
  619.4 14.4 %collective-permute-start.4 = (f32[640]{0:T(1024)S(1)}, f32[640]{0:T(1024)S(1)}, u32[]{:S(2)}, u32[]{:S(2)}) collective-permute-start(f32[640]{0:T(1024)S(1)} %pad_maximum_fusion.1), channel_id=1, source_target_pairs={{0,2},{2,0},{1,3},{3,1},{4,6},{6,4},{5,7},{7,5},{8,10},{10,8},{9,1... | collective-permute-start | bytes 7688 | tf_op jit(solution)/shard_map/ppermute | solution.py:891
  622.8 9.5 %copy-start.11 = (bf16[512,1024]{1,0:T(8,128)(2,1)S(1)}, bf16[512,1024]{1,0:T(8,128)(2,1)}, u32[]{:S(2)}) copy-start(bf16[512,1024]{1,0:T(8,128)(2,1)} %get-tuple-element.142) | copy-start | bytes 3145732
  (27 other events, 112.2 us)
Sparse Core Ops, SparseCore 0:
  22.8 19.8 all-gather.7
  44.2 11.7 all-gather.9
  57.5 12.8 all-gather.13
  72.5 17.1 all-gather.11
  291.0 126.2 reduce-scatter.1
  433.9 113.7 all-gather.15

commit v5 on v4

--- a/solution.py
+++ b/solution.py
@@ -1279,9 +1279,10 @@
 
     half = model // fs
     down_rows = hidden_cols // fs
+
+    leaving = leaving_grad(first, ahead)
+    leaving, mlp_cat = lax.optimization_barrier((leaving, mlp_cat))
     mlp_share = scattered(mlp_cat)
-
-    leaving = leaving_grad(first, ahead)
     dproj, dab, tail_rows, head_rows, dtaps, dhead = delta_grad(
         proj, conv, flags, cum, halo, taps, head, do, tinv, uval, wkey, states, entering, leaving,
         heads, dk, dv,

time: 685 us -> 699 us (1.020)
  transfers between devices with their start and end apart: 15 -> 15, of which waited for: 4 -> 5; matrix products, arithmetic and copies ran while one was open for 18% -> 18% of each run, Pallas kernels for 48% -> 42%
where the time goes in v5:
time: 699 us; the launch traced here: 692 us
  Pallas kernels  435 us (62%)
  matrix products  92.7 us (13%)
  waiting for transfers between devices  54.5 us (8%)
  starting transfers between devices  35.4 us (5%)
  local copies, waits for them, and re-layouts  31.8 us (5%)
  other arithmetic  25.1 us (4%)
  between operations  15.1 us (2%)
    pallas_call x1, Pallas kernels, reduced(): pl.pallas_call(functools.partial(sum_kernel, plan), in_specs=[pl.BlockSpe...  173 us
    pallas_call x1, Pallas kernels, block_rest(): pl.pallas_call(functools.partial(block_kernel, heads, dk, dv, tiles), gri...  110 us
    pallas_call x2, Pallas kernels, chained(): pl.pallas_call(functools.partial(chain_kernel, forward, levels), in_specs...  68.7 us
    pallas_call x1, Pallas kernels, delta_grad(): pl.pallas_call(functools.partial(grad_kernel, heads, dk, dv), grid=(steps...  48.2 us
    dot_general x8, matrix products, moved(): lax.dot_general(maps, values, (((0 if transposed else 1,), (0,)), ((), ()...  43.8 us
    all_to_all x4, waiting for transfers between devices, exchanged(): lax.all_to_all(values, 'ctx', split_axis=0, concat_axis=0, tiled=True)  41.8 us
    pallas_call x1, Pallas kernels, delta_forward(): pl.pallas_call(functools.partial(forward_kernel, heads, dk, dv), grid=(st...  35.4 us
    all_to_all x4, starting transfers between devices, exchanged(): lax.all_to_all(values, 'ctx', split_axis=0, concat_axis=0, tiled=True)  24.7 us
  transfers between devices with their start and end apart: 15, of which 5 were waited for; matrix products, arithmetic and copies ran while one was open for 18% of the time, Pallas kernels for 42%

profile of v5, /device:TPU:0, one launch (start us, length us, event | category | flops | bytes accessed | tf_op | source)
XLA Modules:
  0.0 691.7 jit_solution(5384699761422971845)
XLA Ops:
  12.5 3.7 fusion.51
  16.2 6.4 concatenate.36
  24.2 7.3 %all-to-all-start = ((bf16[8,128,1024]{2,1,0:T(8,128)(2,1)}), bf16[8,128,1024]{2,1,0:T(8,128)(2,1)S(1)}, u32[]{:S(2)}, u32[]{:S(2)}) async-start(bf16[8,128,1024]{2,1,0:T(8,128)(2,1)} %bitcast.4), calls=%async_computation | async-start | bytes 4194304 | tf_op jit(solution)/shard_map/all_to_all | solution.py:1203
  44.8 5.3 fusion.54
  50.1 29.6 %all-to-all-done = bf16[8,128,1024]{2,1,0:T(8,128)(2,1)S(1)} async-done(((bf16[8,128,1024]{2,1,0:T(8,128)(2,1)}), bf16[8,128,1024]{2,1,0:T(8,128)(2,1)S(1)}, u32[]{:S(2)}, u32[]{:S(2)}) %all-to-all-start) | async-done | bytes 2097184 | tf_op jit(solution)/shard_map/all_to_all | solution.py:1203
  79.7 4.4 all-to-all-start.1
  84.3 4.2 fusion.12
  89.2 10.3 %fusion.88.proj.ab.zgate.zgate_late = f32[1024,3200]{1,0:T(8,128)S(1)} fusion(bf16[1024,3200]{1,0:T(8,128)(2,1)} %all-gather.8.cloned.1.call-done, bf16[1024,1024]{1,0:T(8,128)(2,1)S(1)} %get-tuple-element.278.res, f32[1024]{0:T(1024)S(1)} %bitcast.125, f32[1024]{0:T(1024)S(1)} %add_rsqrt_fusion), kind=kOutput, calls=%fused_computation.158 | convolution fusion | flops 6715080704 | bytes 21766144 | tf_op jit(solution)/shard_map/dot_general | solution.py:1257
  99.5 4.0 collective-permute-start
  105.9 35.4 %shard_map.365 = (f32[1024,2048]{1,0:T(8,128)}, f32[1024,1024]{1,0:T(8,128)}, bf16[1024,512]{1,0:T(8,128)(2,1)}, bf16[8,4,128,384]{3,2,1,0:T(8,128)(2,1)}, bf16[...) custom-call(f32[1024,3200]{1,0:T(8,128)} %copy-done.37, ...), custom_call_target="tpu_custom_call" | custom-call | flops 13421772800 | bytes 29360128 | tf_op jit(solution)/shard_map/pallas_call | solution.py:220
  141.3 5.3 fusion.46.e_now.e_late
  146.6 32.2 %shard_map.366 = (bf16[4,128,256]{2,1,0:T(8,128)(2,1)S(1)}, bf16[2,4,128,128]{3,2,1,0:T(8,128)(2,1)S(1)}) custom-call(bf16[4,128,384]{2,1,0:T(8,128)(2,1)S(1)} %copy-done.2), custom_call_target="tpu_custom_call" | custom-call | flops 24999999488 | bytes 3145728 | tf_op jit(solution)/shard_map/pallas_call | solution.py:846
  180.7 109.8 %shard_map.367 = (bf16[1024,1024]{1,0:T(8,128)(2,1)}, bf16[1024,1024]{1,0:T(8,128)(2,1)}, f32[1024,1024]{1,0:T(8,128)}, f32[1024,1024]{1,0:T(8,128)}, bf16[1024,...) custom-call(f32[1024,1024]{1,0:T(8,128)} %get-tuple-element.96.local, ...), custom_call_target="tpu_custom_call" | custom-call | flops 99999997952 | bytes 41943040 | tf_op jit(solution)/shard_map/pallas_call | solution.py:393
  291.4 36.5 %shard_map.368.leaving = bf16[4,128,256]{2,1,0:T(8,128)(2,1)S(1)} custom-call(bf16[4,128,256]{2,1,0:T(8,128)(2,1)S(1)} %copy-done.4, bf16[2,4,128,128]{3,2,1,0:T(8,128)(2,1)S(1)} %get-tuple-element.113.refs_1_), custom_call_target="tpu_custom_call" | custom-call | flops 24999999488 | bytes 2097152 | tf_op jit(solution)/shard_map/pallas_call | solution.py:846
  332.0 48.2 %shard_map.369 = (bf16[1024,2048]{1,0:T(8,128)(2,1)}, bf16[1024,128]{1,0:T(8,128)(2,1)}, f32[8,2048]{1,0:T(8,128)}, f32[8,2048]{1,0:T(8,128)}, f32[8,2048]{1,0:T(8,128)}, /*index=5*/f32[8,128]{1,0:T(8,128)}) custom-call(f32[1024,3200]{1,0:T(8,128)} %copy-done.37, f32[1024,2048]{1,0:T(8,128)} %get-tuple-element.107.conv, f32[1024,3200]{1,0:T(8,128)} %copy-done.37, ...), custom_call_target="tpu_custom_call" | custom-call | flops 53687091200 | bytes 33554432 | tf_op jit(solution)/shard_map/pallas_call | solution.py:679
  384.7 4.2 collective-permute-done.2
  390.5 12.5 %fusion.57 = bf16[1024,1024]{1,0:T(8,128)(2,1)} fusion(bf16[1024,3200]{1,0:T(8,128)(2,1)} %all-gather.8.cloned.1.call-done, bf16[1024,128]{1,0:T(8,128)(2,1)} %get-tuple-element.122, bf16[1024,1024]{1,0:T(8,128)(2,1)} %get-tuple-element.134, bf16[1024,2048]{1,0:T(8,128)(2,1)} %fusion.69), kind=kOutput, calls=%fused_computation.67 | convolution fusion | flops 6731595776 | bytes 15204352 | tf_op jit(solution)/shard_map/dot_general | solution.py:1298
  406.7 7.4 %fusion.47 = bf16[1024,1024]{1,0:T(8,128)(2,1)} fusion(f32[1024,1024]{1,0:T(8,128)} %get-tuple-element.126, bf16[1024,1024]{1,0:T(8,128)(2,1)} %collective-permute-done.1, bf16[1024,1024]{1,0:T(8,128)(2,1)} %get-tuple-element.117, s32[1024]{0:T(1024)S(1)} %copy-done.31), kind=kOutput, calls=%fused_computation.63 | convolution fusion | flops 2154823680 | bytes 10489856 | tf_op jit(solution)/shard_map/dot_general | solution.py:1198
  414.1 8.1 %all-to-all-start.2 = ((bf16[8,128,1024]{2,1,0:T(8,128)(2,1)}), bf16[8,128,1024]{2,1,0:T(8,128)(2,1)}, u32[]{:S(2)}, u32[]{:S(2)}) async-start(bf16[8,128,1024]{2,1,0:T(8,128)(2,1)} %bitcast.107), calls=%async_computation.2 | async-start | bytes 4194304 | tf_op jit(solution)/shard_map/all_to_all | solution.py:1203
  422.9 6.1 convolution_convert_fusion.1.refs_3_
  429.0 4.0 convolution_convert_fusion.2.refs_2_
  433.0 7.3 %convolution_convert_fusion.refs_1_ = bf16[1024,2176]{1,0:T(8,128)(2,1)} fusion(bf16[1024,128]{1,0:T(8,128)(2,1)S(1)} %copy-done.42, bf16[1024,2048]{1,0:T(8,128)(2,1)S(1)} %copy-done.38, bf16[1024,1024]{1,0:T(8,128)(2,1)S(1)} %copy-done.7, f32[1024]{0:T(1024)S(1)} %bitcast.127, f32[1024]{0:T(1024)S(1)} %copy-done.25), kind=kOutput, calls=%fused_computation.14 | convolution fusion | flops 4578738176 | bytes 11018240 | tf_op jit(solution)/shard_map/dot_general | solution.py:1273
  440.3 6.1 reduce-scatter.2.cloned.1.call-done
  446.5 173.3 %shard_map.370 = (f32[64,128]{1,0:T(8,128)}, bf16[512,2176]{1,0:T(8,128)(2,1)}, bf16[512,1024]{1,0:T(8,128)(2,1)}, bf16[512,1024]{1,0:T(8,128)(2,1)}) custom-call(f32[128,128]{1,0:T(8,128)} %reshape.269.refs_0_, bf16[1024,2176]{1,0:T(8,128)(2,1)} %convolution_convert_fusion.refs_1_, bf16[1024,1024]{1,0:T(8,128)(2,1)} %convolution_convert_fusion.2.refs_2_, ...), custom_call_target="tpu_custom_call" | custom-call | flops 109999996928 | bytes 17367040 | tf_op jit(solution)/shard_map/pallas_call | solution.py:1132
  619.8 3.4 fusion.17
  623.2 7.0 %fusion.48 = bf16[1024,1024]{1,0:T(8,128)(2,1)} fusion(bf16[1024,1024]{1,0:T(8,128)(2,1)S(1)} %copy-done.7, f32[1024,1024]{1,0:T(8,128)S(1)} %copy-done.40, bf16[1024,1024]{1,0:T(8,128)(2,1)} %collective-permute-done.3, bf16[1024,1024]{1,0:T(8,128)(2,1)} %fusion.57, f32[1024]{0:T(1024)S(1)} %fusion.75, f32[1024]{0:T(1024)S(1)} %bitcast.129, ...), kind=kOutput, calls=%fused_computation.64 | convolution fusion | flops 2160066560 | bytes 12599296 | tf_op jit(solution)/shard_map/dot_general | solution.py:1198
  630.2 4.9 all-to-all-start.3
  641.8 5.5 convert_bitcast_fusion.1
  657.5 4.1 fusion
  661.6 4.1 fusion.1
  665.6 12.2 %all-to-all-done.3 = bf16[8,128,1024]{2,1,0:T(8,128)(2,1)} async-done(((bf16[8,128,1024]{2,1,0:T(8,128)(2,1)}), bf16[8,128,1024]{2,1,0:T(8,128)(2,1)}, u32[]{:S(2)}, u32[]{:S(2)}) %all-to-all-start.3) | async-done | bytes 2097184 | tf_op jit(solution)/shard_map/all_to_all | solution.py:1203
  679.3 5.4 convert_bitcast_fusion
  (220 shorter events, 58.6 us)
Async XLA Ops:
  7.2 82.0 %all-gather.8.cloned.1.call-start = ((), (), s32[]{:S(2)}) async-start(), calls=%async_computation.5 | async-start | bytes 9830400 | tf_op jit(solution)/shard_map/all_gather | solution.py:1222
  12.5 32.3 %copy-start.28 = (s32[8,128]{1,0:T(8,128)}, s32[8,128]{1,0:T(8,128)S(1)}, u32[]{:S(2)}) copy-start(s32[8,128]{1,0:T(8,128)S(1)} %select_reduce_fusion) | copy-start | bytes 12292
  22.6 8.9 %copy-start.10 = (bf16[512,1408]{1,0:T(8,128)(2,1)S(1)}, bf16[512,1408]{1,0:T(8,128)(2,1)}, u32[]{:S(2)}) copy-start(bf16[512,1408]{1,0:T(8,128)(2,1)} %param.42) | copy-start | bytes 4325380
  22.7 156.8 %all-gather.10.cloned.1.call-start = ((), (), s32[]{:S(2)}) async-start(), calls=%async_computation.6 | async-start | bytes 3145728 | tf_op jit(solution)/shard_map/all_gather | solution.py:1226
  23.4 156.1 %all-gather.14.cloned.1.call-start = ((), (), s32[]{:S(2)}) async-start(), calls=%async_computation.8 | async-start | bytes 4325376 | tf_op jit(solution)/shard_map/all_gather | solution.py:1225
  24.2 55.5 %all-to-all-start = ((bf16[8,128,1024]{2,1,0:T(8,128)(2,1)}), bf16[8,128,1024]{2,1,0:T(8,128)(2,1)S(1)}, u32[]{:S(2)}, u32[]{:S(2)}) async-start(bf16[8,128,1024]{2,1,0:T(8,128)(2,1)} %bitcast.4), calls=%async_computation | async-start | bytes 4194304 | tf_op jit(solution)/shard_map/all_to_all | solution.py:1203
  31.5 148.0 %all-gather.12.cloned.1.call-start = ((), (), s32[]{:S(2)}) async-start(), calls=%async_computation.7 | async-start | bytes 8650752 | tf_op jit(solution)/shard_map/all_gather | solution.py:1224
  41.1 48.1 %copy-start.17 = (f32[1,4,2,128]{3,1,2,0:T(4,128)}, f32[1,4,2,128]{3,1,2,0:T(4,128)S(1)}, u32[]{:S(2)}) copy-start(f32[1,4,2,128]{3,1,2,0:T(4,128)S(1)} %copy.82) | copy-start | bytes 12292
  42.6 7.5 %copy-start.21 = (f32[1024]{0:T(1024)}, f32[1024]{0:T(1024)S(1)}, u32[]{:S(2)}) copy-start(f32[1024]{0:T(1024)S(1)} %get-tuple-element.273) | copy-start | bytes 12292
  42.6 7.5 %copy-start.22 = (f32[1024]{0:T(1024)}, f32[1024]{0:T(1024)S(1)}, u32[]{:S(2)}) copy-start(f32[1024]{0:T(1024)S(1)} %get-tuple-element.272) | copy-start | bytes 12292
  42.6 7.5 %copy-start.23 = (f32[1024]{0:T(1024)}, f32[1024]{0:T(1024)S(1)}, u32[]{:S(2)}) copy-start(f32[1024]{0:T(1024)S(1)} %get-tuple-element.271) | copy-start | bytes 12292
  44.8 96.5 %copy-start.30 = (s32[1024]{0:T(1024)}, s32[1024]{0:T(1024)S(1)}, u32[]{:S(2)}) copy-start(s32[1024]{0:T(1024)S(1)} %fusion.74) | copy-start | bytes 12292
  79.7 61.5 %all-to-all-start.1 = ((bf16[8,128,1024]{2,1,0:T(8,128)(2,1)}), bf16[8,128,1024]{2,1,0:T(8,128)(2,1)}, u32[]{:S(2)}, u32[]{:S(2)}) async-start(bf16[8,128,1024]{2,1,0:T(8,128)(2,1)} %bitcast.108), calls=%async_computation.1 | async-start | bytes 4194304 | tf_op jit(solution)/shard_map/all_to_all | solution.py:1203
  84.1 362.3 %reduce-scatter.2.cloned.1.call-start = ((), (), s32[]{:S(2)}) async-start(), calls=%async_computation.9 | async-start | bytes 9191424 | tf_op jit(solution)/shard_map/reduce_scatter | solution.py:1153
  88.6 10.9 %copy-start.6 = (bf16[1024,1024]{1,0:T(8,128)(2,1)}, bf16[1024,1024]{1,0:T(8,128)(2,1)S(1)}, u32[]{:S(2)}) copy-start(bf16[1024,1024]{1,0:T(8,128)(2,1)S(1)} %get-tuple-element.278.res) | copy-start | bytes 6291460
  89.2 10.3 %copy-start.24 = (f32[1024]{0:T(1024)}, f32[1024]{0:T(1024)S(1)}, u32[]{:S(2)}) copy-start(f32[1024]{0:T(1024)S(1)} %add_rsqrt_fusion) | copy-start | bytes 12292
  89.2 14.3 %copy-start.35 = (f32[4]{0:T(128)S(1)}, f32[4]{0:T(128)}, u32[]{:S(2)}) copy-start(f32[4]{0:T(128)} %param.37) | copy-start | bytes 52
  89.2 14.3 %copy-start.36 = (f32[4]{0:T(128)S(1)}, f32[4]{0:T(128)}, u32[]{:S(2)}) copy-start(f32[4]{0:T(128)} %param.36) | copy-start | bytes 52
  99.5 5.7 collective-permute-start
  331.0 58.0 %collective-permute-start.1 = (bf16[1024,1024]{1,0:T(8,128)(2,1)}, bf16[1024,1024]{1,0:T(8,128)(2,1)}, u32[]{:S(2)}, u32[]{:S(2)}) collective-permute-start(bf16[1024,1024]{1,0:T(8,128)(2,1)} %get-tuple-element.117), channel_id=1, source_target_pairs={{0,2},{2,0},{1,3},{3,1},{4,6},{6,4},{5,7},{7,5},{8,10},{10,8},{9,1... | collective-permute-start | bytes 6291464 | tf_op jit(solution)/shard_map/ppermute | solution.py:891
  332.0 49.0 %copy-start.27 = (f32[8,256]{1,0:T(8,128)S(1)}, f32[8,256]{1,0:T(8,128)}, u32[]{:S(2)}) copy-start(f32[8,256]{1,0:T(8,128)} %get-tuple-element.130) | copy-start | bytes 24580
  382.6 6.4 collective-permute-start.2
  390.5 13.8 %copy-start.7 = (bf16[1024,1024]{1,0:T(8,128)(2,1)S(1)}, bf16[1024,1024]{1,0:T(8,128)(2,1)}, u32[]{:S(2)}) copy-start(bf16[1024,1024]{1,0:T(8,128)(2,1)} %copy-done.6) | copy-start | bytes 6291460
  390.5 13.8 %copy-start.25 = (f32[1024]{0:T(1024)S(1)}, f32[1024]{0:T(1024)}, u32[]{:S(2)}) copy-start(f32[1024]{0:T(1024)} %copy-done.24) | copy-start | bytes 12292
  403.1 216.7 %collective-permute-start.3 = (bf16[1024,1024]{1,0:T(8,128)(2,1)}, bf16[1024,1024]{1,0:T(8,128)(2,1)}, u32[]{:S(2)}, u32[]{:S(2)}) collective-permute-start(bf16[1024,1024]{1,0:T(8,128)(2,1)} %fusion.57), channel_id=1, source_target_pairs={{0,2},{2,0},{1,3},{3,1},{4,6},{6,4},{5,7},{7,5},{8,10},{10,8},{9,1... | collective-permute-start | bytes 6291464 | tf_op jit(solution)/shard_map/ppermute | solution.py:891
  414.1 205.7 %all-to-all-start.2 = ((bf16[8,128,1024]{2,1,0:T(8,128)(2,1)}), bf16[8,128,1024]{2,1,0:T(8,128)(2,1)}, u32[]{:S(2)}, u32[]{:S(2)}) async-start(bf16[8,128,1024]{2,1,0:T(8,128)(2,1)} %bitcast.107), calls=%async_computation.2 | async-start | bytes 4194304 | tf_op jit(solution)/shard_map/all_to_all | solution.py:1203
  422.1 231.8 %all-gather.16.cloned.1.call-start = ((), (), s32[]{:S(2)}) async-start(), calls=%async_computation.10 | async-start | bytes 4866048 | tf_op jit(solution)/shard_map/all_gather | solution.py:1307
  630.2 8.3 %copy-start.8 = (bf16[512,2176]{1,0:T(8,128)(2,1)S(1)}, bf16[512,2176]{1,0:T(8,128)(2,1)}, u32[]{:S(2)}) copy-start(bf16[512,2176]{1,0:T(8,128)(2,1)} %get-tuple-element.144) | copy-start | bytes 6684676
  630.2 47.6 %all-to-all-start.3 = ((bf16[8,128,1024]{2,1,0:T(8,128)(2,1)}), bf16[8,128,1024]{2,1,0:T(8,128)(2,1)}, u32[]{:S(2)}, u32[]{:S(2)}) async-start(bf16[8,128,1024]{2,1,0:T(8,128)(2,1)} %bitcast.106), calls=%async_computation.4 | async-start | bytes 4194304 | tf_op jit(solution)/shard_map/all_to_all | solution.py:1203
  635.7 17.1 %collective-permute-start.4 = (f32[640]{0:T(1024)S(1)}, f32[640]{0:T(1024)S(1)}, u32[]{:S(2)}, u32[]{:S(2)}) collective-permute-start(f32[640]{0:T(1024)S(1)} %pad_maximum_fusion.1), channel_id=1, source_target_pairs={{0,2},{2,0},{1,3},{3,1},{4,6},{6,4},{5,7},{7,5},{8,10},{10,8},{9,1... | collective-permute-start | bytes 7688 | tf_op jit(solution)/shard_map/ppermute | solution.py:891
  641.8 7.9 %copy-start.12 = (bf16[512,1024]{1,0:T(8,128)(2,1)S(1)}, bf16[512,1024]{1,0:T(8,128)(2,1)}, u32[]{:S(2)}) copy-start(bf16[512,1024]{1,0:T(8,128)(2,1)} %get-tuple-element.145) | copy-start | bytes 3145732
  641.8 9.5 %copy-start.11 = (bf16[512,1024]{1,0:T(8,128)(2,1)S(1)}, bf16[512,1024]{1,0:T(8,128)(2,1)}, u32[]{:S(2)}) copy-start(bf16[512,1024]{1,0:T(8,128)(2,1)} %get-tuple-element.146) | copy-start | bytes 3145732
  (26 other events, 95.3 us)
Sparse Core Ops, SparseCore 0:
  22.8 19.8 all-gather.7
  44.2 11.7 all-gather.9
  57.6 12.8 all-gather.13
  72.5 17.1 all-gather.11
  328.8 117.5 reduce-scatter.1
  448.5 126.3 all-gather.15
